TPU v7x, 32 devices: a whole 2x2x4 slice. The times are simulated.
32 devices in a mesh: stream: 2 (over x), page: 16 (over z, y, core).
Axes of the slice: x: 2, y: 2, z: 4, core: 2. Of those that a mesh axis runs over, the one named last changes fastest.
Arguments:
- states: bfloat16 [2, 16, 640, 768], P('stream', 'page'), may hold values from -6 to 6
- counts: int32 [2, 16], P(None, 'page'), may hold values from 160 to 640, as said below
- box_x: int32 [16, 640], P('page'), may hold values from 0 to 63
- box_y: int32 [16, 640], P('page'), may hold values from 0 to 63
- ln1_gain: float32 [2, 768], P('stream'), may hold values from 0.5 to 1.5
- ln2_gain: float32 [2, 768], P('stream'), may hold values from 0.5 to 1.5
- box_table: float32 [2, 128, 24], P('stream'), may hold values from -4 to 4
- w_qkv: bfloat16 [2, 768, 2304], P('stream'), may hold values from -0.21875 to 0.21875
- w_out: bfloat16 [2, 768, 768], P('stream'), may hold values from -0.875 to 0.875
- w_cq: bfloat16 [2, 768, 768], P('stream'), may hold values from -0.21875 to 0.21875
- w_ckv: bfloat16 [2, 768, 1536], P('stream'), may hold values from -0.21875 to 0.21875
- w_cout: bfloat16 [2, 768, 768], P('stream'), may hold values from -0.875 to 0.875
- w_up: bfloat16 [2, 768, 3072], P('stream'), may hold values from -0.21875 to 0.21875
- w_down: bfloat16 [2, 3072, 768], P('stream'), may hold values from -0.109375 to 0.109375
- cotangent: bfloat16 [2, 16, 640, 768], P('stream', 'page'), may hold values from -6 to 6
Outputs:
- result: bfloat16 [2, 16, 640, 768], P('stream', 'page')
- states_grad: float32 [2, 16, 640, 768], P('stream', 'page')
- ln1_gain_grad: float32 [2, 768], P('stream', 'page')
- ln2_gain_grad: float32 [2, 768], P('stream', 'page')
- box_table_grad: float32 [2, 128, 24], P('stream', 'page')
- w_qkv_grad: float32 [2, 768, 2304], P('stream', 'page')
- w_out_grad: float32 [2, 768, 768], P('stream', 'page')
- w_cq_grad: float32 [2, 768, 768], P('stream', 'page')
- w_ckv_grad: float32 [2, 768, 1536], P('stream', 'page')
- w_cout_grad: float32 [2, 768, 768], P('stream', 'page')
- w_up_grad: float32 [2, 768, 3072], P('stream', 'page')
- w_down_grad: float32 [2, 3072, 768], P('stream', 'page')
Inputs may be any that keep to these rules, and one draw needn't show every extreme that they name: counts[0] holds each page's text tokens, 640 on some page; counts[1] holds each page's patches, 256 for a 512-pixel page and 576 for a 768-pixel page.
All inputs are finite; a program needn't handle non-finite values.
Results may differ from a plain program's by a relative error of at most 0.015.
Values may be sent and summed in bfloat16 or wider, within the bound.
A program may use at most 256 MiB of HBM per device.

v0:
```python
import jax
import jax.numpy as jnp
from jax import lax
from jax.sharding import PartitionSpec as P

GRID_SMALL = 16
GRID_LARGE = 24


EPSILON = 1e-05
MASKED = -1000000000.0
PRECISE = lax.Precision.HIGHEST


def swapped(shard, axis, bit):
    return lax.ppermute(shard, axis, [(i, i ^ 1 << bit) for i in range(lax.axis_size(axis))])


def norm_rows(inputs, gain_row):
    centre = inputs - jnp.mean(inputs, axis=-1, keepdims=True)
    spread = jnp.mean(centre * centre, axis=-1, keepdims=True)
    return centre * lax.rsqrt(spread + EPSILON) * gain_row


def bucket_rows(box_left, box_top, bucket_count):
    buckets = jnp.arange(bucket_count)[None, :]
    across = (box_left[:, None] == buckets).astype(jnp.float32)
    down = (box_top[:, None] == buckets).astype(jnp.float32)
    return jnp.concatenate((across, down), axis=1)


def band_blocks(bias_table, head_count):
    bucket_count = bias_table.shape[0] // 2
    steps_range = jnp.arange(bucket_count)
    offsets = steps_range[:, None] - steps_range[None, :] + bucket_count
    picked = jnp.take(bias_table, offsets, axis=0)
    across = jnp.transpose(picked[:, :, :head_count], (2, 0, 1))
    down = jnp.transpose(picked[:, :, head_count:], (2, 0, 1))
    blank = jnp.zeros_like(across)
    upper = jnp.concatenate((across, blank), axis=2)
    lower = jnp.concatenate((blank, down), axis=2)
    return jnp.concatenate((upper, lower), axis=1)


def bias_from_blocks(onehots, blocks):
    partial_rows = jnp.einsum("la,hab->hlb", onehots, blocks, precision=PRECISE)
    return jnp.einsum("hlb,kb->hlk", partial_rows, onehots, precision=PRECISE)


def key_mask(key_count, slot_count):
    return jnp.where(jnp.arange(slot_count) < key_count, 0.0, MASKED).astype(jnp.float32)


def matmul(left_side, right_side):
    return jnp.dot(left_side, right_side, preferred_element_type=jnp.float32)


def matmul_back(left_side, weight):
    return lax.dot_general(
        left_side, weight, (((1,), (1,)), ((), ())), preferred_element_type=jnp.float32
    )


def matmul_outer(left_side, right_side):
    return lax.dot_general(
        left_side, right_side, (((0,), (0,)), ((), ())), preferred_element_type=jnp.float32
    )


def exact_gelu(value_in):
    return jax.nn.gelu(value_in, approximate=False)


def attend_forward(queries, key_rows, values, score_add, score_scale):
    scores = (
        jnp.einsum("qhd,khd->hqk", queries, key_rows, preferred_element_type=jnp.float32)
        * score_scale
        + score_add
    )
    row_max = jnp.max(scores, axis=-1, keepdims=True)
    expsum = jnp.exp(scores - row_max)
    row_total = jnp.sum(expsum, axis=-1, keepdims=True)
    weights = (expsum / row_total).astype(jnp.bfloat16)
    output = jnp.einsum("hqk,khd->qhd", weights, values, preferred_element_type=jnp.float32)
    return (output.astype(jnp.bfloat16), row_max + jnp.log(row_total))


def attend_backward(queries, key_rows, values, score_add, score_scale, log_total, grad_out):
    scores = (
        jnp.einsum("qhd,khd->hqk", queries, key_rows, preferred_element_type=jnp.float32)
        * score_scale
        + score_add
    )
    weights = jnp.exp(scores - log_total)
    d_weights = jnp.einsum("qhd,khd->hqk", grad_out, values, preferred_element_type=jnp.float32)
    d_scores = weights * (d_weights - jnp.sum(d_weights * weights, axis=-1, keepdims=True))
    low_scores = d_scores.astype(jnp.bfloat16)
    d_query = (
        jnp.einsum("hqk,khd->qhd", low_scores, key_rows, preferred_element_type=jnp.float32)
        * score_scale
    )
    d_key = (
        jnp.einsum("hqk,qhd->khd", low_scores, queries, preferred_element_type=jnp.float32)
        * score_scale
    )
    d_value = jnp.einsum(
        "hqk,qhd->khd", weights.astype(jnp.bfloat16), grad_out, preferred_element_type=jnp.float32
    )
    return (d_query, d_key, d_value, d_scores)


def body(
    states,
    counts,
    box_x,
    box_y,
    ln1_gain,
    ln2_gain,
    box_table,
    w_qkv,
    w_out,
    w_cq,
    w_ckv,
    w_cout,
    w_up,
    w_down,
    cotangent,
):
    page_count, slot_count, model_width = (states.shape[1], states.shape[2], states.shape[3])
    head_count = box_table.shape[2] // 2
    bucket_count = box_table.shape[1] // 2
    head_size = model_width // head_count
    score_scale = head_size ** (-0.5)
    row_count = page_count * slot_count
    stream_side = lax.axis_index("stream")
    own_count = jnp.take(counts, stream_side, axis=0)
    other_count = jnp.take(counts, 1 - stream_side, axis=0)
    table_local = box_table[0]
    blocks, block_pull = jax.vjp(lambda tab_arg: band_blocks(tab_arg, head_count), table_local)
    slot_index = jnp.arange(slot_count)[None, :]
    grid_side = jnp.where(own_count > GRID_SMALL * GRID_SMALL, GRID_LARGE, GRID_SMALL).astype(
        jnp.int32
    )[:, None]
    page_left = jnp.where(stream_side == 0, box_x, slot_index % grid_side)
    page_top = jnp.where(stream_side == 0, box_y, slot_index // grid_side)
    inputs = states[0].reshape(row_count, model_width).astype(jnp.float32)
    valid = (
        (jnp.arange(slot_count)[None, :] < own_count[:, None])
        .astype(jnp.float32)
        .reshape(row_count, 1)
    )
    normed, norm_pull = jax.vjp(norm_rows, inputs, ln1_gain[0])
    low_normed = normed.astype(jnp.bfloat16)
    cross_kv = matmul(low_normed, w_ckv[0]).astype(jnp.bfloat16)
    partner = swapped(cross_kv.reshape(page_count, slot_count, 2 * model_width), "stream", 0)
    joined = (
        matmul(low_normed, w_qkv[0])
        .astype(jnp.bfloat16)
        .reshape(page_count, slot_count, 3, head_count, head_size)
    )

    def self_forward(page_items):
        queries, key_rows, values, box_left, box_top, key_count = page_items
        onehots = bucket_rows(box_left, box_top, bucket_count)
        score_add = bias_from_blocks(onehots, blocks) + key_mask(key_count, slot_count)
        return attend_forward(queries, key_rows, values, score_add, score_scale)

    attended, self_total = lax.map(
        self_forward,
        (joined[:, :, 0], joined[:, :, 1], joined[:, :, 2], page_left, page_top, own_count),
    )
    attended_rows = attended.reshape(row_count, model_width)
    middle = inputs + matmul(attended_rows, w_out[0])
    low_middle = middle.astype(jnp.bfloat16)
    cross_query = (
        matmul(low_middle, w_cq[0])
        .astype(jnp.bfloat16)
        .reshape(page_count, slot_count, head_count, head_size)
    )
    partner_pairs = partner.reshape(page_count, slot_count, 2, head_count, head_size)

    def cross_forward(page_items):
        queries, key_rows, values, key_count = page_items
        return attend_forward(
            queries, key_rows, values, key_mask(key_count, slot_count), score_scale
        )

    crossed, cross_total = lax.map(
        cross_forward, (cross_query, partner_pairs[:, :, 0], partner_pairs[:, :, 1], other_count)
    )
    crossed_rows = crossed.reshape(row_count, model_width)
    after_cross = middle + matmul(crossed_rows, w_cout[0])
    second, second_pull = jax.vjp(norm_rows, after_cross, ln2_gain[0])
    low_second = second.astype(jnp.bfloat16)
    up_value = matmul(low_second, w_up[0])
    hidden, gelu_pull = jax.vjp(exact_gelu, up_value)
    low_hidden = hidden.astype(jnp.bfloat16)
    result = ((after_cross + matmul(low_hidden, w_down[0])) * valid).astype(jnp.bfloat16)
    out_grad = cotangent[0].reshape(row_count, model_width).astype(jnp.float32) * valid
    low_out_grad = out_grad.astype(jnp.bfloat16)
    w_down_grad = matmul_outer(low_hidden, low_out_grad)
    (d_up,) = gelu_pull(matmul_back(low_out_grad, w_down[0]))
    low_d_up = d_up.astype(jnp.bfloat16)
    w_up_grad = matmul_outer(low_second, low_d_up)
    d_after, ln2_grad = second_pull(matmul_back(low_d_up, w_up[0]))
    d_after = d_after + out_grad
    low_d_after = d_after.astype(jnp.bfloat16)
    w_cout_grad = matmul_outer(crossed_rows, low_d_after)
    d_crossed = (
        matmul_back(low_d_after, w_cout[0])
        .astype(jnp.bfloat16)
        .reshape(page_count, slot_count, head_count, head_size)
    )

    def cross_backward(page_items):
        queries, key_rows, values, key_count, log_total, grad_out = page_items
        d_query, d_key, d_value, d_scores = attend_backward(
            queries,
            key_rows,
            values,
            key_mask(key_count, slot_count),
            score_scale,
            log_total,
            grad_out,
        )
        return (
            d_query.astype(jnp.bfloat16),
            jnp.stack((d_key, d_value), axis=1).astype(jnp.bfloat16),
        )

    d_cross_query, d_partner = lax.map(
        cross_backward,
        (
            cross_query,
            partner_pairs[:, :, 0],
            partner_pairs[:, :, 1],
            other_count,
            cross_total,
            d_crossed,
        ),
    )
    returned = swapped(d_partner.reshape(page_count, slot_count, 2 * model_width), "stream", 0)
    d_cq_rows = d_cross_query.reshape(row_count, model_width)
    w_cq_grad = matmul_outer(low_middle, d_cq_rows)
    d_middle = d_after + matmul_back(d_cq_rows, w_cq[0])
    low_d_middle = d_middle.astype(jnp.bfloat16)
    w_out_grad = matmul_outer(attended_rows, low_d_middle)
    d_attended = (
        matmul_back(low_d_middle, w_out[0])
        .astype(jnp.bfloat16)
        .reshape(page_count, slot_count, head_count, head_size)
    )

    def self_backward(page_items):
        queries, key_rows, values, box_left, box_top, key_count, log_total, grad_out = page_items
        onehots = bucket_rows(box_left, box_top, bucket_count)
        score_add = bias_from_blocks(onehots, blocks) + key_mask(key_count, slot_count)
        d_query, d_key, d_value, d_scores = attend_backward(
            queries, key_rows, values, score_add, score_scale, log_total, grad_out
        )
        right_sums = jnp.einsum("hlk,kb->hlb", d_scores, onehots, precision=PRECISE)
        d_blocks = jnp.einsum("la,hlb->hab", onehots, right_sums, precision=PRECISE)
        return (jnp.stack((d_query, d_key, d_value), axis=1).astype(jnp.bfloat16), d_blocks)

    d_joined, block_terms = lax.map(
        self_backward,
        (
            joined[:, :, 0],
            joined[:, :, 1],
            joined[:, :, 2],
            page_left,
            page_top,
            own_count,
            self_total,
            d_attended,
        ),
    )
    (table_grad,) = block_pull(jnp.sum(block_terms, axis=0))
    d_qkv_rows = d_joined.reshape(row_count, 3 * model_width)
    returned_rows = returned.reshape(row_count, 2 * model_width)
    w_qkv_grad = matmul_outer(low_normed, d_qkv_rows)
    w_ckv_grad = matmul_outer(low_normed, returned_rows)
    d_normed = matmul_back(d_qkv_rows, w_qkv[0]) + matmul_back(returned_rows, w_ckv[0])
    d_inputs, ln1_grad = norm_pull(d_normed)
    states_grad = (d_inputs + d_middle).reshape(1, page_count, slot_count, model_width)
    summed = (
        lax.psum_scatter(ln1_grad, "page", scatter_dimension=0, tiled=True),
        lax.psum_scatter(ln2_grad, "page", scatter_dimension=0, tiled=True),
        lax.psum_scatter(table_grad, "page", scatter_dimension=0, tiled=True),
        lax.psum_scatter(w_qkv_grad, "page", scatter_dimension=0, tiled=True),
        lax.psum_scatter(w_out_grad, "page", scatter_dimension=0, tiled=True),
        lax.psum_scatter(w_cq_grad, "page", scatter_dimension=0, tiled=True),
        lax.psum_scatter(w_ckv_grad, "page", scatter_dimension=0, tiled=True),
        lax.psum_scatter(w_cout_grad, "page", scatter_dimension=0, tiled=True),
        lax.psum_scatter(w_up_grad, "page", scatter_dimension=0, tiled=True),
        lax.psum_scatter(w_down_grad, "page", scatter_dimension=0, tiled=True),
    )
    ln1_sum, ln2_sum, table_sum, qkv_sum, out_sum, cq_sum, ckv_sum, cout_sum, up_sum, down_sum = (
        summed
    )
    return (
        result.reshape(1, page_count, slot_count, model_width),
        states_grad,
        ln1_sum[None],
        ln2_sum[None],
        table_sum[None],
        qkv_sum[None],
        out_sum[None],
        cq_sum[None],
        ckv_sum[None],
        cout_sum[None],
        up_sum[None],
        down_sum[None],
    )


def solution(mesh):
    placed = (
        P("stream", "page", None, None),
        P(None, "page"),
        P("page", None),
        P("page", None),
        P("stream", None),
        P("stream", None),
        P("stream", None, None),
        P("stream", None, None),
        P("stream", None, None),
        P("stream", None, None),
        P("stream", None, None),
        P("stream", None, None),
        P("stream", None, None),
        P("stream", None, None),
        P("stream", "page", None, None),
    )
    return jax.shard_map(
        body,
        mesh=mesh,
        in_specs=placed,
        out_specs=(
            P("stream", "page", None, None),
            P("stream", "page", None, None),
            P("stream", "page"),
            P("stream", "page"),
            P("stream", "page", None),
            P("stream", "page", None),
            P("stream", "page", None),
            P("stream", "page", None),
            P("stream", "page", None),
            P("stream", "page", None),
            P("stream", "page", None),
            P("stream", "page", None),
        ),
        check_vma=False,
    )
```

profile of v0, /device:TPU:0, one launch (start us, length us, event | category | flops | bytes accessed | tf_op | source)
XLA Modules:
  0.0 821.4 jit_solution(13783801186821331242)
XLA Ops:
  11.8 5.1 fusion.34
  16.8 3.0 collective-permute-start
  29.2 15.5 %gather_fusion = f32[4096,24]{1,0:T(8,128)} fusion(f32[128,24]{1,0:T(8,128)} %bitcast.254, s32[4096]{0:T(1024)S(1)} %broadcast_clamp_fusion), kind=kCustom, calls=%fused_computation | custom fusion | bytes 802816 | tf_op jit(solution)/shard_map/jvp(jit(_take))/gather | solution.py:36
  44.8 3.7 copy.105
  50.7 5.4 convolution_convert_fusion
  56.1 5.5 copy.102
  61.6 11.0 %fusion.100 = f32[12,640,640]{1,2,0:T(8,128)} fusion(bf16[1,640,3,12,64]{1,4,3,2,0:T(8,128)(2,1)} %bitcast.255), kind=kOutput, calls=%fused_computation.135 | convolution fusion | flops 629145600 | bytes 21626880 | tf_op jit(solution)/shard_map/while/body/eval_jaxpr/qhd,khd->hqk/dot_general | solution.py:76
  74.6 20.4 %fusion.138 = (f32[12,640]{1,0:T(8,128)}, f32[12,640,640]{1,2,0:T(8,128)}) fusion(f32[640]{0:T(1024)S(1)} %copy-done.47, pred[640,128,1]{1,0,2:T(32,128)(4,1)S(1)} %add_bitcast_fusion.1, f32[12,128,640]{2,1,0:T(8,128)S(1)} %fusion.102, f32[12,640,640]{1,2,0:T(8,128)} %fusion.100), kind=kOutput, calls=%fused_computation.204 | convolution fusion | flops 7569400320 | bytes 43368960 | tf_op jit(solution)/shard_map/while/body/eval_jaxpr/hlb,kb->hlk/dot_general | solution.py:47
  95.0 9.8 %fusion = f32[12,640]{1,0:T(8,128)} fusion(f32[12,640,640]{1,2,0:T(8,128)} %get-tuple-element.166, f32[12,640]{1,0:T(8,128)} %get-tuple-element.165), kind=kLoop, calls=%fused_computation.14 | loop fusion | flops 9822720 | bytes 19722240 | tf_op jit(solution)/shard_map/while/body/eval_jaxpr/reduce_sum | solution.py:82
  104.9 11.4 %fusion.66 = bf16[12,64,640]{2,1,0:T(8,128)(2,1)} fusion(f32[12,640,640]{1,2,0:T(8,128)} %get-tuple-element.166, f32[12,640]{1,0:T(8,128)} %fusion, f32[12,640]{1,0:T(8,128)} %get-tuple-element.165, bf16[1,640,3,12,64]{1,4,3,2,0:T(8,128)(2,1)} %bitcast.256), kind=kOutput, calls=%fused_computation.104 | convolution fusion | flops 644382720 | bytes 21708800 | tf_op jit(solution)/shard_map/while/body/eval_jaxpr/hqk,khd->qhd/dot_general | solution.py:84
  116.3 2.9 fusion.35
  125.4 4.2 copy.108
  129.6 12.3 %fusion.139 = (f32[12,640]{1,0:T(8,128)}, f32[12,640,640]{1,2,0:T(8,128)}) fusion(f32[640]{0:T(1024)S(1)} %fusion.121, bf16[640,12,64]{0,2,1:T(8,128)(2,1)} %bitcast.264, bf16[1,640,2,12,64]{1,4,3,2,0:T(8,128)(2,1)} %bitcast.260), kind=kOutput, calls=%fused_computation.205 | convolution fusion | flops 643883520 | bytes 21660160 | tf_op jit(solution)/shard_map/while/body/eval_jaxpr/qhd,khd->hqk/dot_general | solution.py:76
  141.9 9.8 %fusion.1 = f32[12,640]{1,0:T(8,128)} fusion(f32[12,640,640]{1,2,0:T(8,128)} %get-tuple-element.168, f32[12,640]{1,0:T(8,128)} %get-tuple-element.167), kind=kLoop, calls=%fused_computation.15 | loop fusion | flops 9822720 | bytes 19722240 | tf_op jit(solution)/shard_map/while/body/eval_jaxpr/reduce_sum | solution.py:82
  153.1 10.6 %fusion.65 = bf16[12,64,640]{2,1,0:T(8,128)(2,1)S(1)} fusion(f32[12,640,640]{1,2,0:T(8,128)} %get-tuple-element.168, f32[12,640]{1,0:T(8,128)} %fusion.1, f32[12,640]{1,0:T(8,128)} %get-tuple-element.167, bf16[1,640,2,12,64]{1,4,3,2,0:T(8,128)(2,1)} %bitcast.261), kind=kOutput, calls=%fused_computation.103 | convolution fusion | flops 644382720 | bytes 21708800 | tf_op jit(solution)/shard_map/while/body/eval_jaxpr/hqk,khd->qhd/dot_general | solution.py:84
  165.3 24.4 %multiply_convert_fusion.1 = (bf16[640,3072]{1,0:T(8,128)(2,1)}, f32[640,3072]{1,0:T(8,128)}, f32[640,3072]{1,0:T(8,128)}) fusion(bf16[1,768,3072]{2,1,0:T(8,128)(2,1)} %param.27, f32[640,768]{1,0:T(8,128)S(1)} %get-tuple-element.170, f32[768]{0:T(1024)S(1)} %reduce.4, f32[640]{0:T(1024)S(1)} %fusion.123, f32[640]{0:T(1024)S(1)} %broadcast_multiply_fusion), kind=kOutput, calls=%fused_computation.27 | convolution fusion | flops 3149660160 | bytes 26353664 | tf_op jit(solution)/shard_map/dot_general | solution.py:55
  189.6 10.3 %add_convert_fusion = bf16[640,3072]{1,0:T(8,128)(2,1)S(1)} fusion(f32[640,3072]{1,0:T(8,128)} %get-tuple-element.158, f32[640,3072]{1,0:T(8,128)} %get-tuple-element.171, bf16[1,3072,768]{2,1,0:T(8,128)(2,1)} %param.28, bf16[1,1,640,768]{3,2,1,0:T(8,128)(2,1)S(1)} %copy-done.26, f32[640]{0:T(1024)S(1)} %fusion.119), kind=kOutput, calls=%fused_computation.26 | convolution fusion | flops 3048898560 | bytes 25364992 | tf_op jit(solution)/shard_map/dot_general | solution.py:59
  199.9 4.1 multiply_reduce_fusion.2
  207.2 2.5 fusion.141
  212.0 18.1 %multiply_reduce_fusion.1 = (f32[12,640]{1,0:T(8,128)S(1)}, f32[12,640,640]{1,2,0:T(8,128)}) fusion(f32[12,640,640]{1,2,0:T(8,128)} %get-tuple-element.168, f32[12,640]{1,0:T(8,128)} %log_add_fusion, bf16[640,12,64]{0,2,1:T(8,128)(2,1)} %bitcast.266, bf16[1,640,2,12,64]{1,4,3,2,0:T(8,128)(2,1)} %bitcast.262), kind=kOutput, calls=%fused_computation.5 | convolution fusion | flops 643883520 | bytes 41359360 | tf_op jit(solution)/shard_map/while/body/eval_jaxpr/qhd,khd->hqk/dot_general | solution.py:95
  230.2 14.1 %multiply_convert_fusion = bf16[12,640,640]{1,2,0:T(8,128)(2,1)S(1)} fusion(f32[12,640,640]{1,2,0:T(8,128)} %get-tuple-element.174, f32[12,640,640]{1,2,0:T(8,128)} %get-tuple-element.168, f32[12,640]{1,0:T(8,128)S(1)} %get-tuple-element.173, f32[12,640]{1,0:T(8,128)S(1)} %copy-done.27), kind=kLoop, calls=%fused_computation.4 | loop fusion | flops 19660800 | bytes 49213440 | tf_op jit(solution)/shard_map/while/body/eval_jaxpr/convert_element_type | solution.py:97
  246.0 2.3 copy-done.1
  249.3 2.6 fusion.109
  252.0 3.8 convolution_add_fusion
  257.1 2.5 fusion.106
  259.7 7.5 fusion.84
  267.2 10.0 %fusion.73 = bf16[640,1,12,64]{0,3,2,1:T(8,128)(2,1)S(1)} fusion(bf16[640,12,64]{0,2,1:T(8,128)(2,1)S(1)} %bitcast.267, f32[12,640,640]{1,2,0:T(8,128)} %get-tuple-element.168, f32[12,640]{1,0:T(8,128)S(1)} %copy-done.28), kind=kOutput, calls=%fused_computation.110 | convolution fusion | flops 639467520 | bytes 21657600 | tf_op jit(solution)/shard_map/while/body/eval_jaxpr/hqk,qhd->khd/dot_general | solution.py:106
  277.6 44.3 %collective-permute-done.1 = bf16[1,640,1536]{1,2,0:T(8,128)(2,1)S(1)} collective-permute-done((bf16[1,640,1536]{1,2,0:T(8,128)(2,1)S(1)}, bf16[1,640,1536]{1,2,0:T(8,128)(2,1)S(1)}, u32[]{:S(2)}, u32[]{:S(2)}) %collective-permute-start.1) | collective-permute-done | bytes 1966112 | tf_op jit(solution)/shard_map/ppermute | solution.py:16
  323.2 4.5 fusion.55
  329.5 3.8 convolution_convert_fusion.2
  335.5 17.8 %multiply_reduce_fusion = (f32[12,640]{1,0:T(8,128)S(1)}, f32[12,640,640]{1,2,0:T(8,128)}) fusion(f32[12,640,640]{1,2,0:T(8,128)} %get-tuple-element.166, f32[12,640]{1,0:T(8,128)} %log_add_fusion.1, bf16[640,12,64]{0,2,1:T(8,128)(2,1)} %bitcast.268, bf16[1,640,3,12,64]{1,4,3,2,0:T(8,128)(2,1)} %bitcast.257), kind=kOutput, calls=%fused_computation.3 | convolution fusion | flops 643883520 | bytes 41359360 | tf_op jit(solution)/shard_map/while/body/eval_jaxpr/qhd,khd->hqk/dot_general | solution.py:95
  353.3 14.7 %fusion.19 = bf16[12,640,640]{1,2,0:T(8,128)(2,1)S(1)} fusion(f32[12,640,640]{1,2,0:T(8,128)} %get-tuple-element.176, f32[12,640]{1,0:T(8,128)S(1)} %get-tuple-element.175, f32[12,640,640]{1,2,0:T(8,128)} %get-tuple-element.166, f32[12,640]{1,0:T(8,128)S(1)} %copy-done.24), kind=kLoop, calls=%fused_computation.42 | loop fusion | flops 19660800 | bytes 49213440 | tf_op jit(solution)/shard_map/while/body/eval_jaxpr/convert_element_type | solution.py:97
  367.9 3.2 fusion.83
  372.9 10.3 %fusion.76 = bf16[640,1,12,64]{0,3,2,1:T(8,128)(2,1)S(1)} fusion(bf16[640,12,64]{0,2,1:T(8,128)(2,1)S(1)} %bitcast.269, f32[12,640,640]{1,2,0:T(8,128)} %get-tuple-element.166, f32[12,640]{1,0:T(8,128)S(1)} %copy-done.24), kind=kOutput, calls=%fused_computation.111 | convolution fusion | flops 639467520 | bytes 21657600 | tf_op jit(solution)/shard_map/while/body/eval_jaxpr/hqk,qhd->khd/dot_general | solution.py:106
  385.4 6.0 fusion.132
  391.4 10.4 %fusion.130 = f32[768,3072]{1,0:T(8,128)} fusion(bf16[640,3072]{1,0:T(8,128)(2,1)} %copy-done.18, f32[640,768]{1,0:T(8,128)} %copy-done.2, f32[768]{0:T(1024)S(1)} %reduce.4, f32[640]{0:T(1024)S(1)} %fusion.123, f32[640]{0:T(1024)S(1)} %broadcast_multiply_fusion), kind=kOutput, calls=%fused_computation.201 | convolution fusion | flops 3021864960 | bytes 15343616 | tf_op jit(solution)/shard_map/dot_general | solution.py:65
  402.5 9.9 %fusion.93 = f32[3072,768]{1,0:T(8,128)} fusion(bf16[640,3072]{1,0:T(8,128)(2,1)} %get-tuple-element.157, bf16[1,1,640,768]{3,2,1,0:T(8,128)(2,1)} %param.29, f32[640]{0:T(1024)S(1)} %copy-done.49), kind=kOutput, calls=%fused_computation.125 | convolution fusion | flops 3021373440 | bytes 14354944 | tf_op jit(solution)/shard_map/dot_general | solution.py:65
  414.9 21.5 %fusion.18 = f32[12,640,128]{1,2,0:T(8,128)} fusion(pred[640,128,1]{1,0,2:T(32,128)(4,1)} %copy-done.20, f32[12,640,640]{1,2,0:T(8,128)} %get-tuple-element.176, f32[12,640,640]{1,2,0:T(8,128)} %get-tuple-element.166, f32[12,640]{1,0:T(8,128)} %copy-done.29, f32[12,640]{1,0:T(8,128)} %log_add_fusion.1), kind=kOutput, calls=%fused_computation.41 | convolution fusion | flops 7564492800 | bytes 43397120 | tf_op jit(solution)/shard_map/while/body/eval_jaxpr/hlk,kb->hlb/dot_general | solution.py:261
  436.4 4.0 convolution_bitcast_fusion
  441.6 4.2 copy.136
  445.8 23.4 %scatter_custom_fusion = f32[128,24]{1,0:T(8,128)} fusion(s32[4096]{0:T(1024)} %reshape.496, f32[4096,24]{1,0:T(8,128)} %bitcast.275, f32[]{:T(128)} %constant.129.clone.1), kind=kCustom, calls=%fused_computation.165 | custom fusion | flops 98304 | bytes 12800 | tf_op jit(solution)/shard_map/transpose(jvp(jit(_take)))/scatter-add | solution.py:36
  469.2 4.5 fusion.29
  473.8 6.6 fusion.79
  484.2 63.7 %all-reduce.7 = (f32[768]{0:T(1024)}, f32[768]{0:T(1024)}, f32[128,24]{1,0:T(8,128)}) all-reduce(f32[768]{0:T(1024)} %get-tuple-element.138, f32[768]{0:T(1024)} %get-tuple-element.136, f32[128,24]{1,0:T(8,128)} %scatter_custom_fusion), channel_id=2, replica_groups=mesh['stream'=2,'page'=16] {'page'}, use_global_device_ids=true, to_apply=%region_15.16.clone | all-reduce | flops 4608 | bytes 36864
  552.4 4.4 add_bitcast_fusion
  556.8 25.7 %reduce-scatter.8.cloned.1.call-done = f32[48,2304]{1,0:T(8,128)} async-done(((f32[768,2304]{1,0:T(8,128)}), f32[48,2304]{1,0:T(8,128)}) %reduce-scatter.8.cloned.1.call-update) | async-done | bytes 442384 | tf_op jit(solution)/shard_map/reduce_scatter | solution.py:290
  582.5 116.0 %reduce-scatter.18.cloned.1.call-done = f32[48,3072]{1,0:T(8,128)} async-done(((f32[768,3072]{1,0:T(8,128)}), f32[48,3072]{1,0:T(8,128)}) %reduce-scatter.18.cloned.1.call-update) | async-done | bytes 589840 | tf_op jit(solution)/shard_map/reduce_scatter | solution.py:295
  698.5 115.8 %reduce-scatter.20.cloned.1.call-done = f32[192,768]{1,0:T(8,128)} async-done(((f32[3072,768]{1,0:T(8,128)}), f32[192,768]{1,0:T(8,128)}) %reduce-scatter.20.cloned.1.call-update) | async-done | bytes 589840 | tf_op jit(solution)/shard_map/reduce_scatter | solution.py:296
  (193 shorter events, 56.1 us)
Async XLA Ops:
  7.2 43.5 %copy-start = (bf16[1,768,2304]{2,1,0:T(8,128)(2,1)S(1)}, bf16[1,768,2304]{2,1,0:T(8,128)(2,1)}, u32[]{:S(2)}) copy-start(bf16[1,768,2304]{2,1,0:T(8,128)(2,1)} %param.22) | copy-start | bytes 10616836
  7.2 549.6 %reduce-scatter.16.cloned.1.call-start = ((), (), s32[]{:S(2)}) async-start(), calls=%async_computation.11 | async-start | bytes 2506752 | tf_op jit(solution)/shard_map/reduce_scatter | solution.py:294
  8.8 8.0 copy-start.32
  11.0 5.8 copy-start.35
  11.7 5.1 copy-start.40
  11.8 9.3 %copy-start.52 = (s32[2,1]{0,1:T(1,128)S(1)}, s32[2,1]{0,1:T(1,128)}, u32[]{:S(2)}) copy-start(s32[2,1]{0,1:T(1,128)} %param.16) | copy-start | bytes 28
  16.8 108.5 %collective-permute-start = (bf16[1,640,1536]{2,1,0:T(8,128)(2,1)}, bf16[1,640,1536]{2,1,0:T(8,128)(2,1)}, u32[]{:S(2)}, u32[]{:S(2)}) collective-permute-start(bf16[1,640,1536]{2,1,0:T(8,128)(2,1)} %fusion.34), channel_id=1, source_target_pairs={{0,16},{16,0},{1,17},{17,1},{2,18},{18,2},{3,19},{19,3},{4,20},{20... | collective-permute-start | bytes 5898248 | tf_op jit(solution)/shard_map/ppermute | solution.py:16
  44.8 5.9 copy-start.33
  44.8 5.9 copy-start.36
  44.8 5.9 copy-start.41
  61.6 11.0 %copy-start.30 = (pred[640,64]{1,0:T(32,128)(4,1)S(1)}, pred[640,64]{1,0:T(32,128)(4,1)}, u32[]{:S(2)}) copy-start(pred[640,64]{1,0:T(32,128)(4,1)} %iota_compare_fusion.4) | copy-start | bytes 122884
  61.6 11.0 %copy-start.31 = (pred[640,64]{1,0:T(32,128)(4,1)S(1)}, pred[640,64]{1,0:T(32,128)(4,1)}, u32[]{:S(2)}) copy-start(pred[640,64]{1,0:T(32,128)(4,1)} %iota_compare_fusion.5) | copy-start | bytes 122884
  61.6 11.2 %copy-start.21 = (f32[12,64,64]{1,2,0:T(8,128)S(1)}, f32[12,64,64]{1,2,0:T(8,128)}, u32[]{:S(2)}) copy-start(f32[12,64,64]{1,2,0:T(8,128)} %get-tuple-element.161) | copy-start | bytes 589828
  61.6 11.2 %copy-start.22 = (f32[12,64,64]{1,2,0:T(8,128)S(1)}, f32[12,64,64]{1,2,0:T(8,128)}, u32[]{:S(2)}) copy-start(f32[12,64,64]{1,2,0:T(8,128)} %get-tuple-element.162) | copy-start | bytes 589828
  72.7 22.3 %copy-start.20 = (pred[640,128,1]{1,0,2:T(32,128)(4,1)}, pred[640,128,1]{1,0,2:T(32,128)(4,1)S(1)}, u32[]{:S(2)}) copy-start(pred[640,128,1]{1,0,2:T(32,128)(4,1)S(1)} %add_bitcast_fusion.1) | copy-start | bytes 245764
  104.9 11.4 %copy-start.51 = (f32[1,768]{1,0:T(1,128)S(1)}, f32[1,768]{1,0:T(1,128)}, u32[]{:S(2)}) copy-start(f32[1,768]{1,0:T(1,128)} %param.20) | copy-start | bytes 9220
  125.3 126.7 %copy-start.48 = (f32[640]{0:T(1024)}, f32[640]{0:T(1024)S(1)}, u32[]{:S(2)}) copy-start(f32[640]{0:T(1024)S(1)} %fusion.119) | copy-start | bytes 7684
  153.1 10.6 %copy-start.15 = (f32[640,768]{1,0:T(8,128)S(1)}, f32[640,768]{1,0:T(8,128)}, u32[]{:S(2)}) copy-start(f32[640,768]{1,0:T(8,128)} %copy-done.14) | copy-start | bytes 5898244
  153.1 10.6 %copy-start.23 = (bf16[1,768,768]{2,1,0:T(8,128)(2,1)S(1)}, bf16[1,768,768]{2,1,0:T(8,128)(2,1)}, u32[]{:S(2)}) copy-start(bf16[1,768,768]{2,1,0:T(8,128)(2,1)} %param.26) | copy-start | bytes 3538948
  163.7 36.2 %slice-start = ((s8[4718592]{0:T(1024)(128)(4,1)}), s8[4194304]{0:T(1024)(128)(4,1)S(1)}, s32[]{:S(2)}) async-start(s8[4718592]{0:T(1024)(128)(4,1)} %bitcast.281), calls=%async_computation.14 | async-start | bytes 8388608
  164.8 39.2 %copy-start.2 = (f32[640,768]{1,0:T(8,128)}, f32[640,768]{1,0:T(8,128)S(1)}, u32[]{:S(2)}) copy-start(f32[640,768]{1,0:T(8,128)S(1)} %get-tuple-element.170) | copy-start | bytes 5898244
  165.2 24.4 %copy-start.26 = (bf16[1,1,640,768]{3,2,1,0:T(8,128)(2,1)S(1)}, bf16[1,1,640,768]{3,2,1,0:T(8,128)(2,1)}, u32[]{:S(2)}) copy-start(bf16[1,1,640,768]{3,2,1,0:T(8,128)(2,1)} %param.29) | copy-start | bytes 2949124
  165.2 34.7 %slice-start.1 = ((s8[4718592]{0:T(1024)(128)(4,1)}), s8[524288]{0:T(1024)(128)(4,1)S(1)}, s32[]{:S(2)}) async-start(s8[4718592]{0:T(1024)(128)(4,1)} %bitcast.281), calls=%async_computation.15 | async-start | bytes 1048576
  211.9 344.8 %reduce-scatter.12.cloned.1.call-start = ((), (), s32[]{:S(2)}) async-start(), calls=%async_computation.9 | async-start | bytes 2506752 | tf_op jit(solution)/shard_map/reduce_scatter | solution.py:292
  212.0 18.2 %copy-start.27 = (f32[12,640]{1,0:T(8,128)S(1)}, f32[12,640]{1,0:T(8,128)}, u32[]{:S(2)}) copy-start(f32[12,640]{1,0:T(8,128)} %log_add_fusion) | copy-start | bytes 92164
  230.2 14.2 %copy-start.8 = (bf16[1,640,1536]{1,2,0:T(8,128)(2,1)S(1)}, bf16[1,640,1536]{1,2,0:T(8,128)(2,1)}, u32[]{:S(2)}) copy-start(bf16[1,640,1536]{1,2,0:T(8,128)(2,1)} %copy.108) | copy-start | bytes 5898244
  244.3 5.0 copy-start.16
  251.9 304.8 %reduce-scatter.10.cloned.1.call-start = ((), (), s32[]{:S(2)}) async-start(), calls=%async_computation.8 | async-start | bytes 2506752 | tf_op jit(solution)/shard_map/reduce_scatter | solution.py:291
  252.0 5.1 copy-start.25
  259.6 297.1 %reduce-scatter.14.cloned.1.call-start = ((), (), s32[]{:S(2)}) async-start(), calls=%async_computation.10 | async-start | bytes 5013504 | tf_op jit(solution)/shard_map/reduce_scatter | solution.py:293
  259.7 7.6 copy-start.9
  259.7 7.6 copy-start.28
  277.3 45.9 %copy-start.5 = (bf16[1,1,640,768]{3,2,1,0:T(8,128)(2,1)S(1)}, bf16[1,1,640,768]{3,2,1,0:T(8,128)(2,1)}, u32[]{:S(2)}) copy-start(bf16[1,1,640,768]{3,2,1,0:T(8,128)(2,1)} %param.15) | copy-start | bytes 2949124
  277.3 45.9 %copy-start.34 = (f32[640]{0:T(1024)S(1)}, f32[640]{0:T(1024)}, u32[]{:S(2)}) copy-start(f32[640]{0:T(1024)} %copy-done.32) | copy-start | bytes 7684
  277.3 45.9 %copy-start.37 = (f32[640]{0:T(1024)S(1)}, f32[640]{0:T(1024)}, u32[]{:S(2)}) copy-start(f32[640]{0:T(1024)} %copy-done.35) | copy-start | bytes 7684
  277.3 45.9 %copy-start.42 = (f32[768]{0:T(1024)S(1)}, f32[768]{0:T(1024)}, u32[]{:S(2)}) copy-start(f32[768]{0:T(1024)} %copy-done.40) | copy-start | bytes 9220
  277.6 44.4 %collective-permute-start.1 = (bf16[1,640,1536]{1,2,0:T(8,128)(2,1)S(1)}, bf16[1,640,1536]{1,2,0:T(8,128)(2,1)S(1)}, u32[]{:S(2)}, u32[]{:S(2)}) collective-permute-start(bf16[1,640,1536]{1,2,0:T(8,128)(2,1)S(1)} %bitcast.276), channel_id=1, source_target_pairs={{0,16},{16,0},{1,17},{17,1},{2,18},{18,2},{3,19},{19,3},{4,20},{20... | collective-permute-start | bytes 5898248 | tf_op jit(solution)/shard_map/ppermute | solution.py:16
  327.8 254.7 %reduce-scatter.8.cloned.1.call-start = ((), (), s32[]{:S(2)}) async-start(), calls=%async_computation.7 | async-start | bytes 7520256 | tf_op jit(solution)/shard_map/reduce_scatter | solution.py:290
  335.5 17.8 %copy-start.24 = (f32[12,640]{1,0:T(8,128)S(1)}, f32[12,640]{1,0:T(8,128)}, u32[]{:S(2)}) copy-start(f32[12,640]{1,0:T(8,128)} %log_add_fusion.1) | copy-start | bytes 92164
  353.3 14.7 %copy-start.29 = (f32[12,640]{1,0:T(8,128)}, f32[12,640]{1,0:T(8,128)S(1)}, u32[]{:S(2)}) copy-start(f32[12,640]{1,0:T(8,128)S(1)} %get-tuple-element.175) | copy-start | bytes 92164
  353.3 14.7 %copy-start.4 = (bf16[640,2304]{0,1:T(8,128)(2,1)S(1)}, bf16[640,2304]{0,1:T(8,128)(2,1)}, u32[]{:S(2)}) copy-start(bf16[640,2304]{0,1:T(8,128)(2,1)} %copy.102) | copy-start | bytes 8847364
  391.4 307.1 %reduce-scatter.18.cloned.1.call-start = ((), (), s32[]{:S(2)}) async-start(), calls=%async_computation.12 | async-start | bytes 10027008 | tf_op jit(solution)/shard_map/reduce_scatter | solution.py:295
  401.8 412.5 %reduce-scatter.20.cloned.1.call-start = ((), (), s32[]{:S(2)}) async-start(), calls=%async_computation.13 | async-start | bytes 10027008 | tf_op jit(solution)/shard_map/reduce_scatter | solution.py:296
  469.2 4.5 copy-start.3
  473.7 6.7 copy-start.7
  473.8 6.7 copy-start.44
  473.8 6.7 copy-start.53
  473.8 6.7 copy-start.55
  (22 other events, 46.3 us)
Sparse Core Ops, SparseCore 0:
  212.1 63.2 reduce-scatter.15
  280.2 62.0 reduce-scatter.11
  346.6 62.0 reduce-scatter.9
  413.5 74.6 reduce-scatter.13
  492.6 89.8 reduce-scatter.7
  587.6 110.8 reduce-scatter.17
  703.1 111.1 reduce-scatter.19
where the time goes:
time: 825 us; the launch traced here: 821 us
  waiting for transfers between devices  302 us (37%)
  matrix products  280 us (34%)
  other arithmetic  95 us (12%)
  blocking collectives  63.7 us (8%)
  local copies, waits for them, and re-layouts  59.7 us (7%)
  between operations  17.8 us (2%)
    reduce_scatter x1, waiting for transfers between devices, body(): lax.psum_scatter(w_up_grad, 'page', scatter_dimension=0, tiled=True)  116 us
    reduce_scatter x1, waiting for transfers between devices, body(): lax.psum_scatter(w_down_grad, 'page', scatter_dimension=0, tiled=True)  116 us
    unnamed x1, blocking collectives  63.7 us
    dot_general x7, matrix products, matmul(): return jnp.dot(left_side, right_side, preferred_element_type=jnp.float32)  47.4 us
    ppermute x2, waiting for transfers between devices, swapped(): lax.ppermute(shard, axis, [(i, i ^ 1 << bit) for i in range(lax.axis_size...  44.3 us
    dot_general x7, matrix products, matmul_outer(): lax.dot_general(left_side, right_side, (((0,), (0,)), ((), ())), preferre...  38.3 us
    dot_general x2, matrix products, attend_backward(): jnp.einsum('qhd,khd->hqk', grad_out, values, preferred_element_type=jnp.f...  35.9 us
    dot_general x7, matrix products, matmul_back(): lax.dot_general(left_side, weight, (((1,), (1,)), ((), ())), preferred_el...  30.5 us
  transfers between devices with their start and end apart: 9, of which 4 were waited for; matrix products, arithmetic and copies ran while one was open for 40% of the time, Pallas kernels for 0%

commit v1 on v0

v1 whole, which is shorter than its diff:
```python
import functools

import jax
import jax.numpy as jnp
from jax import lax
from jax.experimental import pallas as pl
from jax.experimental.pallas import tpu as pltpu
from jax.sharding import PartitionSpec as P

GRID_SMALL = 16
GRID_LARGE = 24
EPSILON = 1e-05
MASKED = -1000000000.0
BF = jnp.bfloat16
F32 = jnp.float32
WIDE = 128


def contract(left, right, left_dim, right_dim):
    return lax.dot_general(
        left, right, (((left_dim,), (right_dim,)), ((), ())), preferred_element_type=F32
    )


def params(mib=48):
    return pltpu.CompilerParams(vmem_limit_bytes=mib << 20)


def cost(us):
    return pl.CostEstimate(flops=int(us * 1.1e9), bytes_accessed=1 << 20, transcendentals=0)


def swapped(shard, axis, mask):
    return lax.ppermute(shard, axis, [(i, i ^ mask) for i in range(lax.axis_size(axis))])


def pieces(row):
    high = row.astype(BF).astype(F32)
    rest = row - high
    middle = rest.astype(BF).astype(F32)
    return high, middle, rest - middle


def extra_rows(rows, count):
    index = lax.broadcasted_iota(jnp.int32, (16, count), 0)
    block = jnp.zeros((16, count), F32)
    for place, row in enumerate(rows):
        block = jnp.where(index == place, row, block)
    return block.astype(BF)


def forward_kernel(has_bias, scale, *refs):
    if has_bias:
        q_ref, k_ref, v_ref, mask_ref, band_ref, onehot_ref, o_ref, lse_ref = refs
        onehot = onehot_ref[...]
    else:
        q_ref, k_ref, v_ref, mask_ref, o_ref, lse_ref = refs
    count = q_ref.shape[0]
    half = WIDE // 2
    queries = (q_ref[...] * scale).T
    key_rows = k_ref[...].T
    values = v_ref[...].T
    ones = jnp.ones((1, count), F32)
    query_extra = extra_rows([ones], count)
    key_extra = extra_rows([mask_ref[...]], count)
    outs = []
    for side in range(2):
        part = slice(half * side, half * side + half)
        if has_bias:
            band = contract(band_ref[side], onehot, 1, 0).astype(BF)
            left = jnp.concatenate([key_rows[part], onehot, key_extra], 0)
            right = jnp.concatenate([queries[part], band, query_extra], 0)
        else:
            left = jnp.concatenate([key_rows[part], key_extra], 0)
            right = jnp.concatenate([queries[part], query_extra], 0)
        scores = contract(left, right, 0, 0)
        top = jnp.max(scores, axis=0, keepdims=True)
        weights = jnp.exp(scores - top).astype(BF)
        output = contract(jnp.concatenate([values[part], query_extra], 0), weights, 1, 0)
        total = output[half : half + 1]
        outs.append(output[:half] * (1.0 / total))
        lse_ref[0, side : side + 1, :] = top + jnp.log(total)
    o_ref[...] = jnp.concatenate(outs, 0).astype(BF).T


def backward_kernel(has_bias, scale, *refs):
    if has_bias:
        (q_ref, k_ref, v_ref, do_ref, o_ref, lse_ref, mask_ref, band_ref, onehot_ref, flipped_ref) = refs[:10]
        dq_ref, dkv_ref, db_ref = refs[10:]
        onehot = onehot_ref[...]
        flipped = flipped_ref[...]
    else:
        q_ref, k_ref, v_ref, do_ref, o_ref, lse_ref, mask_ref = refs[:7]
        dq_ref, dkv_ref = refs[7:]
    count = q_ref.shape[0]
    half = WIDE // 2
    queries = (q_ref[...] * scale).T
    key_rows = k_ref[...].T
    values = v_ref[...].T
    grad_out = do_ref[...].T
    product = grad_out.astype(F32) * o_ref[...].T.astype(F32)
    ones = jnp.ones((1, count), F32)
    key_extra = extra_rows([ones, ones, ones, mask_ref[...]], count)
    value_extra = extra_rows([ones, ones, ones], count)
    d_queries, d_keys, d_values = [], [], []
    for side in range(2):
        part = slice(half * side, half * side + half)
        lse_rows = extra_rows([*pieces(-lse_ref[0, side : side + 1, :]), ones], count)
        delta = jnp.sum(product[part], axis=0, keepdims=True)
        delta_rows = extra_rows(list(pieces(-delta)), count)
        if has_bias:
            band = contract(band_ref[side], onehot, 1, 0).astype(BF)
            left = jnp.concatenate([queries[part], band, lse_rows], 0)
            right = jnp.concatenate([key_rows[part], onehot, key_extra], 0)
        else:
            left = jnp.concatenate([queries[part], lse_rows], 0)
            right = jnp.concatenate([key_rows[part], key_extra], 0)
        weights = jnp.exp(contract(left, right, 0, 0))
        d_weights = contract(
            jnp.concatenate([grad_out[part], delta_rows], 0),
            jnp.concatenate([values[part], value_extra], 0),
            0,
            0,
        )
        d_scores = (weights * d_weights).astype(BF)
        d_values.append(contract(grad_out[part], weights.astype(BF), 1, 0))
        d_keys.append(contract(queries[part], d_scores, 1, 0))
        scaled = key_rows[part] * scale
        if has_bias:
            both = contract(jnp.concatenate([scaled, onehot], 0), d_scores, 1, 1)
            d_queries.append(both[:half])
            db_ref[side] = contract(flipped, both[half:].astype(BF), 1, 1)
        else:
            d_queries.append(contract(scaled, d_scores, 1, 1))
    dq_ref[...] = jnp.concatenate(d_queries, 0).astype(BF).T
    dkv_ref[0] = jnp.concatenate(d_keys, 0).astype(BF).T
    dkv_ref[1] = jnp.concatenate(d_values, 0).astype(BF).T


def column(first):
    return lambda i: (0, first + i)


def attend_forward(query_rows, key_value_rows, first, mask, bias, scale, us):
    count = query_rows.shape[0]
    pairs = key_value_rows.shape[1] // WIDE // (3 if first else 2)
    block = lambda start: pl.BlockSpec((count, WIDE), column(start))
    row = pl.BlockSpec((1, count), lambda i: (0, 0))
    wide = pl.BlockSpec((WIDE, count), lambda i: (0, 0))
    specs = [block(0), block(first), block(first + pairs), row]
    operands = [query_rows, key_value_rows, key_value_rows, mask]
    if bias is not None:
        specs += [pl.BlockSpec((2, WIDE, WIDE), lambda i: (i, 0, 0)), wide]
        operands += [bias[0], bias[1]]
    return pl.pallas_call(
        functools.partial(forward_kernel, bias is not None, scale),
        grid=(pairs,),
        in_specs=specs,
        out_specs=[block(0), pl.BlockSpec((1, 2, count), lambda i: (i, 0, 0))],
        out_shape=[
            jax.ShapeDtypeStruct((count, pairs * WIDE), BF),
            jax.ShapeDtypeStruct((pairs, 2, count), F32),
        ],
        compiler_params=params(),
        cost_estimate=cost(us),
    )(*operands)


def attend_backward(query_rows, key_value_rows, first, grad_out, output, lse, mask, bias, scale, us):
    count = query_rows.shape[0]
    pairs = lse.shape[0]
    block = lambda start: pl.BlockSpec((count, WIDE), column(start))
    row = pl.BlockSpec((1, count), lambda i: (0, 0))
    wide = pl.BlockSpec((WIDE, count), lambda i: (0, 0))
    band = pl.BlockSpec((2, WIDE, WIDE), lambda i: (i, 0, 0))
    specs = [
        block(0),
        block(first),
        block(first + pairs),
        block(0),
        block(0),
        pl.BlockSpec((1, 2, count), lambda i: (i, 0, 0)),
        row,
    ]
    operands = [query_rows, key_value_rows, key_value_rows, grad_out, output, lse, mask]
    out_specs = [block(0), pl.BlockSpec((2, count, WIDE), lambda i: (0, 0, i))]
    out_shape = [
        jax.ShapeDtypeStruct((count, pairs * WIDE), BF),
        jax.ShapeDtypeStruct((2, count, pairs * WIDE), BF),
    ]
    if bias is not None:
        specs += [band, wide, wide]
        operands += list(bias)
        out_specs.append(band)
        out_shape.append(jax.ShapeDtypeStruct((2 * pairs, WIDE, WIDE), F32))
    return pl.pallas_call(
        functools.partial(backward_kernel, bias is not None, scale),
        grid=(pairs,),
        in_specs=specs,
        out_specs=out_specs,
        out_shape=out_shape,
        compiler_params=params(),
        cost_estimate=cost(us),
    )(*operands)


def same_block(shape):
    rows = lax.broadcasted_iota(jnp.int32, shape, 0) // (WIDE // 2)
    columns = lax.broadcasted_iota(jnp.int32, shape, 1) // (WIDE // 2)
    return rows == columns


def band_kernel(table_ref, band_ref):
    heads = band_ref.shape[0]
    shape = (WIDE, WIDE)
    keep = same_block(shape)
    lower = lax.broadcasted_iota(jnp.int32, shape, 0) >= WIDE // 2
    for head in range(heads):
        across = jnp.broadcast_to(table_ref[head : head + 1, :], shape)
        down = jnp.broadcast_to(table_ref[heads + head : heads + head + 1, :], shape)
        rolled = pltpu.roll(jnp.where(lower, down, across), WIDE // 2, 1, stride=1, stride_axis=0)
        band_ref[head] = jnp.where(keep, rolled, 0.0).astype(BF)


def make_bands(table):
    heads = table.shape[1] // 2
    return pl.pallas_call(
        band_kernel,
        out_shape=jax.ShapeDtypeStruct((heads, WIDE, WIDE), BF),
        compiler_params=params(),
        cost_estimate=cost(3),
    )(table.T)


def unband_kernel(grad_ref, table_ref):
    heads = grad_ref.shape[0]
    half = WIDE // 2
    shape = (WIDE, WIDE)
    keep = same_block(shape)
    for head in range(heads):
        rolled = pltpu.roll(jnp.where(keep, grad_ref[head], 0.0), 0, 1, stride=1, stride_axis=0)
        table_ref[head : head + 1, :] = jnp.sum(rolled[:half], axis=0, keepdims=True)
        table_ref[heads + head : heads + head + 1, :] = jnp.sum(rolled[half:], axis=0, keepdims=True)


def gather_bands(grads):
    heads = grads.shape[0]
    flipped = pl.pallas_call(
        unband_kernel,
        out_shape=jax.ShapeDtypeStruct((2 * heads, WIDE), F32),
        compiler_params=params(),
        cost_estimate=cost(3),
    )(grads)
    return flipped[:, ::-1].T


def gelu_pair(value):
    distance = jnp.abs(value) * 0.7071067811865476
    bell = jnp.exp(-0.5 * value * value)
    t = 1.0 / (1.0 + 0.3275911 * distance)
    poly = t * (0.254829592 + t * (-0.284496736 + t * (1.421413741 + t * (-1.453152027 + t * 1.061405429))))
    tail = 0.5 * poly * bell
    phi = jnp.where(value >= 0, 1.0 - tail, tail)
    return value * phi, phi + value * bell * 0.3989422804014327


def feed_kernel(me_ref, second_ref, grad_ref, up_ref, down_ref, hidden_ref, d_up_ref, send_ref, keep_ref, sums_ref):
    tile = pl.program_id(0)
    grad = grad_ref[...]
    value = contract(second_ref[...], up_ref[...], 1, 0)
    hidden, slope = gelu_pair(value)
    hidden = hidden.astype(BF)
    hidden_ref[...] = hidden
    back = contract(grad, down_ref[...], 1, 1)
    d_up_ref[...] = (slope * back).astype(BF)
    sums_ref[...] = contract(hidden, grad, 0, 0)
    rows = send_ref.shape[1]
    per_tile = sums_ref.shape[0] // rows
    place_rows(me_ref[0], tile * per_tile, per_tile, rows, sums_ref, send_ref, keep_ref, 0)


def place_rows(me, first, number, rows, sums_ref, send_ref, keep_ref, offset):
    halves = send_ref.shape[0]
    quarters = halves // 2
    for local in range(number):
        relative = (first + local) ^ me
        slot = ((relative >> 1) & 1) * quarters + (relative >> 2)
        block = sums_ref[local * rows : local * rows + rows, :].astype(BF)

        @pl.when(relative & 1 == 1)
        def _():
            send_ref[slot, offset : offset + rows, :] = block

        @pl.when(relative & 1 == 0)
        def _():
            keep_ref[slot, offset : offset + rows, :] = block


def feed_forward(me, second, grad, w_up, w_down, parts):
    count, width = second.shape
    hidden_width = w_up.shape[1]
    rows = hidden_width // parts
    tiles = hidden_width // width
    whole = pl.BlockSpec((count, width), lambda i, me: (0, 0))
    tile = pl.BlockSpec((count, width), lambda i, me: (0, i))
    slots = pl.BlockSpec((parts // 2, rows, width), lambda i, me: (0, 0, 0))
    return pl.pallas_call(
        feed_kernel,
        grid_spec=pltpu.PrefetchScalarGridSpec(
            num_scalar_prefetch=1,
            grid=(tiles,),
            in_specs=[
                whole,
                whole,
                pl.BlockSpec((width, width), lambda i, me: (0, i)),
                pl.BlockSpec((width, width), lambda i, me: (i, 0)),
            ],
            out_specs=[tile, tile, slots, slots],
            scratch_shapes=[pltpu.VMEM((width, width), F32)],
        ),
        out_shape=[
            jax.ShapeDtypeStruct((count, hidden_width), BF),
            jax.ShapeDtypeStruct((count, hidden_width), BF),
            jax.ShapeDtypeStruct((parts // 2, rows, width), BF),
            jax.ShapeDtypeStruct((parts // 2, rows, width), BF),
        ],
        compiler_params=params(56),
        cost_estimate=cost(22),
    )(me, second, grad, w_up, w_down)


def outer_kernel(plan, rows, me_ref, *refs):
    tile = pl.program_id(0)
    lefts, rights = refs[: len(plan)], refs[len(plan) : 2 * len(plan)]
    send_ref, keep_ref, sums_ref = refs[2 * len(plan) :]
    number = 2 * send_ref.shape[0]
    first = 0
    for (tiles,), left_ref, right_ref in zip(plan, lefts, rights):
        for step in range(tiles):

            @pl.when(tile == first + step)
            def _(left_ref=left_ref, right_ref=right_ref, offset=(first + step) * rows):
                sums_ref[...] = contract(left_ref[...], right_ref[...], 0, 0)
                place_rows(me_ref[0], 0, number, rows, sums_ref, send_ref, keep_ref, offset)

        first += tiles


def outer_products(me, pairs, parts, us, extra=None):
    count, width = pairs[0][0].shape
    rows = width // parts
    plan, specs_left, specs_right = [], [], []
    first = 0
    for left, right in pairs:
        tiles = right.shape[1] // width
        plan.append((tiles,))
        specs_left.append(pl.BlockSpec((count, width), lambda i, me: (0, 0)))
        specs_right.append(
            pl.BlockSpec(
                (count, width),
                lambda i, me, first=first, tiles=tiles: (0, jnp.clip(i - first, 0, tiles - 1)),
            )
        )
        first += tiles
    slots = pl.BlockSpec((parts // 2, first * rows, width), lambda i, me: (0, 0, 0))
    shape = jax.ShapeDtypeStruct((parts // 2, first * rows, width), BF)
    return pl.pallas_call(
        functools.partial(outer_kernel, plan, rows),
        grid_spec=pltpu.PrefetchScalarGridSpec(
            num_scalar_prefetch=1,
            grid=(first,),
            in_specs=specs_left + specs_right,
            out_specs=[slots, slots],
            scratch_shapes=[pltpu.VMEM((width, width), F32)],
        ),
        out_shape=[shape, shape],
        compiler_params=params(56),
        cost_estimate=cost(us),
    )(me, *[left for left, _ in pairs], *[right for _, right in pairs])


def reduce_parts(send, keep):
    half = send.shape[0] // 2
    arrived = swapped(send, "page", 1).astype(F32)
    away = (arrived[half:] + keep[half:].astype(F32)).astype(BF)
    mine = arrived[:half] + keep[:half].astype(F32)
    mine = mine + swapped(away, "page", 2).astype(F32)
    total = mine[0]
    for step in range(1, half):
        total = total + swapped(mine[step].astype(BF), "page", 4 * step).astype(F32)
    return total


def norm_rows(inputs, gain_row):
    centre = inputs - jnp.mean(inputs, axis=-1, keepdims=True)
    spread = jnp.mean(centre * centre, axis=-1, keepdims=True)
    return centre * lax.rsqrt(spread + EPSILON) * gain_row


def matmul(left, right):
    return contract(left, right, 1, 0)


def matmul_back(left, weight):
    return contract(left, weight, 1, 1)


def onehots(left, top, buckets):
    index = jnp.arange(buckets)[:, None]
    return jnp.concatenate([left[None, :] == index, top[None, :] == index], 0).astype(BF)


def body(
    states,
    counts,
    box_x,
    box_y,
    ln1_gain,
    ln2_gain,
    box_table,
    w_qkv,
    w_out,
    w_cq,
    w_ckv,
    w_cout,
    w_up,
    w_down,
    cotangent,
):
    slot_count, width = states.shape[2], states.shape[3]
    heads = box_table.shape[2] // 2
    buckets = box_table.shape[1] // 2
    scale = (width // heads) ** (-0.5)
    pairs = heads // 2
    parts = lax.axis_size("page")
    side = lax.axis_index("stream")
    me = lax.axis_index("page").astype(jnp.int32).reshape(1)
    own_count = jnp.take(counts[:, 0], side)
    other_count = jnp.take(counts[:, 0], 1 - side)
    slots = jnp.arange(slot_count)
    grid_side = jnp.where(own_count > GRID_SMALL * GRID_SMALL, GRID_LARGE, GRID_SMALL)
    left = jnp.where(side == 0, box_x[0], slots % grid_side)
    top = jnp.where(side == 0, box_y[0], slots // grid_side)
    onehot = onehots(left, top, buckets)
    flipped = onehots(buckets - 1 - left, buckets - 1 - top, buckets)
    mask_own = jnp.where(slots < own_count, 0.0, MASKED).astype(F32)[None]
    mask_other = jnp.where(slots < other_count, 0.0, MASKED).astype(F32)[None]
    valid = (slots < own_count).astype(F32)[:, None]
    bands = make_bands(box_table[0])
    weights = [w[0] for w in (w_qkv, w_out, w_cq, w_ckv, w_cout, w_up, w_down)]
    w_qkv, w_out, w_cq, w_ckv, w_cout, w_up, w_down = weights

    inputs = states[0, 0].astype(F32)
    normed, norm_pull = jax.vjp(norm_rows, inputs, ln1_gain[0])
    normed = normed.astype(BF)
    cross_kv = matmul(normed, w_ckv).astype(BF)
    partner = swapped(cross_kv, "stream", 1)
    joined = matmul(normed, w_qkv).astype(BF)
    attended, self_lse = attend_forward(joined, joined, pairs, mask_own, (bands, onehot), scale, 18)
    middle = inputs + matmul(attended, w_out)
    low_middle = middle.astype(BF)
    cross_query = matmul(low_middle, w_cq).astype(BF)
    crossed, cross_lse = attend_forward(cross_query, partner, 0, mask_other, None, scale, 16)
    after_cross = middle + matmul(crossed, w_cout)
    second, second_pull = jax.vjp(norm_rows, after_cross, ln2_gain[0])
    second = second.astype(BF)
    out_grad = cotangent[0, 0].astype(F32) * valid
    low_grad = out_grad.astype(BF)
    hidden, d_up, *down_parts = feed_forward(me, second, low_grad, w_up, w_down, parts)
    down_sum = reduce_parts(*down_parts)
    up_sum = reduce_parts(*outer_products(me, [(second, d_up)], parts, 6))
    d_after, ln2_grad = second_pull(matmul_back(d_up, w_up))
    d_after = d_after + out_grad
    low_after = d_after.astype(BF)
    d_crossed = matmul_back(low_after, w_cout).astype(BF)
    d_cross_query, d_partner = attend_backward(
        cross_query, partner, 0, d_crossed, crossed, cross_lse, mask_other, None, scale, 26
    )
    returned = swapped(d_partner, "stream", 1)
    d_middle = d_after + matmul_back(d_cross_query, w_cq)
    low_d_middle = d_middle.astype(BF)
    d_attended = matmul_back(low_d_middle, w_out).astype(BF)
    mid_sum = reduce_parts(
        *outer_products(
            me, [(crossed, low_after), (low_middle, d_cross_query), (attended, low_d_middle)], parts, 6
        )
    )
    d_query, d_pair, d_bands = attend_backward(
        joined, joined, pairs, d_attended, attended, self_lse, mask_own, (bands, onehot, flipped), scale, 29
    )
    table_grad = gather_bands(d_bands)
    d_normed = (
        matmul_back(d_query, w_qkv[:, :width])
        + matmul_back(d_pair[0], w_qkv[:, width : 2 * width])
        + matmul_back(d_pair[1], w_qkv[:, 2 * width :])
        + matmul_back(returned[0], w_ckv[:, :width])
        + matmul_back(returned[1], w_ckv[:, width:])
    )
    d_inputs, ln1_grad = norm_pull(d_normed)
    states_grad = d_inputs + d_middle
    last_send, last_keep = outer_products(
        me,
        [
            (normed, d_query),
            (normed, d_pair[0]),
            (normed, d_pair[1]),
            (normed, returned[0]),
            (normed, returned[1]),
        ],
        parts,
        10,
    )
    last_sum = reduce_parts(last_send, last_keep)
    small = jnp.concatenate(
        [ln1_grad.reshape(parts, -1), ln2_grad.reshape(parts, -1), table_grad.reshape(parts, -1)], 1
    )
    small_sum = reduce_small(me[0], small)
    result = ((after_cross + matmul(hidden, w_down)) * valid).astype(BF)

    rows = width // parts
    table_rows = 2 * buckets // parts

    def wide(block):
        return block.reshape(-1, rows, width).transpose(1, 0, 2).reshape(1, rows, -1)

    return (
        result[None, None],
        states_grad[None, None],
        small_sum[None, :rows],
        small_sum[None, rows : 2 * rows],
        small_sum[2 * rows :].reshape(1, table_rows, 2 * heads),
        wide(last_sum[: 3 * rows]),
        wide(mid_sum[2 * rows :]),
        wide(mid_sum[rows : 2 * rows]),
        wide(last_sum[3 * rows :]),
        wide(mid_sum[:rows]),
        wide(up_sum),
        down_sum[None],
    )


def reduce_small(me, small):
    parts = small.shape[0]
    order = jnp.arange(parts) ^ me
    small = jnp.take(small, order, axis=0).reshape(parts // 4, 2, 2, -1)
    small = small[:, :, 0] + swapped(small[:, :, 1], "page", 1)
    small = small[:, 0] + swapped(small[:, 1], "page", 2)
    total = small[0]
    for step in range(1, parts // 4):
        total = total + swapped(small[step], "page", 4 * step)
    return total


def solution(mesh):
    placed = (
        P("stream", "page", None, None),
        P(None, "page"),
        P("page", None),
        P("page", None),
        P("stream", None),
        P("stream", None),
        P("stream", None, None),
        P("stream", None, None),
        P("stream", None, None),
        P("stream", None, None),
        P("stream", None, None),
        P("stream", None, None),
        P("stream", None, None),
        P("stream", None, None),
        P("stream", "page", None, None),
    )
    return jax.shard_map(
        body,
        mesh=mesh,
        in_specs=placed,
        out_specs=(
            P("stream", "page", None, None),
            P("stream", "page", None, None),
            P("stream", "page"),
            P("stream", "page"),
            P("stream", "page", None),
            P("stream", "page", None),
            P("stream", "page", None),
            P("stream", "page", None),
            P("stream", "page", None),
            P("stream", "page", None),
            P("stream", "page", None),
            P("stream", "page", None),
        ),
        check_vma=False,
    )
```

time: 825 us -> 394 us (0.48)
  matrix products: 280 us -> 33.4 us
  waiting for transfers between devices: 302 us -> 149 us
  Pallas kernels: 0 us -> 114 us
  blocking collectives: 63.7 us -> 0 us
  other arithmetic: 95 us -> 33.3 us
  local copies, waits for them, and re-layouts: 59.7 us -> 22 us
  starting transfers between devices: 3.58 us -> 33.9 us
  between operations: 17.8 us -> 3.21 us
    reduce_scatter x7 -> x0, waiting for transfers between devices: 258 us -> none  [the longest x1 116 us: body(): lax.psum_scatter(w_up_grad, 'page', scatter_dimension=0, tiled=True)]
    dot_general x37 -> x15, matrix products: 280 us -> 33.4 us  [contract(): lax.dot_general(left, right, (((left_dim,), (right_dim,)), ((), ())), pre...]
    pallas_call x0 -> x10, Pallas kernels: none -> 114 us  [the longest x2 37.3 us: attend_backward(): pl.pallas_call(functools.partial(backward_kernel, bias is not None, scale...]
    ppermute x2 -> x27, waiting for transfers between devices: 44.3 us -> 149 us  [swapped(): lax.ppermute(shard, axis, [(i, i ^ mask) for i in range(lax.axis_size(axi...]
    unnamed x1 -> x0, blocking collectives: 63.7 us -> none
    ppermute x2 -> x27, starting transfers between devices: 3.07 us -> 33.9 us  [swapped(): lax.ppermute(shard, axis, [(i, i ^ mask) for i in range(lax.axis_size(axi...]
    scatter-add x1 -> x0, other arithmetic: 23.4 us -> none  [band_blocks(): picked = jnp.take(bias_table, offsets, axis=0)]
    reduce_sum x2 -> x0, other arithmetic: 19.7 us -> none  [attend_forward(): row_total = jnp.sum(expsum, axis=-1, keepdims=True)]
  transfers between devices with their start and end apart: 9 -> 27, of which waited for: 4 -> 10; matrix products, arithmetic and copies ran while one was open for 40% -> 13% of each run, Pallas kernels for 0% -> 9%
where the time goes in v1:
time: 394 us; the launch traced here: 389 us
  waiting for transfers between devices  149 us (38%)
  Pallas kernels  114 us (29%)
  starting transfers between devices  33.9 us (9%)
  matrix products  33.4 us (8%)
  other arithmetic  33.3 us (8%)
  local copies, waits for them, and re-layouts  22 us (6%)
    ppermute x27, waiting for transfers between devices, swapped(): lax.ppermute(shard, axis, [(i, i ^ mask) for i in range(lax.axis_size(axi...  149 us
    pallas_call x2, Pallas kernels, attend_backward(): pl.pallas_call(functools.partial(backward_kernel, bias is not None, scale...  37.3 us
    ppermute x27, starting transfers between devices, swapped(): lax.ppermute(shard, axis, [(i, i ^ mask) for i in range(lax.axis_size(axi...  33.9 us
    dot_general x15, matrix products, contract(): lax.dot_general(left, right, (((left_dim,), (right_dim,)), ((), ())), pre...  33.4 us
    pallas_call x3, Pallas kernels, outer_products(): pl.pallas_call(functools.partial(outer_kernel, plan, rows), grid_spec=plt...  32.3 us
    pallas_call x2, Pallas kernels, attend_forward(): pl.pallas_call(functools.partial(forward_kernel, bias is not None, scale)...  23.6 us
    pallas_call x1, Pallas kernels, feed_forward(): pl.pallas_call(feed_kernel, grid_spec=pltpu.PrefetchScalarGridSpec(num_sc...  20.5 us
    unnamed x112, local copies, waits for them, and re-layouts  9.2 us
  transfers between devices with their start and end apart: 27, of which 10 were waited for; matrix products, arithmetic and copies ran while one was open for 13% of the time, Pallas kernels for 9%

profile of v1, /device:TPU:0, one launch (start us, length us, event | category | flops | bytes accessed | tf_op | source)
XLA Modules:
  0.0 389.4 jit_solution(13884596367107619927)
XLA Ops:
  0.7 1.6 convert_reduce_fusion
  2.3 1.6 fusion.16
  4.6 4.7 %convolution_convert_fusion.1 = bf16[640,1536]{1,0:T(8,128)(2,1)} fusion(bf16[1,768,1536]{2,1,0:T(8,128)(2,1)} %param.25, bf16[1,1,640,768]{3,2,1,0:T(8,128)(2,1)S(1)} %copy-done.13, f32[768]{0:T(1024)S(1)} %reduce.1, f32[640]{0:T(1024)S(1)} %fusion.62, f32[640]{0:T(1024)S(1)} %broadcast_multiply_fusion.1), kind=kOutput, calls=%fused_computation.2 | convolution fusion | flops 1513390080 | bytes 5316608 | tf_op jit(solution)/shard_map/dot_general | solution.py:20
  9.3 2.9 collective-permute-start
  16.3 1.8 copy-done.52
  18.0 2.6 convolution_convert_fusion.refs_0_.refs_1_.refs_2_
  22.1 11.9 %shard_map.239 = (bf16[640,768]{1,0:T(8,128)(2,1)S(1)}, f32[6,2,640]{2,1,0:T(2,128)S(1)}) custom-call(bf16[640,2304]{1,0:T(8,128)(2,1)S(1)} %convolution_convert_fusion.refs_0_.refs_1_.refs_2_, bf16[640,2304]{1,0:T(8,128)(2,1)S(1)} %convolution_convert_fusion.refs_0_.refs_1_.refs_2_, bf16[640,2304]{1,0:T(8,128)(2,1)S(1)} %convolution_convert_fusion.refs_0_.refs_1_.refs_2_, ...), custom_call_target="tpu_custom_call" | custom-call | flops 19800000512 | bytes 1048576 | tf_op jit(solution)/shard_map/pallas_call | solution.py:155
  36.1 19.3 %collective-permute-done.refs_1_.refs_2_ = bf16[640,1536]{1,0:T(8,128)(2,1)} collective-permute-done((bf16[640,1536]{1,0:T(8,128)(2,1)}, bf16[640,1536]{1,0:T(8,128)(2,1)}, u32[]{:S(2)}, u32[]{:S(2)}) %collective-permute-start) | collective-permute-done | bytes 1966112 | tf_op jit(solution)/shard_map/ppermute | solution.py:34
  55.4 11.7 %shard_map.240 = (bf16[640,768]{1,0:T(8,128)(2,1)S(1)}, f32[6,2,640]{2,1,0:T(2,128)S(1)}) custom-call(bf16[640,768]{1,0:T(8,128)(2,1)S(1)} %convolution_convert_fusion.4.refs_0_, bf16[640,1536]{1,0:T(8,128)(2,1)} %collective-permute-done.refs_1_.refs_2_, bf16[640,1536]{1,0:T(8,128)(2,1)} %collective-permute-done.refs_1_.refs_2_, ...), custom_call_target="tpu_custom_call" | custom-call | flops 17600000000 | bytes 1048576 | tf_op jit(solution)/shard_map/pallas_call | solution.py:155
  69.8 20.5 %shard_map.241 = (bf16[640,3072]{1,0:T(8,128)(2,1)}, bf16[640,3072]{1,0:T(8,128)(2,1)}, bf16[8,192,768]{2,1,0:T(8,128)(2,1)}, bf16[8,192,768]{2,1,0:T(8,128)(2,1)}) custom-call(s32[1]{0:T(128)} %bitcast.15.me_ref, bf16[640,768]{1,0:T(8,128)(2,1)} %multiply_convert_fusion.1.second_ref.refs_0_, bf16[640,768]{1,0:T(8,128)(2,1)} %fusion.22.grad_ref, ...), custom_call_target="tpu_custom_call" | custom-call | flops 24199999488 | bytes 1048576 | tf_op jit(solution)/shard_map/pallas_call | solution.py:307
  90.3 7.1 %multiply_reduce_fusion = (f32[768]{0:T(1024)S(1)}, f32[640]{0:T(1024)S(1)}, f32[640,768]{1,0:T(8,128)S(1)}) fusion(f32[640,768]{1,0:T(8,128)S(1)} %get-tuple-element.126, f32[640]{0:T(1024)S(1)} %fusion.63, f32[640]{0:T(1024)S(1)} %broadcast_multiply_fusion, f32[768]{0:T(1024)S(1)} %reduce.4, bf16[640,3072]{1,0:T(8,128)(2,1)} %get-tuple-element.34.refs_1_, ...), kind=kOutput, calls=%fused_computation.38 | convolution fusion | flops 3023337984 | bytes 12596736 | tf_op jit(solution)/shard_map/dot_general | solution.py:20
  100.4 16.2 %shard_map.242 = (bf16[640,768]{1,0:T(8,128)(2,1)S(1)}, bf16[2,640,768]{2,1,0:T(8,128)(2,1)S(1)}) custom-call(bf16[640,768]{1,0:T(8,128)(2,1)S(1)} %convolution_convert_fusion.4.refs_0_, bf16[640,1536]{1,0:T(8,128)(2,1)} %collective-permute-done.refs_1_.refs_2_, bf16[640,1536]{1,0:T(8,128)(2,1)} %collective-permute-done.refs_1_.refs_2_, ...), custom_call_target="tpu_custom_call" | custom-call | flops 28600000512 | bytes 1048576 | tf_op jit(solution)/shard_map/pallas_call | solution.py:196
  116.6 2.6 fusion.86
  119.2 8.8 %shard_map.246 = (bf16[8,144,768]{2,1,0:T(8,128)(2,1)}, bf16[8,144,768]{2,1,0:T(8,128)(2,1)}) custom-call(s32[1]{0:T(128)} %bitcast.15.me_ref, bf16[640,768]{1,0:T(8,128)(2,1)} %copy-done.4, bf16[640,768]{1,0:T(8,128)(2,1)} %copy-done.33, bf16[640,768]{1,0:T(8,128)(2,1)} %copy-done.2, bf16[640,768]{1,0:T(8,128)(2,1)} %copy-done.35, ...), custom_call_target="tpu_custom_call" | custom-call | flops 6600000000 | bytes 1048576 | tf_op jit(solution)/shard_map/pallas_call | solution.py:367
  130.3 21.1 %shard_map.243 = (bf16[640,768]{1,0:T(8,128)(2,1)S(1)}, bf16[2,640,768]{2,1,0:T(8,128)(2,1)}, f32[12,128,128]{2,1,0:T(8,128)S(1)}) custom-call(bf16[640,2304]{1,0:T(8,128)(2,1)} %copy-done.10, bf16[640,2304]{1,0:T(8,128)(2,1)} %copy-done.10, bf16[640,2304]{1,0:T(8,128)(2,1)} %copy-done.10, bf16[640,768]{1,0:T(8,128)(2,1)S(1)} %convolution_convert_fusion.2.refs_3_, ...), custom_call_target="tpu_custom_call" | custom-call | flops 31900000256 | bytes 1048576 | tf_op jit(solution)/shard_map/pallas_call | solution.py:196
  153.3 1.8 collective-permute-start.1
  155.0 9.3 %shard_map.247 = (bf16[8,192,768]{2,1,0:T(8,128)(2,1)}, bf16[8,192,768]{2,1,0:T(8,128)(2,1)}) custom-call(s32[1]{0:T(128)} %bitcast.15.me_ref, bf16[640,768]{1,0:T(8,128)(2,1)} %multiply_convert_fusion.1.second_ref.refs_0_, bf16[640,3072]{1,0:T(8,128)(2,1)} %get-tuple-element.34.refs_1_), custom_call_target="tpu_custom_call" | custom-call | flops 6600000000 | bytes 1048576 | tf_op jit(solution)/shard_map/pallas_call | solution.py:367
  170.6 1.9 convert_element_type.243
  173.7 1.5 collective-permute-start.13
  175.2 22.0 %collective-permute-done.1 = bf16[2,640,768]{2,1,0:T(8,128)(2,1)S(1)} collective-permute-done((bf16[2,640,768]{2,1,0:T(8,128)(2,1)S(1)}, bf16[2,640,768]{2,1,0:T(8,128)(2,1)S(1)}, u32[]{:S(2)}, u32[]{:S(2)}) %collective-permute-start.1) | collective-permute-done | bytes 1966112 | tf_op jit(solution)/shard_map/ppermute | solution.py:34
  202.6 4.1 %fusion.15 = (bf16[640,768]{1,0:T(8,128)(2,1)}, f32[1,1,640,768]{3,2,1,0:T(8,128)}) fusion(bf16[1,1,640,768]{3,2,1,0:T(8,128)(2,1)S(1)} %copy-done.14, f32[640]{0:T(1024)S(1)} %copy-done.43, f32[768]{0:T(1024)S(1)} %copy-done.41, f32[640]{0:T(1024)S(1)} %copy-done.39, f32[640,768]{1,0:T(8,128)} %get-tuple-element.129, f32[640]{0:T(1024)S(1)} %negate_multiply_fusion, ...), kind=kLoop, calls=%fused_computation.29 | loop fusion | flops 5898240 | bytes 7877632 | tf_op jit(solution)/shard_map/convert_element_type | solution.py:455
  206.7 1.8 collective-permute-start.3
  208.5 1.4 slice_bitcast_fusion
  210.5 1.9 collective-permute-start.4
  212.3 2.5 collective-permute-start.6
  214.8 14.1 %shard_map.245 = (bf16[8,240,768]{2,1,0:T(8,128)(2,1)}, bf16[8,240,768]{2,1,0:T(8,128)(2,1)}) custom-call(s32[1]{0:T(128)} %bitcast.15.me_ref, bf16[640,768]{1,0:T(8,128)(2,1)} %get-tuple-element.107.refs_0_.refs_1_.refs_2_.refs_3_.refs_4_, bf16[640,768]{1,0:T(8,128)(2,1)} %get-tuple-element.107.refs_0_.refs_1_.refs_2_.refs_3_.refs_4_, ...), custom_call_target="tpu_custom_call" | custom-call | flops 11000000512 | bytes 1048576 | tf_op jit(solution)/shard_map/pallas_call | solution.py:367
  229.2 6.5 %fusion.25 = bf16[1,1,640,768]{3,2,1,0:T(8,128)(2,1)} fusion(f32[640,768]{1,0:T(8,128)S(1)} %copy-done.16, bf16[640,3072]{1,0:T(8,128)(2,1)S(1)} %copy-done.54, f32[640]{0:T(1024)S(1)} %fusion.61, bf16[1,3072,768]{2,1,0:T(8,128)(2,1)} %param.28), kind=kOutput, calls=%fused_computation.54 | convolution fusion | flops 3021373440 | bytes 11602432 | tf_op jit(solution)/shard_map/dot_general | solution.py:20
  237.0 2.2 convert_element_type.254
  239.7 1.6 collective-permute-start.18
  241.2 2.1 convert_element_type.265
  243.4 1.7 fusion.77
  245.1 1.9 collective-permute-start.14
  247.0 2.5 collective-permute-start.16
  249.7 3.1 collective-permute-done.14
  253.9 6.7 %collective-permute-done.16 = bf16[144,768]{1,0:T(8,128)(2,1)S(1)} collective-permute-done((bf16[144,768]{1,0:T(8,128)(2,1)S(1)}, bf16[144,768]{1,0:T(8,128)(2,1)S(1)}, u32[]{:S(2)}, u32[]{:S(2)}) %collective-permute-start.16) | collective-permute-done | bytes 221216 | tf_op jit(solution)/shard_map/ppermute | solution.py:34
  260.5 7.8 %collective-permute-done.15 = bf16[144,768]{1,0:T(8,128)(2,1)S(1)} collective-permute-done((bf16[144,768]{1,0:T(8,128)(2,1)S(1)}, bf16[144,768]{1,0:T(8,128)(2,1)S(1)}, u32[]{:S(2)}, u32[]{:S(2)}) %collective-permute-start.15) | collective-permute-done | bytes 221216 | tf_op jit(solution)/shard_map/ppermute | solution.py:34
  268.4 2.5 convert_element_type.232
  273.9 2.7 collective-permute-start.21
  277.4 16.4 %collective-permute-done.23 = bf16[4,192,768]{2,1,0:T(8,128)(2,1)S(1)} collective-permute-done((bf16[4,192,768]{2,1,0:T(8,128)(2,1)S(1)}, bf16[4,192,768]{2,1,0:T(8,128)(2,1)S(1)}, u32[]{:S(2)}, u32[]{:S(2)}) %collective-permute-start.23) | collective-permute-done | bytes 1179680 | tf_op jit(solution)/shard_map/ppermute | solution.py:34
  295.0 1.8 collective-permute-start.24
  296.9 27.9 %collective-permute-done.8 = bf16[4,240,768]{2,1,0:T(8,128)(2,1)S(1)} collective-permute-done((bf16[4,240,768]{2,1,0:T(8,128)(2,1)S(1)}, bf16[4,240,768]{2,1,0:T(8,128)(2,1)S(1)}, u32[]{:S(2)}, u32[]{:S(2)}) %collective-permute-start.8) | collective-permute-done | bytes 1474592 | tf_op jit(solution)/shard_map/ppermute | solution.py:34
  324.8 2.8 collective-permute-start.26
  327.5 2.0 fusion.79
  332.2 2.8 collective-permute-start.11
  337.2 33.1 %collective-permute-done.25 = bf16[192,768]{1,0:T(8,128)(2,1)} collective-permute-done((bf16[192,768]{1,0:T(8,128)(2,1)}, bf16[192,768]{1,0:T(8,128)(2,1)}, u32[]{:S(2)}, u32[]{:S(2)}) %collective-permute-start.25) | collective-permute-done | bytes 294944 | tf_op jit(solution)/shard_map/ppermute | solution.py:34
  370.3 2.1 fusion.52
  372.3 12.6 %collective-permute-done.10 = bf16[240,768]{1,0:T(8,128)(2,1)} collective-permute-done((bf16[240,768]{1,0:T(8,128)(2,1)}, bf16[240,768]{1,0:T(8,128)(2,1)}, u32[]{:S(2)}, u32[]{:S(2)}) %collective-permute-start.10) | collective-permute-done | bytes 368672 | tf_op jit(solution)/shard_map/ppermute | solution.py:34
  385.0 1.6 fusion.48
  (225 shorter events, 45.2 us)
Async XLA Ops:
  0.6 34.4 %copy-start = (bf16[1,768,768]{2,1,0:T(8,128)(2,1)S(1)}, bf16[1,768,768]{2,1,0:T(8,128)(2,1)}, u32[]{:S(2)}) copy-start(bf16[1,768,768]{2,1,0:T(8,128)(2,1)} %param.24) | copy-start | bytes 3538948
  2.2 14.0 %copy-start.38 = (f32[640]{0:T(1024)}, f32[640]{0:T(1024)S(1)}, u32[]{:S(2)}) copy-start(f32[640]{0:T(1024)S(1)} %broadcast_multiply_fusion.1) | copy-start | bytes 7684
  4.5 11.8 %copy-start.42 = (f32[640]{0:T(1024)}, f32[640]{0:T(1024)S(1)}, u32[]{:S(2)}) copy-start(f32[640]{0:T(1024)S(1)} %fusion.62) | copy-start | bytes 7684
  4.5 11.7 %copy-start.40 = (f32[768]{0:T(1024)}, f32[768]{0:T(1024)S(1)}, u32[]{:S(2)}) copy-start(f32[768]{0:T(1024)S(1)} %reduce.1) | copy-start | bytes 9220
  4.5 10.9 %copy-start.48 = (f32[1,768]{1,0:T(1,128)S(1)}, f32[1,768]{1,0:T(1,128)}, u32[]{:S(2)}) copy-start(f32[1,768]{1,0:T(1,128)} %param.20) | copy-start | bytes 9220
  4.6 10.9 %copy-start.49 = (s32[1,640]{1,0:T(1,128)S(1)}, s32[1,640]{1,0:T(1,128)}, u32[]{:S(2)}) copy-start(s32[1,640]{1,0:T(1,128)} %param.18) | copy-start | bytes 7684
  4.6 10.9 %copy-start.50 = (s32[1,640]{1,0:T(1,128)S(1)}, s32[1,640]{1,0:T(1,128)}, u32[]{:S(2)}) copy-start(s32[1,640]{1,0:T(1,128)} %param.17) | copy-start | bytes 7684
  4.6 11.4 %copy-start.8 = (f32[1,128,24]{1,2,0:T(8,128)S(1)}, f32[1,128,24]{1,2,0:T(8,128)}, u32[]{:S(2)}) copy-start(f32[1,128,24]{1,2,0:T(8,128)} %param.21) | copy-start | bytes 36868
  9.3 46.1 %collective-permute-start = (bf16[640,1536]{1,0:T(8,128)(2,1)}, bf16[640,1536]{1,0:T(8,128)(2,1)}, u32[]{:S(2)}, u32[]{:S(2)}) collective-permute-start(bf16[640,1536]{1,0:T(8,128)(2,1)} %convolution_convert_fusion.1), channel_id=1, source_target_pairs={{0,16},{16,0},{1,17},{17,1},{2,18},{18,2},{3,19},{19,3},{4,20},{20... | collective-permute-start | bytes 5898248 | tf_op jit(solution)/shard_map/ppermute | solution.py:34
  20.6 13.4 %copy-start.10 = (bf16[640,2304]{1,0:T(8,128)(2,1)}, bf16[640,2304]{1,0:T(8,128)(2,1)S(1)}, u32[]{:S(2)}) copy-start(bf16[640,2304]{1,0:T(8,128)(2,1)S(1)} %convolution_convert_fusion.refs_0_.refs_1_.refs_2_) | copy-start | bytes 8847364
  22.1 12.0 %copy-start.31 = (bf16[1,768,768]{2,1,0:T(8,128)(2,1)S(1)}, bf16[1,768,768]{2,1,0:T(8,128)(2,1)}, u32[]{:S(2)}) copy-start(bf16[1,768,768]{2,1,0:T(8,128)(2,1)} %param.23) | copy-start | bytes 3538948
  36.1 31.1 %copy-start.29 = (bf16[1,768,768]{2,1,0:T(8,128)(2,1)S(1)}, bf16[1,768,768]{2,1,0:T(8,128)(2,1)}, u32[]{:S(2)}) copy-start(bf16[1,768,768]{2,1,0:T(8,128)(2,1)} %param.26) | copy-start | bytes 3538948
  67.1 33.2 %copy-start.4 = (bf16[640,768]{1,0:T(8,128)(2,1)}, bf16[640,768]{1,0:T(8,128)(2,1)S(1)}, u32[]{:S(2)}) copy-start(bf16[640,768]{1,0:T(8,128)(2,1)S(1)} %get-tuple-element.32.refs_4_.refs_0_) | copy-start | bytes 2949124
  68.1 29.2 %copy-start.15 = (f32[640,768]{1,0:T(8,128)}, f32[640,768]{1,0:T(8,128)S(1)}, u32[]{:S(2)}) copy-start(f32[640,768]{1,0:T(8,128)S(1)} %get-tuple-element.126) | copy-start | bytes 5898244
  100.4 16.2 %copy-start.20 = (bf16[1,1,640,768]{3,2,1,0:T(8,128)(2,1)S(1)}, bf16[1,1,640,768]{3,2,1,0:T(8,128)(2,1)}, u32[]{:S(2)}) copy-start(bf16[1,1,640,768]{3,2,1,0:T(8,128)(2,1)} %param.29) | copy-start | bytes 2949124
  119.2 8.8 %copy-start.34 = (bf16[640,768]{1,0:T(8,128)(2,1)S(1)}, bf16[640,768]{1,0:T(8,128)(2,1)}, u32[]{:S(2)}) copy-start(bf16[640,768]{1,0:T(8,128)(2,1)} %get-tuple-element.128.refs_5_) | copy-start | bytes 2949124
  151.4 18.2 %copy-start.9 = (bf16[640,768]{1,0:T(8,128)(2,1)}, bf16[640,768]{1,0:T(8,128)(2,1)S(1)}, u32[]{:S(2)}) copy-start(bf16[640,768]{1,0:T(8,128)(2,1)S(1)} %get-tuple-element.38.refs_5_) | copy-start | bytes 2949124
  151.9 18.7 %collective-permute-start.12 = (bf16[8,144,768]{2,1,0:T(8,128)(2,1)}, bf16[8,144,768]{2,1,0:T(8,128)(2,1)}, u32[]{:S(2)}, u32[]{:S(2)}) collective-permute-start(bf16[8,144,768]{2,1,0:T(8,128)(2,1)} %get-tuple-element.44), channel_id=1, source_target_pairs={{0,1},{1,0},{2,3},{3,2},{4,5},{5,4},{6,7},{7,6},{8,9},{9,8},{10,11... | collective-permute-start | bytes 5308424 | tf_op jit(solution)/shard_map/ppermute | solution.py:34
  153.3 11.7 %copy-start.26 = (bf16[2,640,768]{2,1,0:T(8,128)(2,1)S(1)}, bf16[2,640,768]{2,1,0:T(8,128)(2,1)}, u32[]{:S(2)}) copy-start(bf16[2,640,768]{2,1,0:T(8,128)(2,1)} %get-tuple-element.39) | copy-start | bytes 5898244
  153.3 44.0 %collective-permute-start.1 = (bf16[2,640,768]{2,1,0:T(8,128)(2,1)S(1)}, bf16[2,640,768]{2,1,0:T(8,128)(2,1)S(1)}, u32[]{:S(2)}, u32[]{:S(2)}) collective-permute-start(bf16[2,640,768]{2,1,0:T(8,128)(2,1)S(1)} %copy-done.7), channel_id=1, source_target_pairs={{0,16},{16,0},{1,17},{17,1},{2,18},{18,2},{3,19},{19,3},{4,20},{20... | collective-permute-start | bytes 5898248 | tf_op jit(solution)/shard_map/ppermute | solution.py:34
  164.4 72.6 %collective-permute-start.17 = (bf16[8,192,768]{2,1,0:T(8,128)(2,1)}, bf16[8,192,768]{2,1,0:T(8,128)(2,1)}, u32[]{:S(2)}, u32[]{:S(2)}) collective-permute-start(bf16[8,192,768]{2,1,0:T(8,128)(2,1)} %get-tuple-element.46), channel_id=1, source_target_pairs={{0,1},{1,0},{2,3},{3,2},{4,5},{5,4},{6,7},{7,6},{8,9},{9,8},{10,11... | collective-permute-start | bytes 7077896 | tf_op jit(solution)/shard_map/ppermute | solution.py:34
  164.5 76.8 %collective-permute-start.22 = (bf16[8,192,768]{2,1,0:T(8,128)(2,1)}, bf16[8,192,768]{2,1,0:T(8,128)(2,1)}, u32[]{:S(2)}, u32[]{:S(2)}) collective-permute-start(bf16[8,192,768]{2,1,0:T(8,128)(2,1)} %get-tuple-element.48), channel_id=1, source_target_pairs={{0,1},{1,0},{2,3},{3,2},{4,5},{5,4},{6,7},{7,6},{8,9},{9,8},{10,11... | collective-permute-start | bytes 7077896 | tf_op jit(solution)/shard_map/ppermute | solution.py:34
  172.5 24.7 %copy-start.17 = (f32[8,144,768]{2,1,0:T(8,128)}, f32[8,144,768]{2,1,0:T(8,128)S(1)}, u32[]{:S(2)}) copy-start(f32[8,144,768]{2,1,0:T(8,128)S(1)} %convert_element_type.243) | copy-start | bytes 10616836
  172.5 24.7 %copy-start.36 = (bf16[1,768,1536]{2,1,0:T(8,128)(2,1)S(1)}, bf16[1,768,1536]{2,1,0:T(8,128)(2,1)}, u32[]{:S(2)}) copy-start(bf16[1,768,1536]{2,1,0:T(8,128)(2,1)} %param.25) | copy-start | bytes 7077892
  173.7 69.6 %collective-permute-start.13 = (bf16[4,144,768]{2,1,0:T(8,128)(2,1)}, bf16[4,144,768]{2,1,0:T(8,128)(2,1)}, u32[]{:S(2)}, u32[]{:S(2)}) collective-permute-start(bf16[4,144,768]{2,1,0:T(8,128)(2,1)} %fusion.23), channel_id=1, source_target_pairs={{0,2},{1,3},{2,0},{3,1},{4,6},{5,7},{6,4},{7,5},{8,10},{9,11},{10,... | collective-permute-start | bytes 2654216 | tf_op jit(solution)/shard_map/ppermute | solution.py:34
  202.5 4.2 %collective-permute-start.2 = (f32[4,2,288]{2,1,0:T(2,128)S(1)}, f32[4,2,288]{2,1,0:T(2,128)S(1)}, u32[]{:S(2)}, u32[]{:S(2)}) collective-permute-start(f32[4,2,288]{2,1,0:T(2,128)S(1)} %bitcast.218), channel_id=1, source_target_pairs={{0,1},{1,0},{2,3},{3,2},{4,5},{5,4},{6,7},{7,6},{8,9},{9,8},{10,11... | collective-permute-start | bytes 27656 | tf_op jit(solution)/shard_map/ppermute | solution.py:34
  206.7 3.7 collective-permute-start.3
  210.5 18.4 %collective-permute-start.4 = (f32[288]{0:T(512)S(1)}, f32[288]{0:T(512)S(1)}, u32[]{:S(2)}, u32[]{:S(2)}) collective-permute-start(f32[288]{0:T(512)S(1)} %get-tuple-element.76), channel_id=1, source_target_pairs={{0,4},{1,5},{2,6},{3,7},{4,0},{5,1},{6,2},{7,3},{8,12},{9,13},{10,... | collective-permute-start | bytes 3464 | tf_op jit(solution)/shard_map/ppermute | solution.py:34
  212.3 16.7 %collective-permute-start.6 = (f32[288]{0:T(512)S(1)}, f32[288]{0:T(512)S(1)}, u32[]{:S(2)}, u32[]{:S(2)}) collective-permute-start(f32[288]{0:T(512)S(1)} %get-tuple-element.77), channel_id=1, source_target_pairs={{0,12},{1,13},{2,14},{3,15},{4,8},{5,9},{6,10},{7,11},{8,4},{9,5},... | collective-permute-start | bytes 3464 | tf_op jit(solution)/shard_map/ppermute | solution.py:34
  214.8 14.4 %copy-start.16 = (f32[640,768]{1,0:T(8,128)S(1)}, f32[640,768]{1,0:T(8,128)}, u32[]{:S(2)}) copy-start(f32[640,768]{1,0:T(8,128)} %copy-done.15) | copy-start | bytes 5898244
  214.8 14.4 %copy-start.54 = (bf16[640,3072]{1,0:T(8,128)(2,1)S(1)}, bf16[640,3072]{1,0:T(8,128)(2,1)}, u32[]{:S(2)}) copy-start(bf16[640,3072]{1,0:T(8,128)(2,1)} %get-tuple-element.33) | copy-start | bytes 11796484
  228.9 39.5 %collective-permute-start.7 = (bf16[8,240,768]{2,1,0:T(8,128)(2,1)}, bf16[8,240,768]{2,1,0:T(8,128)(2,1)}, u32[]{:S(2)}, u32[]{:S(2)}) collective-permute-start(bf16[8,240,768]{2,1,0:T(8,128)(2,1)} %get-tuple-element.42), channel_id=1, source_target_pairs={{0,1},{1,0},{2,3},{3,2},{4,5},{5,4},{6,7},{7,6},{8,9},{9,8},{10,11... | collective-permute-start | bytes 8847368 | tf_op jit(solution)/shard_map/ppermute | solution.py:34
  229.0 6.7 %collective-permute-start.5 = (f32[288]{0:T(512)S(1)}, f32[288]{0:T(512)S(1)}, u32[]{:S(2)}, u32[]{:S(2)}) collective-permute-start(f32[288]{0:T(512)S(1)} %get-tuple-element.78), channel_id=1, source_target_pairs={{0,8},{1,9},{2,10},{3,11},{4,12},{5,13},{6,14},{7,15},{8,0},{9,1},... | collective-permute-start | bytes 3464 | tf_op jit(solution)/shard_map/ppermute | solution.py:34
  239.7 33.7 %collective-permute-start.18 = (bf16[4,192,768]{2,1,0:T(8,128)(2,1)S(1)}, bf16[4,192,768]{2,1,0:T(8,128)(2,1)S(1)}, u32[]{:S(2)}, u32[]{:S(2)}) collective-permute-start(bf16[4,192,768]{2,1,0:T(8,128)(2,1)S(1)} %fusion.10), channel_id=1, source_target_pairs={{0,2},{1,3},{2,0},{3,1},{4,6},{5,7},{6,4},{7,5},{8,10},{9,11},{10,... | collective-permute-start | bytes 3538952 | tf_op jit(solution)/shard_map/ppermute | solution.py:34
  245.1 7.7 %collective-permute-start.14 = (bf16[144,768]{1,0:T(8,128)(2,1)S(1)}, bf16[144,768]{1,0:T(8,128)(2,1)S(1)}, u32[]{:S(2)}, u32[]{:S(2)}) collective-permute-start(bf16[144,768]{1,0:T(8,128)(2,1)S(1)} %get-tuple-element.109), channel_id=1, source_target_pairs={{0,4},{1,5},{2,6},{3,7},{4,0},{5,1},{6,2},{7,3},{8,12},{9,13},{10,... | collective-permute-start | bytes 663560 | tf_op jit(solution)/shard_map/ppermute | solution.py:34
  247.0 13.6 %collective-permute-start.16 = (bf16[144,768]{1,0:T(8,128)(2,1)S(1)}, bf16[144,768]{1,0:T(8,128)(2,1)S(1)}, u32[]{:S(2)}, u32[]{:S(2)}) collective-permute-start(bf16[144,768]{1,0:T(8,128)(2,1)S(1)} %get-tuple-element.110), channel_id=1, source_target_pairs={{0,12},{1,13},{2,14},{3,15},{4,8},{5,9},{6,10},{7,11},{8,4},{9,5},... | collective-permute-start | bytes 663560 | tf_op jit(solution)/shard_map/ppermute | solution.py:34
  249.5 18.9 %collective-permute-start.15 = (bf16[144,768]{1,0:T(8,128)(2,1)S(1)}, bf16[144,768]{1,0:T(8,128)(2,1)S(1)}, u32[]{:S(2)}, u32[]{:S(2)}) collective-permute-start(bf16[144,768]{1,0:T(8,128)(2,1)S(1)} %get-tuple-element.111), channel_id=1, source_target_pairs={{0,8},{1,9},{2,10},{3,11},{4,12},{5,13},{6,14},{7,15},{8,0},{9,1},... | collective-permute-start | bytes 663560 | tf_op jit(solution)/shard_map/ppermute | solution.py:34
  252.8 41.0 %collective-permute-start.23 = (bf16[4,192,768]{2,1,0:T(8,128)(2,1)S(1)}, bf16[4,192,768]{2,1,0:T(8,128)(2,1)S(1)}, u32[]{:S(2)}, u32[]{:S(2)}) collective-permute-start(bf16[4,192,768]{2,1,0:T(8,128)(2,1)S(1)} %fusion.8), channel_id=1, source_target_pairs={{0,2},{1,3},{2,0},{3,1},{4,6},{5,7},{6,4},{7,5},{8,10},{9,11},{10,... | collective-permute-start | bytes 3538952 | tf_op jit(solution)/shard_map/ppermute | solution.py:34
  271.5 53.3 %collective-permute-start.8 = (bf16[4,240,768]{2,1,0:T(8,128)(2,1)S(1)}, bf16[4,240,768]{2,1,0:T(8,128)(2,1)S(1)}, u32[]{:S(2)}, u32[]{:S(2)}) collective-permute-start(bf16[4,240,768]{2,1,0:T(8,128)(2,1)S(1)} %fusion), channel_id=1, source_target_pairs={{0,2},{1,3},{2,0},{3,1},{4,6},{5,7},{6,4},{7,5},{8,10},{9,11},{10,... | collective-permute-start | bytes 4423688 | tf_op jit(solution)/shard_map/ppermute | solution.py:34
  273.8 55.8 %collective-permute-start.19 = (bf16[192,768]{1,0:T(8,128)(2,1)S(1)}, bf16[192,768]{1,0:T(8,128)(2,1)S(1)}, u32[]{:S(2)}, u32[]{:S(2)}) collective-permute-start(bf16[192,768]{1,0:T(8,128)(2,1)S(1)} %get-tuple-element.104), channel_id=1, source_target_pairs={{0,4},{1,5},{2,6},{3,7},{4,0},{5,1},{6,2},{7,3},{8,12},{9,13},{10,... | collective-permute-start | bytes 884744 | tf_op jit(solution)/shard_map/ppermute | solution.py:34
  273.9 57.0 %collective-permute-start.21 = (bf16[192,768]{1,0:T(8,128)(2,1)S(1)}, bf16[192,768]{1,0:T(8,128)(2,1)S(1)}, u32[]{:S(2)}, u32[]{:S(2)}) collective-permute-start(bf16[192,768]{1,0:T(8,128)(2,1)S(1)} %get-tuple-element.105), channel_id=1, source_target_pairs={{0,12},{1,13},{2,14},{3,15},{4,8},{5,9},{6,10},{7,11},{8,4},{9,5},... | collective-permute-start | bytes 884744 | tf_op jit(solution)/shard_map/ppermute | solution.py:34
  276.6 55.6 %collective-permute-start.20 = (bf16[192,768]{1,0:T(8,128)(2,1)S(1)}, bf16[192,768]{1,0:T(8,128)(2,1)S(1)}, u32[]{:S(2)}, u32[]{:S(2)}) collective-permute-start(bf16[192,768]{1,0:T(8,128)(2,1)S(1)} %get-tuple-element.106), channel_id=1, source_target_pairs={{0,8},{1,9},{2,10},{3,11},{4,12},{5,13},{6,14},{7,15},{8,0},{9,1},... | collective-permute-start | bytes 884744 | tf_op jit(solution)/shard_map/ppermute | solution.py:34
  295.0 40.0 %collective-permute-start.24 = (bf16[192,768]{1,0:T(8,128)(2,1)S(1)}, bf16[192,768]{1,0:T(8,128)(2,1)S(1)}, u32[]{:S(2)}, u32[]{:S(2)}) collective-permute-start(bf16[192,768]{1,0:T(8,128)(2,1)S(1)} %get-tuple-element.101), channel_id=1, source_target_pairs={{0,4},{1,5},{2,6},{3,7},{4,0},{5,1},{6,2},{7,3},{8,12},{9,13},{10,... | collective-permute-start | bytes 884744 | tf_op jit(solution)/shard_map/ppermute | solution.py:34
  324.8 12.4 %collective-permute-start.26 = (bf16[192,768]{1,0:T(8,128)(2,1)}, bf16[192,768]{1,0:T(8,128)(2,1)}, u32[]{:S(2)}, u32[]{:S(2)}) collective-permute-start(bf16[192,768]{1,0:T(8,128)(2,1)} %get-tuple-element.102), channel_id=1, source_target_pairs={{0,12},{1,13},{2,14},{3,15},{4,8},{5,9},{6,10},{7,11},{8,4},{9,5},... | collective-permute-start | bytes 884744 | tf_op jit(solution)/shard_map/ppermute | solution.py:34
  329.6 40.7 %collective-permute-start.25 = (bf16[192,768]{1,0:T(8,128)(2,1)}, bf16[192,768]{1,0:T(8,128)(2,1)}, u32[]{:S(2)}, u32[]{:S(2)}) collective-permute-start(bf16[192,768]{1,0:T(8,128)(2,1)} %get-tuple-element.103), channel_id=1, source_target_pairs={{0,8},{1,9},{2,10},{3,11},{4,12},{5,13},{6,14},{7,15},{8,0},{9,1},... | collective-permute-start | bytes 884744 | tf_op jit(solution)/shard_map/ppermute | solution.py:34
  330.9 41.4 %collective-permute-start.9 = (bf16[240,768]{1,0:T(8,128)(2,1)}, bf16[240,768]{1,0:T(8,128)(2,1)}, u32[]{:S(2)}, u32[]{:S(2)}) collective-permute-start(bf16[240,768]{1,0:T(8,128)(2,1)} %get-tuple-element.98), channel_id=1, source_target_pairs={{0,4},{1,5},{2,6},{3,7},{4,0},{5,1},{6,2},{7,3},{8,12},{9,13},{10,... | collective-permute-start | bytes 1105928 | tf_op jit(solution)/shard_map/ppermute | solution.py:34
  332.2 40.1 %collective-permute-start.11 = (bf16[240,768]{1,0:T(8,128)(2,1)}, bf16[240,768]{1,0:T(8,128)(2,1)}, u32[]{:S(2)}, u32[]{:S(2)}) collective-permute-start(bf16[240,768]{1,0:T(8,128)(2,1)} %get-tuple-element.99), channel_id=1, source_target_pairs={{0,12},{1,13},{2,14},{3,15},{4,8},{5,9},{6,10},{7,11},{8,4},{9,5},... | collective-permute-start | bytes 1105928 | tf_op jit(solution)/shard_map/ppermute | solution.py:34
  335.0 50.0 %collective-permute-start.10 = (bf16[240,768]{1,0:T(8,128)(2,1)}, bf16[240,768]{1,0:T(8,128)(2,1)}, u32[]{:S(2)}, u32[]{:S(2)}) collective-permute-start(bf16[240,768]{1,0:T(8,128)(2,1)} %get-tuple-element.100), channel_id=1, source_target_pairs={{0,8},{1,9},{2,10},{3,11},{4,12},{5,13},{6,14},{7,15},{8,0},{9,1},... | collective-permute-start | bytes 1105928 | tf_op jit(solution)/shard_map/ppermute | solution.py:34
  (34 other events, 91.4 us)

commit v2 on v1

--- a/solution.py
+++ b/solution.py
@@ -83,33 +83,27 @@
     o_ref[...] = jnp.concatenate(outs, 0).astype(BF).T
 
 
-def backward_kernel(has_bias, scale, *refs):
-    if has_bias:
-        (q_ref, k_ref, v_ref, do_ref, o_ref, lse_ref, mask_ref, band_ref, onehot_ref, flipped_ref) = refs[:10]
-        dq_ref, dkv_ref, db_ref = refs[10:]
-        onehot = onehot_ref[...]
-        flipped = flipped_ref[...]
-    else:
-        q_ref, k_ref, v_ref, do_ref, o_ref, lse_ref, mask_ref = refs[:7]
-        dq_ref, dkv_ref = refs[7:]
-    count = q_ref.shape[0]
+def backward_pair(scale, queries, key_rows, values, grad_out, output, lse, mask, bias):
+    if bias is not None:
+        bands, onehot, flipped = bias
+    count = queries.shape[0]
     half = WIDE // 2
-    queries = (q_ref[...] * scale).T
-    key_rows = k_ref[...].T
-    values = v_ref[...].T
-    grad_out = do_ref[...].T
-    product = grad_out.astype(F32) * o_ref[...].T.astype(F32)
+    queries = (queries * scale).T
+    key_rows = key_rows.T
+    values = values.T
+    grad_out = grad_out.T
+    product = grad_out.astype(F32) * output.T.astype(F32)
     ones = jnp.ones((1, count), F32)
-    key_extra = extra_rows([ones, ones, ones, mask_ref[...]], count)
+    key_extra = extra_rows([ones, ones, ones, mask], count)
     value_extra = extra_rows([ones, ones, ones], count)
-    d_queries, d_keys, d_values = [], [], []
+    d_queries, d_keys, d_values, d_bands = [], [], [], []
     for side in range(2):
         part = slice(half * side, half * side + half)
-        lse_rows = extra_rows([*pieces(-lse_ref[0, side : side + 1, :]), ones], count)
+        lse_rows = extra_rows([*pieces(-lse[side : side + 1, :]), ones], count)
         delta = jnp.sum(product[part], axis=0, keepdims=True)
         delta_rows = extra_rows(list(pieces(-delta)), count)
-        if has_bias:
-            band = contract(band_ref[side], onehot, 1, 0).astype(BF)
+        if bias is not None:
+            band = contract(bands[side], onehot, 1, 0).astype(BF)
             left = jnp.concatenate([queries[part], band, lse_rows], 0)
             right = jnp.concatenate([key_rows[part], onehot, key_extra], 0)
         else:
@@ -126,15 +120,28 @@
         d_values.append(contract(grad_out[part], weights.astype(BF), 1, 0))
         d_keys.append(contract(queries[part], d_scores, 1, 0))
         scaled = key_rows[part] * scale
-        if has_bias:
+        if bias is not None:
             both = contract(jnp.concatenate([scaled, onehot], 0), d_scores, 1, 1)
             d_queries.append(both[:half])
-            db_ref[side] = contract(flipped, both[half:].astype(BF), 1, 1)
+            d_bands.append(contract(flipped, both[half:].astype(BF), 1, 1))
         else:
             d_queries.append(contract(scaled, d_scores, 1, 1))
-    dq_ref[...] = jnp.concatenate(d_queries, 0).astype(BF).T
-    dkv_ref[0] = jnp.concatenate(d_keys, 0).astype(BF).T
-    dkv_ref[1] = jnp.concatenate(d_values, 0).astype(BF).T
+    out = tuple(jnp.concatenate(each, 0).astype(BF).T for each in (d_queries, d_keys, d_values))
+    return out if bias is None else (*out, jnp.stack(d_bands))
+
+
+def backward_kernel(has_bias, scale, *refs):
+    q_ref, k_ref, v_ref, do_ref, o_ref, lse_ref, mask_ref = refs[:7]
+    bias = tuple(ref[...] for ref in refs[7:10]) if has_bias else None
+    outs = refs[10:] if has_bias else refs[7:]
+    grads = backward_pair(
+        scale, q_ref[...], k_ref[...], v_ref[...], do_ref[...], o_ref[...], lse_ref[0], mask_ref[...], bias
+    )
+    outs[0][...] = grads[0]
+    outs[1][0] = grads[1]
+    outs[1][1] = grads[2]
+    if has_bias:
+        outs[2][...] = grads[3]
 
 
 def column(first):
@@ -389,6 +396,625 @@
     for step in range(1, half):
         total = total + swapped(mine[step].astype(BF), "page", 4 * step).astype(F32)
     return total
+
+
+def flip(position, mask):
+    out = position
+    bit = 1
+    while bit <= mask:
+        if mask & bit:
+            out = out + bit * (1 - 2 * lax.rem(lax.div(position, bit), 2))
+        bit *= 2
+    return out
+
+
+LINK_US = 6.7
+CORE_US = 2.6
+
+
+class Flow:
+    def __init__(self, refs, me, side):
+        self.r = refs
+        self.me = me
+        self.side = side
+        self.now = 0.0
+        self.y_free = 0.0
+        self.z_free = 0.0
+        self.pending = []
+        self.started = 0
+
+    def at(self, mask):
+        return {"page": flip(self.me, mask)}
+
+    def core_copy(self, unit):
+        r = self.r
+        return pltpu.make_async_remote_copy(
+            src_ref=r.ring.at[unit % 3],
+            dst_ref=r.core_in.at[unit % 4],
+            send_sem=r.core_sent.at[unit],
+            recv_sem=r.core_got.at[unit],
+            device_id=self.at(1),
+            device_id_type=pl.DeviceIdType.MESH,
+        )
+
+    def y_copy(self, unit):
+        r = self.r
+        return pltpu.make_async_remote_copy(
+            src_ref=r.keep.at[unit, pl.ds(4, 4)],
+            dst_ref=r.y_in.at[unit],
+            send_sem=r.y_sent.at[unit],
+            recv_sem=r.y_got.at[unit],
+            device_id=self.at(2),
+            device_id_type=pl.DeviceIdType.MESH,
+        )
+
+    def z_copies(self, unit, arriving=False):
+        r = self.r
+        copies = []
+        if unit in DOWN_UNITS:
+            step = DOWN_UNITS.index(unit)
+            if step:
+                copies.append(
+                    pltpu.make_async_remote_copy(
+                        src_ref=r.keep.at[unit, pl.ds(0, 4)],
+                        dst_ref=r.z_down.at[step - 1],
+                        send_sem=r.z_sent.at[unit, 0],
+                        recv_sem=r.z_got.at[unit, 0],
+                        device_id=self.at(4 * step),
+                        device_id_type=pl.DeviceIdType.MESH,
+                    )
+                )
+        else:
+            for step in range(1, 4):
+                target = unit
+                if unit in UP_UNITS and not arriving:
+                    target = UP_UNITS[UP_UNITS.index(unit) ^ step]
+                copies.append(
+                    pltpu.make_async_remote_copy(
+                        src_ref=r.keep.at[unit, step],
+                        dst_ref=r.z_in.at[PLAIN_UNITS.index(target), step - 1],
+                        send_sem=r.z_sent.at[unit, step - 1],
+                        recv_sem=r.z_got.at[target, step - 1],
+                        device_id=self.at(4 * step),
+                        device_id_type=pl.DeviceIdType.MESH,
+                    )
+                )
+        return copies
+
+    def produce(self, unit, left, right):
+        r = self.r
+        r.sums[...] = contract(left, right, 0, 0).astype(BF)
+        self.tick(1.2)
+        if unit >= 3:
+            self.core_copy(unit - 3).wait_send()
+        core = lax.rem(self.me, 2)
+        y = lax.rem(lax.div(self.me, 2), 2)
+        z = lax.div(self.me, 4)
+        for rel_y in range(2):
+            for rel_z in range(4):
+                y_at = flip(y, rel_y)
+                if unit in DOWN_UNITS:
+                    first = y_at * 8 * ROWS
+                    mine = first + core * 4 * ROWS + rel_z * ROWS
+                    other = first + (1 - core) * 4 * ROWS + rel_z * ROWS
+                else:
+                    first = flip(z, rel_z) * 4 * ROWS + y_at * 2 * ROWS
+                    mine = first + core * ROWS
+                    other = first + (1 - core) * ROWS
+                slot = rel_y * 4 + rel_z
+                r.ring[unit % 3, slot] = r.sums[pl.ds(pl.multiple_of(other, 16), ROWS), :]
+                r.keep[unit, slot] = r.sums[pl.ds(pl.multiple_of(mine, 16), ROWS), :]
+        if unit >= 4:
+            pl.semaphore_wait(r.credit.at[unit - 4], 1)
+        self.core_copy(unit).start()
+        self.now += 0.5
+        self.pending.append([unit, 0, self.now + CORE_US])
+
+    def advance(self, entry):
+        self.plan(entry)()
+
+    def plan(self, entry):
+        unit, stage, _ = entry
+        if stage == 0:
+            self.y_free = max(self.now, self.y_free) + LINK_US
+            entry[1:] = [1, self.y_free + 0.3]
+        elif stage == 1:
+            self.z_free = max(self.now, self.z_free) + LINK_US
+            entry[1:] = [2, self.z_free + 0.5]
+            if unit in UP_UNITS:
+                entry[2] = float("inf")
+                ups = [e for e in self.pending if e[0] in UP_UNITS and e[1] == 2]
+                if len(ups) == len(UP_UNITS):
+                    for other in ups:
+                        other[2] = self.z_free + 0.5
+        else:
+            entry[1] = 3
+        return functools.partial(self.run, unit, stage)
+
+    def run(self, unit, stage):
+        r = self.r
+        if stage == 0:
+            self.core_copy(unit).wait_recv()
+            for slot in (4, 5, 6, 7, 0, 1, 2, 3):
+                total = r.keep[unit, slot].astype(F32) + r.core_in[unit % 4, slot].astype(F32)
+                r.keep[unit, slot] = total.astype(BF)
+                if slot == 7:
+                    self.y_copy(unit).start()
+            if unit < UNITS - 4:
+                pl.semaphore_signal(
+                    r.credit.at[unit], 1, device_id=self.at(1), device_id_type=pl.DeviceIdType.MESH
+                )
+        elif stage == 1:
+            self.y_copy(unit).wait_recv()
+            for slot in (1, 2, 3, 0):
+                total = r.keep[unit, slot].astype(F32) + r.y_in[unit, slot].astype(F32)
+                r.keep[unit, slot] = total.astype(BF)
+            for copy in self.z_copies(unit):
+                copy.start()
+        else:
+            for copy in self.z_copies(unit, arriving=True):
+                copy.wait_recv()
+            self.finish(unit)
+
+    def due(self):
+        while True:
+            ready = [e for e in self.pending if e[2] <= self.now]
+            if not ready:
+                return
+            entry = min(ready, key=lambda e: e[2])
+            yield entry
+            self.pending = [e for e in self.pending if e[1] < 3]
+
+    def tick(self, us):
+        self.now += us
+        for entry in self.due():
+            self.advance(entry)
+
+    def drain(self):
+        while self.pending:
+            self.now = max(self.now, min(e[2] for e in self.pending))
+            for entry in self.due():
+                self.advance(entry)
+        for unit in range(UNITS - 3, UNITS):
+            self.core_copy(unit).wait_send()
+        for unit in range(UNITS):
+            self.y_copy(unit).wait_send()
+            for copy in self.z_copies(unit):
+                copy.wait_send()
+
+    def finish(self, unit):
+        r = self.r
+        if unit in DOWN_UNITS:
+            step = DOWN_UNITS.index(unit)
+            total = r.keep[unit, 0:4].astype(F32) if step == 0 else r.z_down[step - 1].astype(F32)
+            total = total.reshape(4 * ROWS, -1)
+            if step == 0:
+                r.down_out[...] = total
+            else:
+                r.down_out[...] += total
+            return
+        total = r.keep[unit, 0].astype(F32)
+        for step in range(3):
+            total = total + r.z_in[PLAIN_UNITS.index(unit), step].astype(F32)
+        if unit in UP_UNITS:
+            tile = flip(lax.div(self.me, 4), UP_UNITS.index(unit))
+            r.up_out[:, pl.ds(pl.multiple_of(tile * WIDTH, WIDE), WIDTH)] = total
+            return
+        name, first = PLACES[unit]
+        getattr(r, name)[:, first : first + total.shape[1]] = total
+
+
+WIDTH = 768
+ROWS = 48
+DOWN_UNITS = (0, 2, 4, 6)
+UP_UNITS = (1, 3, 5, 7)
+PLAIN_UNITS = (1, 3, 5, 7, 8, 9, 10, 11, 12, 13, 14, 15)
+UNITS = 16
+PLACES = {
+    8: ("cout_out", 0),
+    9: ("cq_out", 0),
+    10: ("out_out", 0),
+    11: ("qkv_out", 0),
+    12: ("qkv_out", WIDTH),
+    13: ("qkv_out", 2 * WIDTH),
+    14: ("ckv_out", 0),
+    15: ("ckv_out", WIDTH),
+}
+
+
+class Refs:
+    pass
+
+
+INPUTS = (
+    "second", "low_grad", "after_cross", "w_up", "w_down", "w_cout", "crossed", "cross_query", "partner",
+    "low_middle", "attended", "w_cq", "w_out", "joined", "normed", "states", "w_qkv", "w_ckv",
+)
+SMALL_INPUTS = (
+    "valid", "gain1", "gain2", "cross_lse", "mask_other", "self_lse", "mask_own", "bands", "onehot", "flipped",
+)
+OUTPUTS = (
+    "result_out", "states_out",
+)
+KEPT_OUTPUTS = (
+    "down_out", "up_out", "cout_out", "cq_out", "out_out", "qkv_out", "ckv_out", "small_out",
+)
+SCRATCH = (
+    "s", "f", "w", "fetched", "stored", "sums", "keep", "ring", "core_in", "y_in", "z_in", "z_down",
+    "core_sent", "core_got", "y_sent", "y_got", "z_sent", "z_got", "credit", "back_sent", "back_got",
+    "small_in", "small_sent", "small_got", "d_bands",
+)
+
+
+def back_kernel(scale, *refs):
+    r = Refs()
+    for name, ref in zip(INPUTS + SMALL_INPUTS + OUTPUTS + KEPT_OUTPUTS + SCRATCH, refs, strict=True):
+        setattr(r, name, ref)
+    me = lax.axis_index("page")
+    side = lax.axis_index("stream")
+    flow = Flow(r, me, side)
+    count, width = r.second.shape
+    pairs = width // WIDE
+    half_rows = count // 2
+    z = lax.div(me, 4)
+
+    copies = []
+
+    def fetch(source, target):
+        copy = pltpu.make_async_copy(source, target, r.fetched.at[len(copies)])
+        copies.append(copy)
+        copy.start()
+        return copy
+
+    def tile_of(step):
+        return pl.ds(pl.multiple_of(flip(z, step) * width, WIDE), width)
+
+    got_second = fetch(r.second, r.s.at[0])
+    got_up = [fetch(r.w_up.at[:, tile_of(0)], r.w.at[0])]
+    got_grad = fetch(r.low_grad, r.s.at[1])
+    got_down = [fetch(r.w_down.at[tile_of(0)], r.w.at[1])]
+    got_after = fetch(r.after_cross, r.f.at[2])
+    got_up.append(fetch(r.w_up.at[:, tile_of(1)], r.w.at[2]))
+    got_down.append(fetch(r.w_down.at[tile_of(1)], r.w.at[3]))
+    got_cout = fetch(r.w_cout, r.w.at[4])
+    got_crossed = fetch(r.crossed, r.s.at[2])
+    got_query = fetch(r.cross_query, r.s.at[8])
+    got_keys = fetch(r.partner.at[:, 0:width], r.s.at[9])
+    got_values = fetch(r.partner.at[:, width : 2 * width], r.s.at[10])
+    got_middle = fetch(r.low_middle, r.s.at[11])
+    got_attended = fetch(r.attended, r.s.at[12])
+
+    barrier = pltpu.get_barrier_semaphore()
+    others = [{"page": flip(me, mask)} for mask in (1, 2, 4, 8, 12)] + [{"stream": 1 - side}]
+    for other in others:
+        pl.semaphore_signal(barrier, 1, device_id=other, device_id_type=pl.DeviceIdType.MESH)
+    pl.semaphore_wait(barrier, len(others))
+
+    hidden_at, d_up_at = 5, 6
+    for step in range(4):
+        up_at, down_at = (0, 1) if step % 2 == 0 else (2, 3)
+        if step == 0:
+            got_second.wait()
+        got_up[step].wait()
+        if step == 0:
+            got_grad.wait()
+        got_down[step].wait()
+        if step == 0:
+            got_after.wait()
+
+        @pl.loop(0, 2)
+        def _(part, step=step, up_at=up_at, down_at=down_at):
+            rows = pl.ds(pl.multiple_of(part * half_rows, 16), half_rows)
+            value = contract(r.s[0, rows, :], r.w[up_at], 1, 0)
+            hidden, slope = gelu_pair(value)
+            hidden = hidden.astype(BF)
+            r.s[hidden_at, rows, :] = hidden
+            back = contract(r.s[1, rows, :], r.w[down_at], 1, 1)
+            d_up = (slope * back).astype(BF)
+            r.s[d_up_at, rows, :] = d_up
+
+        flow.tick(2.4)
+        flow.produce(DOWN_UNITS[step], r.s[hidden_at], r.s[1])
+        flow.tick(0.1)
+        flow.produce(UP_UNITS[step], r.s[0], r.s[d_up_at])
+
+        @pl.loop(0, 2)
+        def _(part, step=step, up_at=up_at, down_at=down_at):
+            rows = pl.ds(pl.multiple_of(part * half_rows, 16), half_rows)
+            forward = contract(r.s[hidden_at, rows, :], r.w[down_at], 1, 0)
+            back = contract(r.s[d_up_at, rows, :], r.w[up_at], 1, 1)
+            if step == 0:
+                r.f[1, rows, :] = r.f[2, rows, :] + forward
+                r.f[0, rows, :] = back
+            else:
+                r.f[1, rows, :] += forward
+                r.f[0, rows, :] += back
+
+        if step < 2:
+            got_up.append(fetch(r.w_up.at[:, tile_of(step + 2)], r.w.at[up_at]))
+            got_down.append(fetch(r.w_down.at[tile_of(step + 2)], r.w.at[down_at]))
+        flow.tick(2.2)
+    got_w_cq = fetch(r.w_cq, r.w.at[0])
+    got_w_out = fetch(r.w_out, r.w.at[1])
+
+    r.s[7] = (r.f[1] * r.valid[...]).astype(BF)
+    sent_result = pltpu.make_async_copy(r.s.at[7], r.result_out, r.stored.at[0])
+    sent_result.start()
+    gain2_grad = norm_back(r.f, 2, 0, 0, r.gain2, r.s, 1, r.s, 3)
+    r.small_out[6:12, :] = fold(gain2_grad)
+    flow.tick(1.5)
+    got_cout.wait()
+    r.s[4] = contract(r.s[3], r.w[4], 1, 1).astype(BF)
+    flow.tick(1.2)
+    got_crossed.wait()
+    got_qkv = [fetch(r.joined.at[:, width * i : width * (i + 1)], r.s.at[at]) for i, at in enumerate((0, 1, 13))]
+    got_w_q = [fetch(r.w_qkv.at[:, width * i : width * (i + 1)], r.w.at[at]) for i, at in enumerate((2, 3, 4))]
+    flow.produce(8, r.s[2], r.s[3])
+    flow.tick(0.1)
+
+    got_query.wait()
+    got_keys.wait()
+    got_values.wait()
+    sent_result.wait()
+
+    def back_copy(pair):
+        lanes = pl.ds(pl.multiple_of(pair * WIDE, WIDE), WIDE)
+        return pltpu.make_async_remote_copy(
+            src_ref=r.s.at[pl.ds(6, 2), :, lanes],
+            dst_ref=r.s.at[pl.ds(15, 2), :, lanes],
+            send_sem=r.back_sent.at[pair],
+            recv_sem=r.back_got.at[pair],
+            device_id={"stream": 1 - side},
+            device_id_type=pl.DeviceIdType.MESH,
+        )
+
+    def pair_loop(us, step):
+        events = []
+        for pair in range(pairs):
+            flow.now += us
+            events.append([])
+            for entry in flow.due():
+                events[-1].append(flow.plan(entry))
+
+        @pl.loop(0, pairs)
+        def _(pair):
+            step(pair)
+            for place, steps in enumerate(events):
+                if steps:
+
+                    @pl.when(pair == place)
+                    def _(steps=steps):
+                        for run in steps:
+                            run()
+
+    def cross_step(pair):
+        lanes = pl.ds(pl.multiple_of(pair * WIDE, WIDE), WIDE)
+        d_query, d_key, d_value = backward_pair(
+            scale,
+            r.s[8, :, lanes],
+            r.s[9, :, lanes],
+            r.s[10, :, lanes],
+            r.s[4, :, lanes],
+            r.s[2, :, lanes],
+            r.cross_lse[pair],
+            r.mask_other[...],
+            None,
+        )
+        r.s[5, :, lanes] = d_query
+        r.s[6, :, lanes] = d_key
+        r.s[7, :, lanes] = d_value
+        back_copy(pair).start()
+
+    pair_loop(2.6, cross_step)
+
+    got_middle.wait()
+    flow.produce(9, r.s[11], r.s[5])
+    got_w_cq.wait()
+    r.f[0] = r.f[0] + contract(r.s[5], r.w[0], 1, 1)
+    r.s[3] = r.f[0].astype(BF)
+    got_w_ck = fetch(r.w_ckv.at[:, 0:width], r.w.at[0])
+    flow.tick(1.5)
+    got_attended.wait()
+    flow.produce(10, r.s[12], r.s[3])
+    got_w_out.wait()
+    r.s[4] = contract(r.s[3], r.w[1], 1, 1).astype(BF)
+    got_w_cv = fetch(r.w_ckv.at[:, width : 2 * width], r.w.at[1])
+    got_normed = fetch(r.normed, r.s.at[14])
+    got_states = fetch(r.states, r.s.at[2])
+    flow.tick(1.2)
+
+    for copy in got_qkv:
+        copy.wait()
+
+    def self_step(pair):
+        lanes = pl.ds(pl.multiple_of(pair * WIDE, WIDE), WIDE)
+        d_query, d_key, d_value, d_bands = backward_pair(
+            scale,
+            r.s[0, :, lanes],
+            r.s[1, :, lanes],
+            r.s[13, :, lanes],
+            r.s[4, :, lanes],
+            r.s[12, :, lanes],
+            r.self_lse[pair],
+            r.mask_own[...],
+            (r.bands[pair], r.onehot[...], r.flipped[...]),
+        )
+        r.s[8, :, lanes] = d_query
+        r.s[9, :, lanes] = d_key
+        r.s[10, :, lanes] = d_value
+        r.d_bands[pair] = d_bands
+
+    pair_loop(3.4, self_step)
+
+    got_normed.wait()
+    for unit, at in ((11, 8), (12, 9), (13, 10)):
+        flow.produce(unit, r.s[14], r.s[at])
+        flow.tick(0.1)
+    for copy in got_w_q:
+        copy.wait()
+    r.f[1] = (
+        contract(r.s[8], r.w[2], 1, 1) + contract(r.s[9], r.w[3], 1, 1) + contract(r.s[10], r.w[4], 1, 1)
+    )
+    flow.tick(3)
+    for head in range(2 * pairs):
+        across, down = unband(r.d_bands[head // 2, head % 2])
+        r.small_out[16 + head : 17 + head, :] = across
+        r.small_out[16 + 2 * pairs + head : 17 + 2 * pairs + head, :] = down
+    flow.tick(1)
+
+    @pl.loop(0, pairs)
+    def _(pair):
+        back_copy(pair).wait_send()
+        back_copy(pair).wait_recv()
+
+    for unit, at in ((14, 15), (15, 16)):
+        flow.produce(unit, r.s[14], r.s[at])
+        flow.tick(0.1)
+    got_w_ck.wait()
+    got_w_cv.wait()
+    r.f[1] += contract(r.s[15], r.w[0], 1, 1) + contract(r.s[16], r.w[1], 1, 1)
+    flow.tick(2)
+    got_states.wait()
+
+    @pl.loop(0, 2)
+    def _(part):
+        rows = pl.ds(pl.multiple_of(part * half_rows, 16), half_rows)
+        r.f[2, rows, :] = r.s[2, rows, :].astype(F32)
+
+    gain1_grad = norm_back(r.f, 2, 1, 0, r.gain1, None, None, None, None)
+    sent_states = pltpu.make_async_copy(r.f.at[0], r.states_out, r.stored.at[1])
+    sent_states.start()
+    r.small_out[0:6, :] = fold(gain1_grad)
+    r.small_out[12:16, :] = jnp.zeros((4, WIDE), F32)
+    flow.tick(2)
+
+    def small_copy(place, mask):
+        return pltpu.make_async_remote_copy(
+            src_ref=r.small_in.at[5 + SMALL_STAGE[place]],
+            dst_ref=r.small_in.at[place],
+            send_sem=r.small_sent.at[place],
+            recv_sem=r.small_got.at[place],
+            device_id={"page": flip(me, mask)},
+            device_id_type=pl.DeviceIdType.MESH,
+        )
+
+    for stage, places in enumerate(((0,), (1,), (2, 3, 4))):
+        r.small_in[5 + stage] = r.small_out[...]
+        moves = [small_copy(place, (1, 2, 4, 8, 12)[place]) for place in places]
+        for move in moves:
+            move.start()
+        flow.tick(1.5)
+        for place, move in zip(places, moves):
+            move.wait_recv()
+            r.small_out[...] += r.small_in[place]
+        for move in moves:
+            move.wait_send()
+
+    flow.drain()
+    sent_states.wait()
+
+
+SMALL_STAGE = (0, 1, 2, 2, 2)
+
+
+def fold(row):
+    return jnp.concatenate([row[:, WIDE * i : WIDE * (i + 1)] for i in range(row.shape[1] // WIDE)], 0)
+
+
+def norm_back(f, inputs_at, grad_at, total_at, gain, s, s_grad_at, s_out, s_out_at):
+    count = f.shape[1]
+    chunk = count // 4
+    gain_grad = jnp.zeros((1, f.shape[2]), F32)
+    for part in range(4):
+        rows = slice(part * chunk, (part + 1) * chunk)
+        inputs = f[inputs_at, rows, :]
+        grad = f[grad_at, rows, :]
+        centre = inputs - jnp.mean(inputs, axis=-1, keepdims=True)
+        spread = lax.rsqrt(jnp.mean(centre * centre, axis=-1, keepdims=True) + EPSILON)
+        normed = centre * spread
+        gain_grad = gain_grad + jnp.sum(grad * normed, axis=0, keepdims=True)
+        scaled = grad * gain[...]
+        back = spread * (
+            scaled
+            - jnp.mean(scaled, axis=-1, keepdims=True)
+            - normed * jnp.mean(scaled * normed, axis=-1, keepdims=True)
+        )
+        if s is not None:
+            total = s[s_grad_at, rows, :].astype(F32) + back
+            s_out[s_out_at, rows, :] = total.astype(BF)
+        else:
+            total = f[total_at, rows, :] + back
+        f[total_at, rows, :] = total
+    return gain_grad
+
+
+def unband(grad):
+    half = WIDE // 2
+    rolled = pltpu.roll(jnp.where(same_block((WIDE, WIDE)), grad, 0.0), 0, 1, stride=1, stride_axis=0)
+    return jnp.sum(rolled[:half], axis=0, keepdims=True), jnp.sum(rolled[half:], axis=0, keepdims=True)
+
+
+def backward_pass(operands, scale):
+    count, width = operands["second"].shape
+    hidden_width = operands["w_up"].shape[1]
+    heads = operands["bands"].shape[0]
+    pairs = heads // 2
+    operands = dict(operands)
+    operands["bands"] = operands["bands"].reshape(pairs, 2, WIDE, WIDE)
+    rows = width // 16
+    outs = [
+        jax.ShapeDtypeStruct((count, width), BF),
+        jax.ShapeDtypeStruct((count, width), F32),
+        jax.ShapeDtypeStruct((hidden_width // 16, width), F32),
+        jax.ShapeDtypeStruct((rows, hidden_width), F32),
+        jax.ShapeDtypeStruct((rows, width), F32),
+        jax.ShapeDtypeStruct((rows, width), F32),
+        jax.ShapeDtypeStruct((rows, width), F32),
+        jax.ShapeDtypeStruct((rows, 3 * width), F32),
+        jax.ShapeDtypeStruct((rows, 2 * width), F32),
+        jax.ShapeDtypeStruct((16 + 2 * heads, WIDE), F32),
+    ]
+    anywhere = pl.BlockSpec(memory_space=pl.ANY)
+    inside = pl.BlockSpec(memory_space=pltpu.VMEM)
+    dma = pltpu.SemaphoreType.DMA
+    small = (16 + 2 * heads, WIDE)
+    return pl.pallas_call(
+        functools.partial(back_kernel, scale),
+        in_specs=[anywhere] * len(INPUTS) + [inside] * len(SMALL_INPUTS),
+        out_specs=[anywhere] * len(OUTPUTS) + [inside] * len(KEPT_OUTPUTS),
+        out_shape=outs,
+        scratch_shapes=[
+            pltpu.VMEM((17, count, width), BF),
+            pltpu.VMEM((3, count, width), F32),
+            pltpu.VMEM((5, width, width), BF),
+            dma((32,)),
+            dma((2,)),
+            pltpu.VMEM((width, width), BF),
+            pltpu.VMEM((UNITS, 8, rows, width), BF),
+            pltpu.VMEM((3, 8, rows, width), BF),
+            pltpu.VMEM((4, 8, rows, width), BF),
+            pltpu.VMEM((UNITS, 4, rows, width), BF),
+            pltpu.VMEM((len(PLAIN_UNITS), 3, rows, width), BF),
+            pltpu.VMEM((3, 4, rows, width), BF),
+            dma((UNITS,)),
+            dma((UNITS,)),
+            dma((UNITS,)),
+            dma((UNITS,)),
+            dma((UNITS, 3)),
+            dma((UNITS, 3)),
+            pltpu.SemaphoreType.REGULAR((UNITS,)),
+            dma((pairs,)),
+            dma((pairs,)),
+            pltpu.VMEM((8, *small), F32),
+            dma((5,)),
+            dma((5,)),
+            pltpu.VMEM((pairs, 2, WIDE, WIDE), F32),
+        ],
+        compiler_params=pltpu.CompilerParams(
+            collective_id=0, has_side_effects=True, vmem_limit_bytes=(64 << 20) - (256 << 10)
+        ),
+        cost_estimate=cost(150),
+    )(*[operands[name] for name in INPUTS + SMALL_INPUTS])
 
 
 def norm_rows(inputs, gain_row):
@@ -466,6 +1092,58 @@
     second = second.astype(BF)
     out_grad = cotangent[0, 0].astype(F32) * valid
     low_grad = out_grad.astype(BF)
+    if parts == 16 and width == WIDTH and w_up.shape[1] == 4 * width:
+        operands = dict(
+            second=second,
+            low_grad=low_grad,
+            after_cross=after_cross,
+            w_up=w_up,
+            w_down=w_down,
+            w_cout=w_cout,
+            crossed=crossed,
+            cross_query=cross_query,
+            partner=partner,
+            low_middle=low_middle,
+            attended=attended,
+            w_cq=w_cq,
+            w_out=w_out,
+            joined=joined,
+            normed=normed,
+            states=states[0, 0],
+            w_qkv=w_qkv,
+            w_ckv=w_ckv,
+            valid=valid,
+            gain1=ln1_gain,
+            gain2=ln2_gain,
+            cross_lse=cross_lse,
+            mask_other=mask_other,
+            self_lse=self_lse,
+            mask_own=mask_own,
+            bands=bands,
+            onehot=onehot,
+            flipped=flipped,
+        )
+        result, states_grad, down, up, cout, cq, out, qkv, ckv, small = backward_pass(operands, scale)
+        rows = width // parts
+        table_rows = 2 * buckets // parts
+        gain_sums = small[:12].reshape(2, parts, rows)
+        gain_sums = lax.dynamic_index_in_dim(gain_sums, me[0], 1, keepdims=True)
+        table_sum = small[16:, ::-1].T.reshape(parts, table_rows, 2 * heads)
+        table_sum = lax.dynamic_index_in_dim(table_sum, me[0], 0, keepdims=True)
+        return (
+            result[None, None],
+            states_grad[None, None],
+            gain_sums[0],
+            gain_sums[1],
+            table_sum,
+            qkv[None],
+            out[None],
+            cq[None],
+            ckv[None],
+            cout[None],
+            up[None],
+            down[None],
+        )
     hidden, d_up, *down_parts = feed_forward(me, second, low_grad, w_up, w_down, parts)
     down_sum = reduce_parts(*down_parts)
     up_sum = reduce_parts(*outer_products(me, [(second, d_up)], parts, 6))

time: 394 us -> 248 us (0.63)
  waiting for transfers between devices: 149 us -> 12.3 us
  Pallas kernels: 114 us -> 187 us
  starting transfers between devices: 33.9 us -> 2.94 us
  other arithmetic: 33.3 us -> 9.91 us
  matrix products: 33.4 us -> 13.9 us
  local copies, waits for them, and re-layouts: 22 us -> 15 us
    ppermute x27 -> x1, waiting for transfers between devices: 149 us -> 12.3 us  [swapped(): lax.ppermute(shard, axis, [(i, i ^ mask) for i in range(lax.axis_size(axi...]
    pallas_call x7 -> x1, Pallas kernels: 90.4 us -> 163 us  [backward_pass(): pl.pallas_call(functools.partial(back_kernel, scale), in_specs=[anywhere]...]
    ppermute x27 -> x1, starting transfers between devices: 33.9 us -> 2.94 us  [swapped(): lax.ppermute(shard, axis, [(i, i ^ mask) for i in range(lax.axis_size(axi...]
    dot_general x15 -> x5, matrix products: 33.4 us -> 13.9 us  [contract(): lax.dot_general(left, right, (((left_dim,), (right_dim,)), ((), ())), pre...]
    convert_element_type x10 -> x0, other arithmetic: 12.4 us -> none  [the longest x4 8.73 us: reduce_parts(): arrived = swapped(send, 'page', 1).astype(F32)]
    another operation x4 -> x0, other arithmetic: 4.45 us -> none
    reshape x8 -> x1, local copies, waits for them, and re-layouts: 4.35 us -> 0.07 us  [body(): gain_sums = small[:12].reshape(2, parts, rows)]
    unnamed x112 -> x87, local copies, waits for them, and re-layouts: 9.2 us -> 11.5 us
  transfers between devices with their start and end apart: 27 -> 1, of which waited for: 10 -> 1; matrix products, arithmetic and copies ran while one was open for 13% -> 6% of each run, Pallas kernels for 9% -> 5%
where the time goes in v2:
time: 248 us; the launch traced here: 243 us
  Pallas kernels  187 us (75%)
  local copies, waits for them, and re-layouts  15 us (6%)
  matrix products  13.9 us (6%)
  waiting for transfers between devices  12.3 us (5%)
  other arithmetic  9.91 us (4%)
  starting transfers between devices  2.94 us (1%)
  between operations  2.64 us (1%)
    pallas_call x1, Pallas kernels, backward_pass(): pl.pallas_call(functools.partial(back_kernel, scale), in_specs=[anywhere]...  163 us
    pallas_call x2, Pallas kernels, attend_forward(): pl.pallas_call(functools.partial(forward_kernel, bias is not None, scale)...  23.3 us
    dot_general x5, matrix products, contract(): lax.dot_general(left, right, (((left_dim,), (right_dim,)), ((), ())), pre...  13.9 us
    ppermute x1, waiting for transfers between devices, swapped(): lax.ppermute(shard, axis, [(i, i ^ mask) for i in range(lax.axis_size(axi...  12.3 us
    unnamed x87, local copies, waits for them, and re-layouts  11.5 us
  transfers between devices with their start and end apart: 1, of which 1 were waited for; matrix products, arithmetic and copies ran while one was open for 6% of the time, Pallas kernels for 5%

profile of v2, /device:TPU:0, one launch (start us, length us, event | category | flops | bytes accessed | tf_op | source)
XLA Modules:
  0.0 243.3 jit_solution(18001979603249047936)
XLA Ops:
  0.7 1.5 convert_reduce_fusion
  2.2 1.6 fusion.2
  3.9 0.0 copy-start.37
  3.9 0.0 copy-start.35
  3.9 4.7 %convolution_convert_fusion.1 = bf16[640,1536]{1,0:T(8,128)(2,1)} fusion(bf16[1,768,1536]{2,1,0:T(8,128)(2,1)} %param.25, bf16[1,1,640,768]{3,2,1,0:T(8,128)(2,1)S(1)} %copy-done.13, f32[768]{0:T(1024)S(1)} %reduce, f32[640]{0:T(1024)S(1)} %add_rsqrt_fusion.1, f32[640]{0:T(1024)S(1)} %broadcast_multiply_fusion.1), kind=kOutput, calls=%fused_computation.1 | convolution fusion | flops 1513390080 | bytes 5316608 | tf_op jit(solution)/shard_map/dot_general | solution.py:20
  8.6 2.9 %collective-permute-start = (bf16[640,1536]{1,0:T(8,128)(2,1)}, bf16[640,1536]{1,0:T(8,128)(2,1)S(1)}, u32[]{:S(2)}, u32[]{:S(2)}) collective-permute-start(bf16[640,1536]{1,0:T(8,128)(2,1)} %convolution_convert_fusion.1), channel_id=1, source_target_pairs={{0,16},{16,0},{1,17},{17,1},{2,18},{18,2},{3,19},{19,3},{4,20},{20... | collective-permute-start | bytes 5898248 | tf_op jit(solution)/shard_map/ppermute | solution.py:34
  11.6 0.6 constant_dynamic-slice_fusion.1
  12.8 1.0 subtract_reduce_fusion
  13.9 0.6 iota_compare_fusion.4
  15.3 0.0 copy-start.6
  15.3 4.6 %convolution_convert_fusion.refs_0_.refs_1_.refs_2_.refs_13_ = bf16[640,2304]{1,0:T(8,128)(2,1)S(1)} fusion(bf16[1,768,2304]{2,1,0:T(8,128)(2,1)} %param.22, bf16[1,1,640,768]{3,2,1,0:T(8,128)(2,1)S(1)} %copy-done.13, f32[768]{0:T(1024)S(1)} %reduce, f32[640]{0:T(1024)S(1)} %add_rsqrt_fusion.1, f32[640]{0:T(1024)S(1)} %broadcast_multiply_fusion.1), kind=kOutput, calls=%fused_computation | convolution fusion | flops 2268856320 | bytes 7479296 | tf_op jit(solution)/shard_map/dot_general | solution.py:20
  19.9 0.0 copy-start.23
  19.9 0.2 shard_map.238.refs_4_
  20.1 0.7 copy-done.23
  20.8 0.0 copy-start.2
  20.8 0.7 copy-done.9
  21.5 12.3 %shard_map.239 = (bf16[640,768]{1,0:T(8,128)(2,1)S(1)}, f32[6,2,640]{2,1,0:T(2,128)S(1)}) custom-call(bf16[640,2304]{1,0:T(8,128)(2,1)S(1)} %convolution_convert_fusion.refs_0_.refs_1_.refs_2_.refs_13_, bf16[640,2304]{1,0:T(8,128)(2,1)S(1)} %convolution_convert_fusion.refs_0_.refs_1_.refs_2_.refs_13_, ...), custom_call_target="tpu_custom_call" | custom-call | flops 19800000512 | bytes 1048576 | tf_op jit(solution)/shard_map/pallas_call | solution.py:162
  33.8 0.6 copy-done.11
  34.5 0.8 add_convert_fusion.1.refs_27_
  35.3 0.8 fusion.7.refs_18_
  36.1 2.6 %fusion.18 = (bf16[640,768]{1,0:T(8,128)(2,1)S(1)}, f32[640,768]{1,0:T(8,128)S(1)}) fusion(bf16[640,768]{1,0:T(8,128)(2,1)S(1)} %get-tuple-element.26.refs_10_, bf16[1,768,768]{2,1,0:T(8,128)(2,1)} %param.23, bf16[1,1,640,768]{3,2,1,0:T(8,128)(2,1)} %param.15), kind=kOutput, calls=%fused_computation.52 | convolution fusion | flops 756449280 | bytes 6094848 | tf_op jit(solution)/shard_map/dot_general | solution.py:20
  38.7 0.9 convolution_convert_fusion.2.refs_0_.refs_7_
  39.7 0.0 copy-done.17
  39.7 0.6 copy-done.14
  40.2 0.3 copy-done.18
  40.5 1.8 fusion.4
  42.3 12.3 %collective-permute-done.refs_1_.refs_2_.refs_8_ = bf16[640,1536]{1,0:T(8,128)(2,1)S(1)} collective-permute-done((bf16[640,1536]{1,0:T(8,128)(2,1)}, bf16[640,1536]{1,0:T(8,128)(2,1)S(1)}, u32[]{:S(2)}, u32[]{:S(2)}) %collective-permute-start) | collective-permute-done | bytes 1966112 | tf_op jit(solution)/shard_map/ppermute | solution.py:34
  54.6 11.0 %shard_map.240 = (bf16[640,768]{1,0:T(8,128)(2,1)S(1)}, f32[6,2,640]{2,1,0:T(2,128)S(1)}) custom-call(bf16[640,768]{1,0:T(8,128)(2,1)S(1)} %convolution_convert_fusion.2.refs_0_.refs_7_, bf16[640,1536]{1,0:T(8,128)(2,1)S(1)} %collective-permute-done.refs_1_.refs_2_.refs_8_, bf16[640,1536]{1,0:T(8,128)(2,1)S(1)} %collective-permute-done.refs_1_.refs_2_.refs_8_, ...), custom_call_target="tpu_custom_call" | custom-call | flops 17600000000 | bytes 1048576 | tf_op jit(solution)/shard_map/pallas_call | solution.py:162
  65.7 1.0 fusion.19
  66.7 0.4 multiply_reduce_fusion
  67.1 1.3 multiply_convert_fusion.refs_0_
  68.4 163.2 %shard_map.241 = (bf16[640,768]{1,0:T(8,128)(2,1)}, f32[640,768]{1,0:T(8,128)}, f32[192,768]{1,0:T(8,128)}, f32[48,3072]{1,0:T(8,128)}, f32[48,768]{1,0:T(8,128)...) custom-call(bf16[640,768]{1,0:T(8,128)(2,1)} %multiply_convert_fusio, ...), custom_call_target="tpu_custom_call" | custom-call | flops 165000003584 | bytes 1048576 | tf_op jit(solution)/shard_map/pallas_call | solution.py:981
  231.6 0.9 slice.15
  232.5 0.7 slice.12
  233.2 0.1 rev.3
  233.2 0.1 copy.28
  233.3 0.1 reshape.193
  233.4 0.6 constant_dynamic-slice_fusion.3
  234.0 0.5 fusion.9
  234.5 2.2 copy.38
  236.8 1.3 copy.39
  238.0 0.8 copy.40
  238.8 0.7 copy.41
  239.5 0.7 copy.42
  240.1 0.7 copy.43
  240.9 0.7 copy.44
  241.5 0.8 copy.45
  242.3 0.8 copy.46
  (79 shorter events, 0.3 us)
Async XLA Ops:
  0.6 3.2 %copy-start.13 = (bf16[1,1,640,768]{3,2,1,0:T(8,128)(2,1)S(1)}, bf16[1,1,640,768]{3,2,1,0:T(8,128)(2,1)}, u32[]{:S(2)}) copy-start(bf16[1,1,640,768]{3,2,1,0:T(8,128)(2,1)} %param.15) | copy-start | bytes 2949124
  0.7 3.1 %copy-start.33 = (f32[1,768]{1,0:T(1,128)S(1)}, f32[1,768]{1,0:T(1,128)}, u32[]{:S(2)}) copy-start(f32[1,768]{1,0:T(1,128)} %refs_19_.1) | copy-start | bytes 9220
  3.8 11.4 %copy-start.29 = (f32[640]{0:T(1024)}, f32[640]{0:T(1024)S(1)}, u32[]{:S(2)}) copy-start(f32[640]{0:T(1024)S(1)} %add_rsqrt_fusion.1) | copy-start | bytes 7684
  3.8 11.4 %copy-start.31 = (f32[768]{0:T(1024)}, f32[768]{0:T(1024)S(1)}, u32[]{:S(2)}) copy-start(f32[768]{0:T(1024)S(1)} %reduce) | copy-start | bytes 9220
  3.9 7.7 %copy-start.37 = (s32[2,1]{0,1:T(1,128)S(1)}, s32[2,1]{0,1:T(1,128)}, u32[]{:S(2)}) copy-start(s32[2,1]{0,1:T(1,128)} %param.16) | copy-start | bytes 28
  3.9 9.0 %copy-start.35 = (s32[1,640]{1,0:T(1,128)S(1)}, s32[1,640]{1,0:T(1,128)}, u32[]{:S(2)}) copy-start(s32[1,640]{1,0:T(1,128)} %param.18) | copy-start | bytes 7684
  3.9 8.9 %copy-start.36 = (s32[1,640]{1,0:T(1,128)S(1)}, s32[1,640]{1,0:T(1,128)}, u32[]{:S(2)}) copy-start(s32[1,640]{1,0:T(1,128)} %param.17) | copy-start | bytes 7684
  8.6 46.0 %collective-permute-start = (bf16[640,1536]{1,0:T(8,128)(2,1)}, bf16[640,1536]{1,0:T(8,128)(2,1)S(1)}, u32[]{:S(2)}, u32[]{:S(2)}) collective-permute-start(bf16[640,1536]{1,0:T(8,128)(2,1)} %convolution_convert_fusion.1), channel_id=1, source_target_pairs={{0,16},{16,0},{1,17},{17,1},{2,18},{18,2},{3,19},{19,3},{4,20},{20... | collective-permute-start | bytes 5898248 | tf_op jit(solution)/shard_map/ppermute | solution.py:34
  15.2 5.5 %copy-start.4 = (f32[1,640]{1,0:T(1,128)}, f32[1,640]{1,0:T(1,128)S(1)}, u32[]{:S(2)}) copy-start(f32[1,640]{1,0:T(1,128)S(1)} %get-tuple-element.79.refs_3_.refs_24_) | copy-start | bytes 7684
  15.2 39.4 %copy-start.3 = (f32[1,640]{1,0:T(1,128)}, f32[1,640]{1,0:T(1,128)S(1)}, u32[]{:S(2)}) copy-start(f32[1,640]{1,0:T(1,128)S(1)} %get-tuple-element.78.refs_3_.refs_22_) | copy-start | bytes 7684
  15.3 4.6 %copy-start.6 = (f32[1,128,24]{1,2,0:T(8,128)S(1)}, f32[1,128,24]{1,2,0:T(8,128)}, u32[]{:S(2)}) copy-start(f32[1,128,24]{1,2,0:T(8,128)} %param.21) | copy-start | bytes 36868
  19.9 1.6 copy-start.9
  19.9 0.9 copy-start.23
  20.7 13.0 %copy-start.7 = (bf16[12,128,128]{2,1,0:T(8,128)(2,1)}, bf16[12,128,128]{2,1,0:T(8,128)(2,1)S(1)}, u32[]{:S(2)}) copy-start(bf16[12,128,128]{2,1,0:T(8,128)(2,1)S(1)} %shard_map.238.refs_4_) | copy-start | bytes 1179652
  20.8 13.0 %copy-start.2 = (bf16[128,640]{1,0:T(8,128)(2,1)}, bf16[128,640]{1,0:T(8,128)(2,1)S(1)}, u32[]{:S(2)}) copy-start(bf16[128,640]{1,0:T(8,128)(2,1)S(1)} %add_convert_fusion.refs_5_.refs_26_) | copy-start | bytes 491524
  21.5 12.9 %copy-start.34 = (f32[1,768]{1,0:T(1,128)S(1)}, f32[1,768]{1,0:T(1,128)}, u32[]{:S(2)}) copy-start(f32[1,768]{1,0:T(1,128)} %refs_20_.1) | copy-start | bytes 9220
  21.5 13.0 %copy-start.28 = (s32[640]{0:T(1024)S(1)}, s32[640]{0:T(1024)}, u32[]{:S(2)}) copy-start(s32[640]{0:T(1024)} %get-tuple-element.64) | copy-start | bytes 7684
  21.5 13.0 %copy-start.27 = (s32[640]{0:T(1024)S(1)}, s32[640]{0:T(1024)}, u32[]{:S(2)}) copy-start(s32[640]{0:T(1024)} %get-tuple-element.75) | copy-start | bytes 7684
  33.8 0.6 copy-start.11
  34.4 4.3 %copy-start = (bf16[640,768]{1,0:T(8,128)(2,1)}, bf16[640,768]{1,0:T(8,128)(2,1)S(1)}, u32[]{:S(2)}) copy-start(bf16[640,768]{1,0:T(8,128)(2,1)S(1)} %get-tuple-element.26.refs_10_) | copy-start | bytes 2949124
  36.1 2.6 %copy-start.38 = (bf16[1,768,768]{2,1,0:T(8,128)(2,1)S(1)}, bf16[1,768,768]{2,1,0:T(8,128)(2,1)}, u32[]{:S(2)}) copy-start(bf16[1,768,768]{2,1,0:T(8,128)(2,1)} %param.24) | copy-start | bytes 3538948
  38.7 1.0 copy-start.17
  38.7 1.6 copy-start.14
  38.7 1.8 copy-start.18
  38.7 1.8 copy-start.30
  38.7 1.8 copy-start.32
  40.5 14.1 %copy-start.8 = (bf16[640,768]{1,0:T(8,128)(2,1)}, bf16[640,768]{1,0:T(8,128)(2,1)S(1)}, u32[]{:S(2)}) copy-start(bf16[640,768]{1,0:T(8,128)(2,1)S(1)} %convolution_convert_fusion.2.refs_0_.refs_7_) | copy-start | bytes 2949124
  54.6 11.0 %copy-start.5 = (bf16[640,1536]{1,0:T(8,128)(2,1)}, bf16[640,1536]{1,0:T(8,128)(2,1)S(1)}, u32[]{:S(2)}) copy-start(bf16[640,1536]{1,0:T(8,128)(2,1)S(1)} %collective-permute-done.refs_1_.refs_2_.refs_8_) | copy-start | bytes 5898244
  54.6 11.1 %copy-start.16 = (bf16[1,768,768]{2,1,0:T(8,128)(2,1)S(1)}, bf16[1,768,768]{2,1,0:T(8,128)(2,1)}, u32[]{:S(2)}) copy-start(bf16[1,768,768]{2,1,0:T(8,128)(2,1)} %param.26) | copy-start | bytes 3538948
  65.6 1.1 copy-start.1
  65.6 1.1 copy-start.10
  66.7 1.7 copy-start.12
  231.6 5.1 %copy-start.15 = (f32[640,768]{1,0:T(8,128)S(1)}, f32[640,768]{1,0:T(8,128)}, u32[]{:S(2)}) copy-start(f32[640,768]{1,0:T(8,128)} %get-tuple-element.31) | copy-start | bytes 5898244
  236.7 1.3 copy-start.21
  236.7 2.1 copy-start.26
  236.7 2.7 %copy-start.25 = (f32[48,768]{1,0:T(8,128)S(1)}, f32[48,768]{1,0:T(8,128)}, u32[]{:S(2)}) copy-start(f32[48,768]{1,0:T(8,128)} %get-tuple-element.35) | copy-start | bytes 442372
  236.8 3.4 %copy-start.22 = (f32[48,1536]{1,0:T(8,128)S(1)}, f32[48,1536]{1,0:T(8,128)}, u32[]{:S(2)}) copy-start(f32[48,1536]{1,0:T(8,128)} %get-tuple-element.36) | copy-start | bytes 884740
  238.0 2.8 %copy-start.24 = (f32[48,768]{1,0:T(8,128)S(1)}, f32[48,768]{1,0:T(8,128)}, u32[]{:S(2)}) copy-start(f32[48,768]{1,0:T(8,128)} %get-tuple-element.37) | copy-start | bytes 442372
  238.0 3.5 %copy-start.20 = (f32[48,3072]{1,0:T(8,128)S(1)}, f32[48,3072]{1,0:T(8,128)}, u32[]{:S(2)}) copy-start(f32[48,3072]{1,0:T(8,128)} %get-tuple-element.38) | copy-start | bytes 1769476
  238.0 4.3 %copy-start.19 = (f32[192,768]{1,0:T(8,128)S(1)}, f32[192,768]{1,0:T(8,128)}, u32[]{:S(2)}) copy-start(f32[192,768]{1,0:T(8,128)} %get-tuple-element.39) | copy-start | bytes 1769476

commit v3 on v1

--- a/solution.py
+++ b/solution.py
@@ -1,4 +1,5 @@
 import functools
+from typing import Any, NamedTuple
 
 import jax
 import jax.numpy as jnp
@@ -11,6 +12,8 @@
 GRID_LARGE = 24
 EPSILON = 1e-05
 MASKED = -1000000000.0
+PAGE = "page"
+STREAM = "stream"
 BF = jnp.bfloat16
 F32 = jnp.float32
 WIDE = 128
@@ -49,25 +52,21 @@
     return block.astype(BF)
 
 
-def forward_kernel(has_bias, scale, *refs):
-    if has_bias:
-        q_ref, k_ref, v_ref, mask_ref, band_ref, onehot_ref, o_ref, lse_ref = refs
-        onehot = onehot_ref[...]
-    else:
-        q_ref, k_ref, v_ref, mask_ref, o_ref, lse_ref = refs
-    count = q_ref.shape[0]
+def forward_pair(scale, queries, key_rows, values, mask, bias):
+    count = queries.shape[0]
     half = WIDE // 2
-    queries = (q_ref[...] * scale).T
-    key_rows = k_ref[...].T
-    values = v_ref[...].T
+    queries = (queries * scale).T
+    key_rows = key_rows.T
+    values = values.T
     ones = jnp.ones((1, count), F32)
     query_extra = extra_rows([ones], count)
-    key_extra = extra_rows([mask_ref[...]], count)
-    outs = []
+    key_extra = extra_rows([mask], count)
+    outs, logs = [], []
     for side in range(2):
         part = slice(half * side, half * side + half)
-        if has_bias:
-            band = contract(band_ref[side], onehot, 1, 0).astype(BF)
+        if bias is not None:
+            bands, onehot = bias
+            band = contract(bands[side], onehot, 1, 0).astype(BF)
             left = jnp.concatenate([key_rows[part], onehot, key_extra], 0)
             right = jnp.concatenate([queries[part], band, query_extra], 0)
         else:
@@ -79,37 +78,38 @@
         output = contract(jnp.concatenate([values[part], query_extra], 0), weights, 1, 0)
         total = output[half : half + 1]
         outs.append(output[:half] * (1.0 / total))
-        lse_ref[0, side : side + 1, :] = top + jnp.log(total)
-    o_ref[...] = jnp.concatenate(outs, 0).astype(BF).T
-
-
-def backward_kernel(has_bias, scale, *refs):
-    if has_bias:
-        (q_ref, k_ref, v_ref, do_ref, o_ref, lse_ref, mask_ref, band_ref, onehot_ref, flipped_ref) = refs[:10]
-        dq_ref, dkv_ref, db_ref = refs[10:]
-        onehot = onehot_ref[...]
-        flipped = flipped_ref[...]
-    else:
-        q_ref, k_ref, v_ref, do_ref, o_ref, lse_ref, mask_ref = refs[:7]
-        dq_ref, dkv_ref = refs[7:]
-    count = q_ref.shape[0]
+        logs.append(top + jnp.log(total))
+    return jnp.concatenate(outs, 0).astype(BF).T, jnp.concatenate(logs, 0)
+
+
+def forward_kernel(has_bias, scale, *refs):
+    q_ref, k_ref, v_ref, mask_ref = refs[:4]
+    bias = (refs[4][...], refs[5][...]) if has_bias else None
+    o_ref, lse_ref = refs[-2:]
+    o_ref[...], lse_ref[0] = forward_pair(scale, q_ref[...], k_ref[...], v_ref[...], mask_ref[...], bias)
+
+
+def backward_pair(scale, queries, key_rows, values, grad_out, output, lse, mask, bias):
+    if bias is not None:
+        bands, onehot, flipped = bias
+    count = queries.shape[0]
     half = WIDE // 2
-    queries = (q_ref[...] * scale).T
-    key_rows = k_ref[...].T
-    values = v_ref[...].T
-    grad_out = do_ref[...].T
-    product = grad_out.astype(F32) * o_ref[...].T.astype(F32)
+    queries = (queries * scale).T
+    key_rows = key_rows.T
+    values = values.T
+    grad_out = grad_out.T
+    product = grad_out.astype(F32) * output.T.astype(F32)
     ones = jnp.ones((1, count), F32)
-    key_extra = extra_rows([ones, ones, ones, mask_ref[...]], count)
+    key_extra = extra_rows([ones, ones, ones, mask], count)
     value_extra = extra_rows([ones, ones, ones], count)
-    d_queries, d_keys, d_values = [], [], []
+    d_queries, d_keys, d_values, d_bands = [], [], [], []
     for side in range(2):
         part = slice(half * side, half * side + half)
-        lse_rows = extra_rows([*pieces(-lse_ref[0, side : side + 1, :]), ones], count)
+        lse_rows = extra_rows([*pieces(-lse[side : side + 1, :]), ones], count)
         delta = jnp.sum(product[part], axis=0, keepdims=True)
         delta_rows = extra_rows(list(pieces(-delta)), count)
-        if has_bias:
-            band = contract(band_ref[side], onehot, 1, 0).astype(BF)
+        if bias is not None:
+            band = contract(bands[side], onehot, 1, 0).astype(BF)
             left = jnp.concatenate([queries[part], band, lse_rows], 0)
             right = jnp.concatenate([key_rows[part], onehot, key_extra], 0)
         else:
@@ -126,15 +126,28 @@
         d_values.append(contract(grad_out[part], weights.astype(BF), 1, 0))
         d_keys.append(contract(queries[part], d_scores, 1, 0))
         scaled = key_rows[part] * scale
-        if has_bias:
-            both = contract(jnp.concatenate([scaled, onehot], 0), d_scores, 1, 1)
+        if bias is not None:
+            both = contract(jnp.concatenate([scaled, flipped], 0), d_scores, 1, 1)
             d_queries.append(both[:half])
-            db_ref[side] = contract(flipped, both[half:].astype(BF), 1, 1)
+            d_bands.append(contract(onehot, both[half:].astype(BF), 1, 1))
         else:
             d_queries.append(contract(scaled, d_scores, 1, 1))
-    dq_ref[...] = jnp.concatenate(d_queries, 0).astype(BF).T
-    dkv_ref[0] = jnp.concatenate(d_keys, 0).astype(BF).T
-    dkv_ref[1] = jnp.concatenate(d_values, 0).astype(BF).T
+    out = tuple(jnp.concatenate(each, 0).astype(BF).T for each in (d_queries, d_keys, d_values))
+    return out if bias is None else (*out, jnp.stack(d_bands))
+
+
+def backward_kernel(has_bias, scale, *refs):
+    q_ref, k_ref, v_ref, do_ref, o_ref, lse_ref, mask_ref = refs[:7]
+    bias = tuple(ref[...] for ref in refs[7:10]) if has_bias else None
+    outs = refs[10:] if has_bias else refs[7:]
+    grads = backward_pair(
+        scale, q_ref[...], k_ref[...], v_ref[...], do_ref[...], o_ref[...], lse_ref[0], mask_ref[...], bias
+    )
+    outs[0][...] = grads[0]
+    outs[1][0] = grads[1]
+    outs[1][1] = grads[2]
+    if has_bias:
+        outs[2][...] = grads[3]
 
 
 def column(first):
@@ -238,20 +251,20 @@
     shape = (WIDE, WIDE)
     keep = same_block(shape)
     for head in range(heads):
-        rolled = pltpu.roll(jnp.where(keep, grad_ref[head], 0.0), 0, 1, stride=1, stride_axis=0)
+        rolled = pltpu.roll(jnp.where(keep, grad_ref[head], 0.0), 1, 1, stride=1, stride_axis=0)
         table_ref[head : head + 1, :] = jnp.sum(rolled[:half], axis=0, keepdims=True)
         table_ref[heads + head : heads + head + 1, :] = jnp.sum(rolled[half:], axis=0, keepdims=True)
 
 
 def gather_bands(grads):
     heads = grads.shape[0]
-    flipped = pl.pallas_call(
+    table = pl.pallas_call(
         unband_kernel,
         out_shape=jax.ShapeDtypeStruct((2 * heads, WIDE), F32),
         compiler_params=params(),
         cost_estimate=cost(3),
     )(grads)
-    return flipped[:, ::-1].T
+    return table.T
 
 
 def gelu_pair(value):
@@ -381,14 +394,1165 @@
 
 def reduce_parts(send, keep):
     half = send.shape[0] // 2
-    arrived = swapped(send, "page", 1).astype(F32)
+    arrived = swapped(send, PAGE, 1).astype(F32)
     away = (arrived[half:] + keep[half:].astype(F32)).astype(BF)
     mine = arrived[:half] + keep[:half].astype(F32)
-    mine = mine + swapped(away, "page", 2).astype(F32)
+    mine = mine + swapped(away, PAGE, 2).astype(F32)
     total = mine[0]
     for step in range(1, half):
-        total = total + swapped(mine[step].astype(BF), "page", 4 * step).astype(F32)
+        total = total + swapped(mine[step].astype(BF), PAGE, 4 * step).astype(F32)
     return total
+
+
+def flip(position, mask):
+    out = position
+    bit = 1
+    while bit <= mask:
+        if mask & bit:
+            out = out + bit * (1 - 2 * lax.rem(lax.div(position, bit), 2))
+        bit *= 2
+    return out
+
+
+RING = 2
+STORES = 8
+FETCHES = 14
+LANDINGS = 3
+LINK_US = 6.7
+CORE_US = 2.6
+LATE_US = 30.0
+LATENCY_US = 2.0
+
+
+CORE, NEAR, FAR, JOIN, LAST, DONE, Y, Z = range(8)
+KV = 98
+WEIGHTS = (96, 97)
+
+
+class Flow:
+    def __init__(self, refs, me, side):
+        self.r = refs
+        self.me = me
+        self.side = side
+        self.now = 0.0
+        self.y_free = 0.0
+        self.z_free = 0.0
+        self.pending = []
+        self.near_done = {}
+        self.stores = []
+
+    def at(self, mask):
+        return {PAGE: flip(self.me, mask)}
+
+    def core_copy(self, unit):
+        r = self.r
+        return pltpu.make_async_remote_copy(
+            src_ref=r.ring.at[unit % RING],
+            dst_ref=r.core_in.at[unit % LANDINGS],
+            send_sem=r.core_sent.at[unit % RING],
+            recv_sem=r.core_got.at[unit % LANDINGS],
+            device_id=self.at(1),
+            device_id_type=pl.DeviceIdType.MESH,
+        )
+
+    def y_copy(self, unit):
+        r = self.r
+        source, landing = r.keep.at[unit, 1], r.y_in.at[Y_PLACES[unit]]
+        if unit in TURNED_UNITS:
+            source, landing = r.keep.at[unit, 1, 0], r.z_in.at[PLAIN_UNITS.index(unit), 2]
+        return pltpu.make_async_remote_copy(
+            src_ref=source,
+            dst_ref=landing,
+            send_sem=r.y_sent.at[0],
+            recv_sem=r.y_got.at[Y_PLACES[unit]],
+            device_id=self.at(2),
+            device_id_type=pl.DeviceIdType.MESH,
+        )
+
+    def z_place(self, unit):
+        if unit in PLAIN_UNITS:
+            return PLAIN_UNITS.index(unit)
+        return len(PLAIN_UNITS) + DOWN_STEPS[DOWN_UNITS.index(unit)] // 2
+
+    def near_copy(self, unit, arriving=False):
+        r = self.r
+        if unit in DOWN_UNITS:
+            step = DOWN_STEPS[DOWN_UNITS.index(unit)]
+            if (step & 1 == 1) == arriving:
+                return None
+            target = unit if arriving else DOWN_UNITS[DOWN_STEPS.index(step ^ 1)]
+            source, landing = r.keep.at[unit], r.near_down.at[step // 2]
+        elif unit in TURNED_UNITS:
+            target = unit
+            source = r.keep.at[unit, :, pl.ds(2, 2)]
+            landing = r.turned_in.at[TURNED_UNITS.index(unit)]
+        else:
+            target = unit
+            if unit in UP_UNITS and not arriving:
+                target = UP_UNITS[DOWN_STEPS.index(DOWN_STEPS[UP_UNITS.index(unit)] ^ 1)]
+            source = r.keep.at[unit, 0, pl.ds(2, 2)]
+            landing = r.z_in.at[PLAIN_UNITS.index(target), pl.ds(0, 2)]
+        return pltpu.make_async_remote_copy(
+            src_ref=source,
+            dst_ref=landing,
+            send_sem=r.near_sent.at[0],
+            recv_sem=r.near_got.at[self.z_place(target)],
+            device_id=self.at(4),
+            device_id_type=pl.DeviceIdType.MESH,
+        )
+
+    def far_copy(self, unit, arriving=False):
+        r = self.r
+        if unit in DOWN_UNITS:
+            step = DOWN_STEPS[DOWN_UNITS.index(unit)]
+            if step != (0 if arriving else 2):
+                return None
+            target = DOWN_UNITS[DOWN_STEPS.index(0)]
+            source, landing = r.keep.at[unit, 0], r.far_down
+        elif unit in TURNED_UNITS:
+            target = unit
+            source, landing = r.keep.at[unit, :, 1], r.z_in.at[PLAIN_UNITS.index(unit), pl.ds(0, 2)]
+        else:
+            target = unit
+            if unit in UP_UNITS and not arriving:
+                target = UP_UNITS[DOWN_STEPS.index(DOWN_STEPS[UP_UNITS.index(unit)] ^ 2)]
+            source, landing = r.keep.at[unit, 0, 1], r.z_in.at[PLAIN_UNITS.index(target), 2]
+        return pltpu.make_async_remote_copy(
+            src_ref=source,
+            dst_ref=landing,
+            send_sem=r.far_sent.at[0],
+            recv_sem=r.far_got.at[self.z_place(target)],
+            device_id=self.at(8),
+            device_id_type=pl.DeviceIdType.MESH,
+        )
+
+    def produce(self, unit, left, *rights):
+        r = self.r
+        first = 0
+        for right in rights:
+            last = first + right.shape[1]
+            r.sums[:, first:last] = contract(left, right, 0, 0).astype(BF)
+            first = last
+        self.tick(1.2)
+        if unit >= RING:
+            self.core_copy(unit - RING).wait_send()
+        core = lax.rem(self.me, 2)
+        y = lax.rem(lax.div(self.me, 2), 2)
+        z = lax.div(self.me, 4)
+        for rel_y in range(2):
+            for rel_z in range(4):
+                y_at = flip(y, rel_y)
+                if unit in DOWN_UNITS:
+                    first = y_at * 8 * ROWS
+                    mine = first + core * 4 * ROWS + rel_z * ROWS
+                    other = first + (1 - core) * 4 * ROWS + rel_z * ROWS
+                else:
+                    first = flip(z, rel_z) * 4 * ROWS + y_at * 2 * ROWS
+                    mine = first + core * ROWS
+                    other = first + (1 - core) * ROWS
+                slot = rel_y * 4 + (rel_z if unit in DOWN_UNITS else SLOT_OF[rel_z])
+                r.ring[unit % RING, rel_y, slot - 4 * rel_y] = r.sums[pl.ds(pl.multiple_of(other, 16), ROWS), :]
+                r.keep[unit, rel_y, slot - 4 * rel_y] = r.sums[pl.ds(pl.multiple_of(mine, 16), ROWS), :]
+        if unit >= LANDINGS:
+            pl.semaphore_wait(r.credit.at[unit - LANDINGS], 1)
+        self.core_copy(unit).start()
+        self.now += 0.5
+        self.pending.append([unit, CORE, self.now + CORE_US])
+
+    def advance(self, entry):
+        self.plan(entry)()
+
+    def z_busy(self, us):
+        self.z_free = max(self.now, self.z_free) + us
+        return self.z_free + LATENCY_US
+
+    def y_busy(self, us):
+        self.y_free = max(self.now, self.y_free) + us
+        return self.y_free + 0.3
+
+    def plan(self, entry):
+        unit, stage, _ = entry
+        step = None
+        if unit in WEIGHTS:
+            if stage < 3:
+                entry[1:] = [stage + 1, self.now + (3.8, 8.0, 2.5)[stage]]
+            else:
+                entry[1] = DONE
+            return functools.partial(self.run, unit, stage)
+        if unit in DOWN_UNITS:
+            step = DOWN_STEPS[DOWN_UNITS.index(unit)]
+        if unit == KV:
+            entry[1] = DONE
+        elif unit == SMALL:
+            free = max(self.now, self.y_free if stage == CORE else self.z_free)
+            following = {CORE: Y, Y: Z, Z: DONE}[stage]
+            entry[1:] = [following, free + (2.0 if stage == CORE else 6.0)]
+        elif unit in TURNED_UNITS and stage != DONE:
+            if stage == CORE:
+                entry[1:] = [NEAR, self.z_busy(LINK_US)]
+            elif stage == NEAR:
+                entry[1:] = [FAR, self.z_busy(LINK_US)]
+            elif stage == FAR:
+                entry[1:] = [LAST, self.y_busy(LINK_US / 4) + LATE_US]
+            else:
+                entry[1] = DONE
+        elif stage == CORE:
+            if step is not None and step & 1:
+                self.near_done[step ^ 1] = self.z_busy(2 * LINK_US)
+                entry[1] = DONE
+            elif step is not None:
+                entry[1:] = [JOIN, self.near_done[step]]
+            else:
+                entry[1:] = [Y, self.y_busy(LINK_US)]
+        elif stage == JOIN:
+            entry[1:] = [Y, self.y_busy(LINK_US)]
+        elif stage == Y:
+            if step is not None:
+                done = self.z_busy(2 * LINK_US) if step == 2 else self.z_free + LATE_US
+                entry[1:] = [DONE, 0.0] if step == 2 else [FAR, done + LATE_US]
+            else:
+                entry[1:] = [NEAR, self.z_busy(LINK_US / 2)]
+                if unit in UP_UNITS:
+                    self.meet(entry, [unit, UP_UNITS[DOWN_STEPS.index(DOWN_STEPS[UP_UNITS.index(unit)] ^ 1)]])
+        elif stage == NEAR:
+            entry[1:] = [FAR, self.z_busy(LINK_US / 2) + (8.0 if unit in KV_UNITS else LATE_US)]
+            if unit in UP_UNITS:
+                self.meet(entry, UP_UNITS)
+        else:
+            entry[1] = DONE
+            if unit == KV_UNITS[1]:
+                self.pending.append([KV, CORE, self.now + LATE_US])
+        return functools.partial(self.run, unit, stage)
+
+    def meet(self, entry, units):
+        due, entry[2] = entry[2], float("inf")
+        waiting = [e for e in self.pending if e[0] in units and e[1] == entry[1]]
+        if len(waiting) == len(units):
+            for other in waiting:
+                other[2] = due
+
+    def join(self, unit, half, places, arrived):
+        r = self.r
+        for place in places:
+            total = r.keep[unit, half, place].astype(F32) + arrived[place].astype(F32)
+            r.keep[unit, half, place] = total.astype(BF)
+
+    def run(self, unit, stage):
+        r = self.r
+        if unit in WEIGHTS:
+            self.weight_arrival(WEIGHTS.index(unit), stage).wait_recv()
+            if stage < 3:
+                self.weight_copy(WEIGHTS.index(unit), stage + 1).start()
+            return
+        if unit == KV:
+            self.kv_copy().wait_recv()
+            self.store(KV)
+            return
+        if unit == SMALL:
+            self.run_small((CORE, Y, Z).index(stage))
+            return
+        step = None
+        if unit in DOWN_UNITS:
+            step = DOWN_STEPS[DOWN_UNITS.index(unit)]
+        turned = unit in TURNED_UNITS
+        if stage == CORE:
+            self.core_copy(unit).wait_recv()
+            arrived = r.core_in.at[unit % LANDINGS]
+            self.join(unit, 1, (0, 1, 2, 3), arrived.at[1])
+            if step is None and not turned:
+                self.y_copy(unit).start()
+            self.join(unit, 0, (0, 1, 2, 3), arrived.at[0])
+            if turned or (step is not None and step & 1):
+                self.near_copy(unit).start()
+            if unit < UNITS - LANDINGS:
+                pl.semaphore_signal(
+                    r.credit.at[unit], 1, device_id=self.at(1), device_id_type=pl.DeviceIdType.MESH
+                )
+        elif stage == JOIN:
+            self.near_copy(unit, arriving=True).wait_recv()
+            arrived = r.near_down.at[step // 2]
+            self.join(unit, 1, (0, 1, 2, 3), arrived.at[1])
+            self.y_copy(unit).start()
+            self.join(unit, 0, (0, 1, 2, 3), arrived.at[0])
+        elif stage == Y:
+            self.y_copy(unit).wait_recv()
+            self.join(unit, 0, (2, 3, 0, 1), r.y_in.at[Y_PLACES[unit]])
+            if step is None:
+                self.near_copy(unit).start()
+            elif step == 2:
+                self.far_copy(unit).start()
+        elif stage == NEAR:
+            self.near_copy(unit, arriving=True).wait_recv()
+            if turned:
+                arrived = r.turned_in.at[TURNED_UNITS.index(unit)]
+                for half in (0, 1):
+                    self.join(unit, half, (1, 0), arrived.at[half])
+            else:
+                self.join(unit, 0, (1, 0), r.z_in.at[PLAIN_UNITS.index(unit)])
+            self.far_copy(unit).start()
+        elif turned and stage == FAR:
+            self.far_copy(unit, arriving=True).wait_recv()
+            arrived = r.z_in.at[PLAIN_UNITS.index(unit)]
+            for half in (1, 0):
+                total = r.keep[unit, half, 0].astype(F32) + arrived[half].astype(F32)
+                r.keep[unit, half, 0] = total.astype(BF)
+                if half:
+                    self.y_copy(unit).start()
+        elif turned:
+            self.y_copy(unit).wait_recv()
+            self.finish(unit)
+        else:
+            self.far_copy(unit, arriving=True).wait_recv()
+            self.finish(unit)
+
+    def small_copies(self, stage):
+        r = self.r
+        return [
+            pltpu.make_async_remote_copy(
+                src_ref=r.small_in.at[5 + stage],
+                dst_ref=r.small_in.at[place],
+                send_sem=r.small_sent.at[0],
+                recv_sem=r.small_got.at[place],
+                device_id=self.at(mask),
+                device_id_type=pl.DeviceIdType.MESH,
+            )
+            for place, mask in SMALL_STEPS[stage]
+        ]
+
+    def kv_copy(self):
+        r = self.r
+        return pltpu.make_async_remote_copy(
+            src_ref=r.kv_out,
+            dst_ref=r.kv_in,
+            send_sem=r.kv_sent.at[0],
+            recv_sem=r.kv_got.at[0],
+            device_id={STREAM: 1 - self.side},
+            device_id_type=pl.DeviceIdType.MESH,
+        )
+
+    def weight_copy(self, half, stage):
+        r = self.r
+        core, y, z = lax.rem(self.me, 2), lax.rem(lax.div(self.me, 2), 2), lax.rem(lax.div(self.me, 4), 2)
+        share = r.other_w.shape[-2]
+        target, device = r.other_w.at[half, z, y, core], {STREAM: 1 - self.side}
+        source = target
+        if stage == 0:
+            first = pl.multiple_of((z * 4 + y * 2 + core) * share, 16)
+            source = r.w_ckv.at[pl.ds(first, share), half * WIDTH : (half + 1) * WIDTH]
+        elif stage == 1:
+            device = self.at(4)
+        elif stage == 2:
+            source = target = r.other_w.at[half, :, y, core]
+            device = self.at(2)
+        else:
+            source = target = r.other_w.at[half, :, :, core]
+            device = self.at(1)
+        return pltpu.make_async_remote_copy(
+            src_ref=source,
+            dst_ref=target,
+            send_sem=r.weight_sent.at[0],
+            recv_sem=r.weight_got.at[half, stage],
+            device_id=device,
+            device_id_type=pl.DeviceIdType.MESH,
+        )
+
+    def weight_arrival(self, half, stage):
+        r = self.r
+        core, y, z = lax.rem(self.me, 2), lax.rem(lax.div(self.me, 2), 2), lax.rem(lax.div(self.me, 4), 2)
+        target = (
+            r.other_w.at[half, z, y, core],
+            r.other_w.at[half, 1 - z, y, core],
+            r.other_w.at[half, :, 1 - y, core],
+            r.other_w.at[half, :, :, 1 - core],
+        )[stage]
+        return pltpu.make_async_remote_copy(
+            src_ref=target,
+            dst_ref=target,
+            send_sem=r.weight_sent.at[0],
+            recv_sem=r.weight_got.at[half, stage],
+            device_id=self.at(1),
+            device_id_type=pl.DeviceIdType.MESH,
+        )
+
+    def start_weights(self):
+        for half in range(2):
+            self.weight_copy(half, 0).start()
+            self.pending.append([WEIGHTS[half], 0, self.now + 4.0 + 3.0 * half])
+
+    def finish_weights(self):
+        while True:
+            left = [e for e in self.pending if e[0] in WEIGHTS]
+            if not left:
+                return
+            entry = min(left, key=lambda e: e[2])
+            self.now = max(self.now, entry[2])
+            self.advance(entry)
+            self.pending = [e for e in self.pending if e[1] != DONE]
+
+    def start_small(self):
+        r = self.r
+        r.small_in[5] = r.small_sum[...]
+        for copy in self.small_copies(0):
+            copy.start()
+        self.pending.append([SMALL, CORE, self.now + CORE_US + 1.0])
+
+    def run_small(self, stage):
+        r = self.r
+        for copy in self.small_copies(stage):
+            copy.wait_recv()
+        for place, _ in SMALL_STEPS[stage]:
+            r.small_sum[...] += r.small_in[place]
+        if stage < 2:
+            r.small_in[6 + stage] = r.small_sum[...]
+            for copy in self.small_copies(stage + 1):
+                copy.start()
+
+    def due(self):
+        while True:
+            ready = [e for e in self.pending if e[2] <= self.now]
+            if not ready:
+                return
+            entry = min(ready, key=lambda e: e[2])
+            yield entry
+            self.pending = [e for e in self.pending if e[1] != DONE]
+
+    def tick(self, us):
+        self.now += us
+        for entry in self.due():
+            self.advance(entry)
+
+    def drain(self):
+        while self.pending:
+            self.now = max(self.now, min(e[2] for e in self.pending))
+            for entry in self.due():
+                self.advance(entry)
+        for unit in range(UNITS - RING, UNITS):
+            self.core_copy(unit).wait_send()
+        r = self.r
+        for whole, sent in (
+            (r.y_in, r.y_sent),
+            (r.keep.at[pl.ds(0, 5)], r.near_sent),
+            (r.keep.at[pl.ds(0, 2)], r.far_sent),
+            (r.small_in.at[pl.ds(0, 5)], r.small_sent),
+            (r.other_w, r.weight_sent),
+            (r.s.at[Slot.normed], r.normed_sent),
+        ):
+            pltpu.make_async_copy(whole, whole, sent.at[0]).wait()
+        self.kv_copy().wait_send()
+        for place in range(max(0, len(self.stores) - STORES), len(self.stores)):
+            self.store_copy(place).wait()
+
+    def store_copy(self, place):
+        r = self.r
+        unit, part = self.stores[place]
+        if unit == KV:
+            pairs = [(r.kv_in, r.ckv_out)]
+        elif unit in DOWN_UNITS:
+            pairs = [(r.done.at[pl.ds(0, 4)], r.down_out)]
+        elif unit in UP_UNITS:
+            tile = flip(lax.div(self.me, 4), DOWN_STEPS[UP_UNITS.index(unit)])
+            columns = pl.ds(pl.multiple_of(tile * WIDTH, WIDE), WIDTH)
+            pairs = [(r.done.at[self.done_at(unit)], r.up_out.at[:, columns])]
+        elif unit in THIRD_UNITS:
+            third = WIDTH // 3
+            first = third * THIRD_UNITS.index(unit)
+            source = r.done.at[self.done_at(unit)]
+            pairs = [
+                (source.at[:, pl.ds(i * third, third)], r.qkv_out.at[:, pl.ds(i * WIDTH + first, third)])
+                for i in range(3)
+            ]
+        else:
+            pairs = [(r.done.at[self.done_at(unit)], {8: r.cout_out, 11: r.cq_out, 12: r.out_out}[unit])]
+        return pltpu.make_async_copy(*pairs[part], r.stored_sums.at[place % STORES])
+
+    def done_at(self, unit):
+        return 4 + PLAIN_UNITS.index(unit)
+
+    def store(self, unit):
+        for part in range(3 if unit in THIRD_UNITS else 1):
+            place = len(self.stores)
+            if place >= STORES:
+                self.store_copy(place - STORES).wait()
+            self.stores.append((unit, part))
+            self.store_copy(place).start()
+
+    def finish(self, unit):
+        r = self.r
+        if unit in DOWN_UNITS:
+            r.done[0:4] = r.keep[unit, 0].astype(F32) + r.far_down[...].astype(F32)
+            self.store(unit)
+            return
+        total = r.keep[unit, 0, 0].astype(F32) + r.z_in[PLAIN_UNITS.index(unit), 2].astype(F32)
+        if unit in KV_UNITS:
+            half = KV_UNITS.index(unit)
+            r.kv_out[:, half * WIDTH : (half + 1) * WIDTH] = total
+            if half:
+                self.kv_copy().start()
+            return
+        r.done[self.done_at(unit)] = total
+        self.store(unit)
+
+
+WIDTH = 768
+ROWS = 48
+DOWN_UNITS = (1, 3, 5, 7)
+TURNED_UNITS = ()
+UP_UNITS = (0, 2, 4, 6)
+DOWN_STEPS = (1, 3, 2, 0)
+SLOT_OF = (0, 2, 1, 3)
+PLAIN_UNITS = (0, 2, 4, 6, 8, 9, 10, 11, 12, 13, 14, 15)
+UNITS = 16
+Y_PLACES = {unit: at for at, unit in enumerate((0, 2, 4, 5, 6, 7, 8, 9, 10, 11, 12, 13, 14, 15))}
+KV_UNITS = (9, 10)
+THIRD_UNITS = (13, 14, 15)
+
+
+class Fetch:
+    def __init__(self, source, target, semaphores, free):
+        self.free = free
+        self.place = free.pop(0)
+        self.copy = pltpu.make_async_copy(source, target, semaphores.at[self.place])
+        self.copy.start()
+
+    def wait(self):
+        self.copy.wait()
+        self.free.append(self.place)
+
+
+class Refs(NamedTuple):
+    states: Any
+    cotangent: Any
+    w_qkv: Any
+    w_out: Any
+    w_cq: Any
+    w_ckv: Any
+    w_cout: Any
+    w_up: Any
+    w_down: Any
+    counts: Any
+    box_x: Any
+    box_y: Any
+    gain1: Any
+    gain2: Any
+    table_in: Any
+    result_out: Any
+    states_out: Any
+    held_out: Any
+    down_out: Any
+    up_out: Any
+    cout_out: Any
+    cq_out: Any
+    out_out: Any
+    qkv_out: Any
+    ckv_out: Any
+    gain1_out: Any
+    gain2_out: Any
+    table_out: Any
+    s: Any
+    f: Any
+    w: Any
+    fetched: Any
+    stored: Any
+    sums: Any
+    keep: Any
+    ring: Any
+    core_in: Any
+    y_in: Any
+    z_in: Any
+    near_down: Any
+    far_down: Any
+    turned_in: Any
+    core_sent: Any
+    core_got: Any
+    y_sent: Any
+    y_got: Any
+    near_sent: Any
+    near_got: Any
+    far_sent: Any
+    far_got: Any
+    credit: Any
+    normed_sent: Any
+    normed_got: Any
+    back_sent: Any
+    back_got: Any
+    weight_sent: Any
+    weight_got: Any
+    other_w: Any
+    done: Any
+    stored_sums: Any
+    kv_out: Any
+    kv_in: Any
+    kv_sent: Any
+    kv_got: Any
+    self_lse: Any
+    cross_lse: Any
+    bands: Any
+    onehot: Any
+    flipped: Any
+    small_sum: Any
+    table: Any
+    gain_sums: Any
+    table_sum: Any
+    small_in: Any
+    small_sent: Any
+    small_got: Any
+    d_bands: Any
+
+
+INPUTS, SMALL_INPUTS, OUTPUTS, KEPT_OUTPUTS = 9, 6, 13, 0
+
+
+def layer_kernel(scale, *refs):
+    r = Refs(*refs)
+    me = lax.axis_index(PAGE)
+    side = lax.axis_index(STREAM)
+    flow = Flow(r, me, side)
+    count, width = r.states.shape
+    pairs = width // WIDE
+    half_rows = count // 2
+    core, y, z = lax.rem(me, 2), lax.rem(lax.div(me, 2), 2), lax.div(me, 4)
+    partner = {STREAM: 1 - side}
+
+    free = list(range(FETCHES))
+
+    def fetch(source, target):
+        return Fetch(source, target, r.fetched, free)
+
+    def slot(name):
+        return r.s.at[name]
+
+    def tile_of(step):
+        return pl.ds(pl.multiple_of(flip(z, DOWN_STEPS[step]) * width, WIDE), width)
+
+    def columns(ref, first):
+        return ref.at[:, width * first : width * (first + 1)]
+
+    got_states = fetch(r.states, slot(Slot.second))
+    got_q, got_k, got_v = [fetch(columns(r.w_qkv, i), r.w.at[i]) for i in range(3)]
+    got_out = fetch(r.w_out, r.w.at[3])
+    got_cq = fetch(r.w_cq, r.w.at[4])
+    got_grad = fetch(r.cotangent, slot(Slot.low_grad))
+
+    barrier = pltpu.get_barrier_semaphore()
+    others = [{PAGE: flip(me, mask)} for mask in (1, 2, 4, 8, 12)] + [partner]
+    for other in others:
+        pl.semaphore_signal(barrier, 1, device_id=other, device_id_type=pl.DeviceIdType.MESH)
+
+    own_count, other_count = r.counts[side], r.counts[1 - side]
+    slots_row = lax.broadcasted_iota(jnp.int32, (1, count), 1)
+    mask_own = jnp.where(slots_row < own_count, 0.0, MASKED).astype(F32)
+    mask_other = jnp.where(slots_row < other_count, 0.0, MASKED).astype(F32)
+    slots_column = lax.broadcasted_iota(jnp.int32, (count, 1), 0)
+    valid = jnp.where(slots_column < own_count, 1.0, 0.0).astype(F32)
+    buckets = WIDE // 2
+    small = own_count <= GRID_SMALL * GRID_SMALL
+    tall = [jnp.floor((slots_row.astype(F32) + 0.5) * (1.0 / grid)).astype(jnp.int32) for grid in (GRID_SMALL, GRID_LARGE)]
+    grid_top = jnp.where(small, tall[0], tall[1])
+    grid_left = slots_row - jnp.where(small, tall[0] * GRID_SMALL, tall[1] * GRID_LARGE)
+    left = jnp.where(side == 0, r.box_x[...], grid_left)
+    top = jnp.where(side == 0, r.box_y[...], grid_top)
+    index = lax.broadcasted_iota(jnp.int32, (buckets, count), 0)
+
+    def marks(first, second):
+        both = [jnp.where(index == first, 1.0, 0.0), jnp.where(index == second, 1.0, 0.0)]
+        return jnp.concatenate(both, 0).astype(BF)
+
+    r.onehot[...] = marks(left, top)
+    r.flipped[...] = marks(buckets - 1 - left, buckets - 1 - top)
+    keep = same_block((WIDE, WIDE))
+    lower = lax.broadcasted_iota(jnp.int32, (WIDE, WIDE), 0) >= buckets
+    heads = 2 * pairs
+    for head in range(heads):
+        across = jnp.broadcast_to(r.table_in[head : head + 1, :], (WIDE, WIDE))
+        down = jnp.broadcast_to(r.table_in[heads + head : heads + head + 1, :], (WIDE, WIDE))
+        rolled = pltpu.roll(jnp.where(lower, down, across), buckets, 1, stride=1, stride_axis=0)
+        r.bands[head // 2, head % 2] = jnp.where(keep, rolled, 0.0).astype(BF)
+
+    def normed_copy(part):
+        rows = pl.ds(part * half_rows, half_rows)
+        return pltpu.make_async_remote_copy(
+            src_ref=slot(Slot.normed).at[rows],
+            dst_ref=slot(Slot.other).at[rows],
+            send_sem=r.normed_sent.at[0],
+            recv_sem=r.normed_got.at[part],
+            device_id=partner,
+            device_id_type=pl.DeviceIdType.MESH,
+        )
+
+    got_states.wait()
+    for part in range(2):
+        rows = slice(part * half_rows, (part + 1) * half_rows)
+        inputs = r.s[Slot.second, rows, :].astype(F32)
+        r.f[2, rows, :] = inputs
+        r.s[Slot.normed, rows, :] = norm_rows(inputs, r.gain1[...]).astype(BF)
+    pl.semaphore_wait(barrier, len(others))
+
+    flow.start_weights()
+    for part in range(2):
+        normed_copy(part).start()
+    flow.tick(0.1)
+    for name, copy, at in ((Slot.query, got_q, 0), (Slot.key, got_k, 1), (Slot.value, got_v, 2)):
+        copy.wait()
+        slot(name)[...] = contract(slot(Slot.normed)[...], r.w[at], 1, 0).astype(BF)
+        flow.tick(1.0)
+    held = [pltpu.make_async_copy(slot(name), r.held_out.at[i], r.stored.at[2 + i]) for i, name in enumerate((Slot.query, Slot.key, Slot.value))]
+    for copy in held:
+        copy.start()
+    got_cout = fetch(r.w_cout, r.w.at[0])
+    got_down = [fetch(r.w_down.at[tile_of(step)], r.w.at[1 + step]) for step in range(2)]
+
+    def pair_loop(us, step, first=0, last=pairs):
+        events = []
+        for pair in range(first, last):
+            flow.now += us
+            events.append([])
+            for entry in flow.due():
+                events[-1].append(flow.plan(entry))
+
+        @pl.loop(first, last)
+        def _(pair):
+            step(pair)
+            for place, steps in enumerate(events, first):
+                if steps:
+
+                    @pl.when(pair == place)
+                    def _(steps=steps):
+                        for run in steps:
+                            run()
+
+    def lanes_of(pair):
+        return pl.ds(pl.multiple_of(pair * WIDE, WIDE), WIDE)
+
+    def self_forward(pair):
+        lanes = lanes_of(pair)
+        output, lse = forward_pair(
+            scale,
+            r.s[Slot.query, :, lanes],
+            r.s[Slot.key, :, lanes],
+            r.s[Slot.value, :, lanes],
+            mask_own,
+            (r.bands[pair], r.onehot[...]),
+        )
+        r.s[Slot.attended, :, lanes] = output
+        r.self_lse[pair] = lse
+
+    pair_loop(1.95, self_forward)
+
+    got_out.wait()
+    r.f[2] = r.f[2] + contract(slot(Slot.attended)[...], r.w[3], 1, 0)
+    slot(Slot.low_middle)[...] = r.f[2].astype(BF)
+    got_down.append(fetch(r.w_down.at[tile_of(2)], r.w.at[3]))
+    got_cq.wait()
+    slot(Slot.cross_query)[...] = contract(slot(Slot.low_middle)[...], r.w[4], 1, 0).astype(BF)
+    got_down.append(fetch(r.w_down.at[tile_of(3)], r.w.at[4]))
+    flow.tick(2.2)
+    got_grad.wait()
+    slot(Slot.low_grad)[...] = (slot(Slot.low_grad)[...].astype(F32) * valid).astype(BF)
+    flow.tick(0.5)
+
+    back_slots = (Slot.back0, Slot.back1, Slot.back2, Slot.back3)
+    hidden_slots = (Slot.query, Slot.key, Slot.value, Slot.hidden3)
+    got_up = []
+    for step in range(4):
+        got_down[step].wait()
+        r.s[back_slots[step]] = contract(slot(Slot.low_grad)[...], r.w[1 + step], 1, 1).astype(BF)
+        got_up.append(fetch(r.w_up.at[:, tile_of(step)], r.w.at[1 + step]))
+        flow.tick(1.05)
+    flow.finish_weights()
+    for copy in held:
+        copy.wait()
+    for part in range(2):
+        normed_copy(part).wait_recv()
+    flow.now = max(flow.now, 30.0)
+    for at, name in enumerate((Slot.cross_key, Slot.cross_value)):
+        slot(name)[...] = contract(slot(Slot.other)[...], r.other_w[at].reshape(width, width), 1, 0).astype(BF)
+    flow.tick(2.0)
+
+    def cross_forward(pair):
+        lanes = lanes_of(pair)
+        output, lse = forward_pair(
+            scale,
+            r.s[Slot.cross_query, :, lanes],
+            r.s[Slot.cross_key, :, lanes],
+            r.s[Slot.cross_value, :, lanes],
+            mask_other,
+            None,
+        )
+        r.s[Slot.crossed, :, lanes] = output
+        r.cross_lse[pair] = lse
+
+    pair_loop(1.8, cross_forward)
+    got_cout.wait()
+    r.f[2] = r.f[2] + contract(slot(Slot.crossed)[...], r.w[0], 1, 0)
+    for part in range(2):
+        rows = slice(part * half_rows, (part + 1) * half_rows)
+        r.s[Slot.second, rows, :] = norm_rows(r.f[2, rows, :], r.gain2[...]).astype(BF)
+    flow.tick(2.0)
+
+    second_at, grad_at = Slot.second, Slot.low_grad
+    for step in range(4):
+        hidden_at, d_up_at, up_at = hidden_slots[step], back_slots[step], 1 + step
+        got_up[step].wait()
+
+        @pl.loop(0, 2)
+        def _(part, hidden_at=hidden_at, d_up_at=d_up_at, up_at=up_at):
+            rows = pl.ds(pl.multiple_of(part * half_rows, 16), half_rows)
+            hidden, slope = gelu_pair(contract(r.s[second_at, rows, :], r.w[up_at], 1, 0))
+            r.s[hidden_at, rows, :] = hidden.astype(BF)
+            r.s[d_up_at, rows, :] = (slope * r.s[d_up_at, rows, :].astype(F32)).astype(BF)
+
+        flow.tick(2.0)
+        flow.produce(UP_UNITS[step], r.s[second_at], r.s[d_up_at])
+        flow.tick(0.1)
+        flow.produce(DOWN_UNITS[step], r.s[hidden_at], r.s[grad_at])
+        flow.tick(0.1)
+        back = contract(r.s[d_up_at], r.w[up_at], 1, 1)
+        r.f[0] = back if step == 0 else r.f[0] + back
+        flow.tick(1.2)
+    got_cq, got_out = fetch(r.w_cq, r.w.at[1]), fetch(r.w_out, r.w.at[2])
+    got_q, got_k = [fetch(columns(r.w_qkv, i), r.w.at[3 + i]) for i in range(2)]
+
+    low_after_at, d_crossed_at = Slot.back0, Slot.second
+    r.small_sum[6:12, :] = fold(norm_back(r.f.at[2], r.f, 0, r.gain2, r.s, grad_at, low_after_at))
+    flow.tick(1.7)
+    r.s[d_crossed_at] = contract(r.s[low_after_at], r.w[0], 1, 1).astype(BF)
+    got_v = fetch(columns(r.w_qkv, 2), r.w.at[0])
+    flow.tick(1.1)
+    flow.produce(8, slot(Slot.crossed)[...], r.s[low_after_at])
+    flow.tick(0.1)
+
+    d_query_at, d_key_at, d_value_at = Slot.back1, Slot.low_grad, Slot.d_value
+
+    def cross_backward(pair):
+        lanes = lanes_of(pair)
+        d_query, d_key, d_value = backward_pair(
+            scale,
+            r.s[Slot.cross_query, :, lanes],
+            r.s[Slot.cross_key, :, lanes],
+            r.s[Slot.cross_value, :, lanes],
+            r.s[d_crossed_at, :, lanes],
+            r.s[Slot.crossed, :, lanes],
+            r.cross_lse[pair],
+            mask_other,
+            None,
+        )
+        r.s[d_query_at, :, lanes] = d_query
+        r.s[d_key_at, :, lanes] = d_key
+        r.s[d_value_at, :, lanes] = d_value
+
+    pair_loop(2.45, cross_backward)
+
+    flow.produce(9, slot(Slot.other)[...], r.s[d_key_at])
+    flow.tick(0.1)
+    flow.produce(10, slot(Slot.other)[...], r.s[d_value_at])
+    back_at = Slot.crossed
+    r.s[back_at] = (
+        contract(r.s[d_key_at], r.other_w[0].reshape(width, width), 1, 1)
+        + contract(r.s[d_value_at], r.other_w[1].reshape(width, width), 1, 1)
+    ).astype(BF)
+    back_copy = pltpu.make_async_remote_copy(
+        src_ref=r.s.at[back_at],
+        dst_ref=slot(Slot.returned),
+        send_sem=r.back_sent.at[0],
+        recv_sem=r.back_got.at[0],
+        device_id=partner,
+        device_id_type=pl.DeviceIdType.MESH,
+    )
+    back_copy.start()
+    flow.tick(2.0)
+    got_states = fetch(r.states, r.s.at[d_key_at])
+
+    query_at, key_at, value_at = Slot.back3, Slot.back0, Slot.d_value
+    got_held = [fetch(r.held_out.at[i], r.s.at[at]) for i, at in enumerate((query_at, key_at, value_at))]
+
+    flow.produce(11, slot(Slot.low_middle)[...], r.s[d_query_at])
+    got_cq.wait()
+    r.f[0] = r.f[0] + contract(r.s[d_query_at], r.w[1], 1, 1)
+    d_middle_at, d_attended_at = Slot.cross_key, Slot.cross_value
+    r.s[d_middle_at] = r.f[0].astype(BF)
+    flow.tick(1.5)
+    flow.produce(12, slot(Slot.attended)[...], r.s[d_middle_at])
+    got_out.wait()
+    r.s[d_attended_at] = contract(r.s[d_middle_at], r.w[2], 1, 1).astype(BF)
+    got_down = [fetch(r.w_down.at[tile_of(step)], r.w.at[1 + step]) for step in range(2)]
+    flow.tick(1.2)
+
+    dq_at, dk_at, dv_at = Slot.cross_query, Slot.back2, Slot.second
+    for copy in got_held:
+        copy.wait()
+
+    def self_backward(pair):
+        lanes = lanes_of(pair)
+        d_query, d_key, d_value, d_bands = backward_pair(
+            scale,
+            r.s[query_at, :, lanes],
+            r.s[key_at, :, lanes],
+            r.s[value_at, :, lanes],
+            r.s[d_attended_at, :, lanes],
+            r.s[Slot.attended, :, lanes],
+            r.self_lse[pair],
+            mask_own,
+            (r.bands[pair], r.onehot[...], r.flipped[...]),
+        )
+        r.s[dq_at, :, lanes] = d_query
+        r.s[dk_at, :, lanes] = d_key
+        r.s[dv_at, :, lanes] = d_value
+        r.d_bands[pair] = d_bands
+
+    third = width // 3
+    normed_at = Slot.normed
+    for part in range(3):
+        pair_loop(3.2, self_backward, part * pairs // 3, (part + 1) * pairs // 3)
+        wanted = slice(part * third, (part + 1) * third)
+        flow.produce(13 + part, r.s[normed_at], r.s[dq_at, :, wanted], r.s[dk_at, :, wanted], r.s[dv_at, :, wanted])
+    for copy in (got_q, got_k, got_v):
+        copy.wait()
+    r.f[1] = (
+        contract(r.s[dq_at], r.w[3], 1, 1)
+        + contract(r.s[dk_at], r.w[4], 1, 1)
+        + contract(r.s[dv_at], r.w[0], 1, 1)
+    )
+    got_down += [fetch(r.w_down.at[tile_of(step)], r.w.at[1 + step]) for step in range(2, 4)]
+    flow.tick(3.2)
+    for head in range(heads):
+        across, down = unband(r.d_bands[head // 2, head % 2])
+        r.small_sum[16 + head : 17 + head, :] = across
+        r.small_sum[16 + heads + head : 17 + heads + head, :] = down
+    flow.tick(1.0)
+    got_states.wait()
+    back_copy.wait_recv()
+    for part in range(2):
+        rows = slice(part * half_rows, (part + 1) * half_rows)
+        r.f[1, rows, :] += r.s[Slot.returned, rows, :].astype(F32)
+    gain1_grad = norm_back(r.s.at[d_key_at], r.f, 1, r.gain1, None, None, None)
+    sent_states = pltpu.make_async_copy(r.f.at[0], r.states_out, r.stored.at[1])
+    sent_states.start()
+    r.small_sum[0:6, :] = fold(gain1_grad)
+    r.small_sum[12:16, :] = jnp.zeros((4, WIDE), F32)
+    flow.tick(2.0)
+
+    flow.start_small()
+    flow.tick(0.2)
+
+    result_at = Slot.back3
+    for step in range(4):
+        got_down[step].wait()
+        r.f[2] = r.f[2] + contract(r.s[hidden_slots[step]], r.w[1 + step], 1, 0)
+        flow.tick(1.3)
+    r.s[result_at] = (r.f[2] * valid).astype(BF)
+    sent_result = pltpu.make_async_copy(r.s.at[result_at], r.result_out, r.stored.at[0])
+    sent_result.start()
+    flow.tick(0.4)
+    flow.drain()
+    gains = r.small_sum[...]
+    shift = width - me * ROWS
+    for place in range(2):
+        row = jnp.concatenate([gains[6 * place + i : 6 * place + i + 1] for i in range(width // WIDE)], 1)
+        r.gain_sums[place] = pltpu.roll(row, lax.rem(shift, width), 1)[:, :ROWS]
+    flat = jnp.concatenate([gains[16:], jnp.zeros((WIDE - 2 * heads, WIDE), F32)], 0)
+    r.table[...] = flat.T
+    table_rows = r.table_out.shape[0]
+    r.table_sum[...] = r.table[pl.ds(pl.multiple_of(me * table_rows, 8), table_rows), 0 : 2 * heads]
+    last = [
+        pltpu.make_async_copy(source, target, r.stored.at[5 + i])
+        for i, (source, target) in enumerate(
+            ((r.gain_sums.at[0], r.gain1_out), (r.gain_sums.at[1], r.gain2_out), (r.table_sum, r.table_out))
+        )
+    ]
+    for copy in last:
+        copy.start()
+    for copy in last:
+        copy.wait()
+    back_copy.wait_send()
+    sent_result.wait()
+    sent_states.wait()
+
+
+class Slot:
+    (
+        normed,
+        other,
+        query,
+        key,
+        value,
+        attended,
+        low_middle,
+        cross_query,
+        cross_key,
+        cross_value,
+        crossed,
+        second,
+        low_grad,
+        hidden3,
+        back0,
+        back1,
+        back2,
+        back3,
+        d_value,
+        returned,
+    ) = range(20)
+
+
+SMALL = 99
+SMALL_STEPS = (((0, 1),), ((1, 2),), ((2, 4), (3, 8), (4, 12)))
+
+
+def fold(row):
+    return jnp.concatenate([row[:, WIDE * i : WIDE * (i + 1)] for i in range(row.shape[1] // WIDE)], 0)
+
+
+def norm_back(source, f, grad_at, gain, s, s_grad_at, s_out_at):
+    count = f.shape[1]
+    chunk = count // 4
+    gain_grad = jnp.zeros((1, f.shape[2]), F32)
+    for part in range(4):
+        rows = slice(part * chunk, (part + 1) * chunk)
+        inputs = source[rows, :].astype(F32)
+        grad = f[grad_at, rows, :]
+        centre = inputs - jnp.mean(inputs, axis=-1, keepdims=True)
+        spread = lax.rsqrt(jnp.mean(centre * centre, axis=-1, keepdims=True) + EPSILON)
+        normed = centre * spread
+        gain_grad = gain_grad + jnp.sum(grad * normed, axis=0, keepdims=True)
+        scaled = grad * gain[...]
+        back = spread * (
+            scaled
+            - jnp.mean(scaled, axis=-1, keepdims=True)
+            - normed * jnp.mean(scaled * normed, axis=-1, keepdims=True)
+        )
+        if s is not None:
+            total = s[s_grad_at, rows, :].astype(F32) + back
+            s[s_out_at, rows, :] = total.astype(BF)
+        else:
+            total = f[0, rows, :] + back
+        f[0, rows, :] = total
+    return gain_grad
+
+
+def unband(grad):
+    half = WIDE // 2
+    rolled = pltpu.roll(jnp.where(same_block((WIDE, WIDE)), grad, 0.0), 1, 1, stride=1, stride_axis=0)
+    return jnp.sum(rolled[:half], axis=0, keepdims=True), jnp.sum(rolled[half:], axis=0, keepdims=True)
+
+
+def deliver_kernel(*refs):
+    number = (len(refs) - 2) // 3
+    sources, targets, held = refs[:number], refs[number : 2 * number], refs[2 * number : 3 * number]
+    came, went = refs[-2:]
+    arrivals = [pltpu.make_async_copy(sources[i], held[i], came.at[i]) for i in range(number)]
+    departures = [pltpu.make_async_copy(held[i], targets[i], went.at[i]) for i in range(number)]
+    for copy in arrivals:
+        copy.start()
+    for arrival, departure in zip(arrivals, departures):
+        arrival.wait()
+        departure.start()
+    for copy in departures:
+        copy.wait()
+
+
+def deliver(arrays):
+    anywhere = pl.BlockSpec(memory_space=pl.ANY)
+    return pl.pallas_call(
+        deliver_kernel,
+        in_specs=[anywhere] * len(arrays),
+        out_specs=[anywhere] * len(arrays),
+        out_shape=[jax.ShapeDtypeStruct(array.shape, array.dtype) for array in arrays],
+        scratch_shapes=[pltpu.VMEM(array.shape, array.dtype) for array in arrays]
+        + [pltpu.SemaphoreType.DMA((len(arrays),))] * 2,
+        compiler_params=params(63),
+        cost_estimate=cost(3),
+    )(*arrays)
+
+
+def whole_layer(operands, scale):
+    count, width = operands[0].shape
+    hidden_width = operands[7].shape[1]
+    heads = operands[-1].shape[0] // 2
+    pairs = heads // 2
+    rows = width // 16
+    outs = [
+        jax.ShapeDtypeStruct((count, width), BF),
+        jax.ShapeDtypeStruct((count, width), F32),
+        jax.ShapeDtypeStruct((3, count, width), BF),
+        jax.ShapeDtypeStruct((4, rows, width), F32),
+        jax.ShapeDtypeStruct((rows, hidden_width), F32),
+        jax.ShapeDtypeStruct((rows, width), F32),
+        jax.ShapeDtypeStruct((rows, width), F32),
+        jax.ShapeDtypeStruct((rows, width), F32),
+        jax.ShapeDtypeStruct((rows, 3 * width), F32),
+        jax.ShapeDtypeStruct((rows, 2 * width), F32),
+        jax.ShapeDtypeStruct((1, rows), F32),
+        jax.ShapeDtypeStruct((1, rows), F32),
+        jax.ShapeDtypeStruct((WIDE // 16, 2 * heads), F32),
+    ]
+    anywhere = pl.BlockSpec(memory_space=pl.ANY)
+    inside = pl.BlockSpec(memory_space=pltpu.VMEM)
+    scalars = pl.BlockSpec(memory_space=pltpu.SMEM)
+    dma = pltpu.SemaphoreType.DMA
+    small = (16 + 2 * heads, WIDE)
+    scratch = [
+        pltpu.VMEM((20, count, width), BF),
+        pltpu.VMEM((3, count, width), F32),
+        pltpu.VMEM((5, width, width), BF),
+        dma((FETCHES,)),
+        dma((8,)),
+        pltpu.VMEM((width, width), BF),
+        pltpu.VMEM((UNITS, 2, 4, rows, width), BF),
+        pltpu.VMEM((RING, 2, 4, rows, width), BF),
+        pltpu.VMEM((LANDINGS, 2, 4, rows, width), BF),
+        pltpu.VMEM((len(Y_PLACES), 4, rows, width), BF),
+        pltpu.VMEM((len(PLAIN_UNITS), 3, rows, width), BF),
+        pltpu.VMEM((2, 2, 4, rows, width), BF),
+        pltpu.VMEM((4, rows, width), BF),
+        pltpu.VMEM((max(1, len(TURNED_UNITS)), 2, 2, 16 if not TURNED_UNITS else rows, width), BF),
+        dma((RING,)),
+        dma((LANDINGS,)),
+        dma((1,)),
+        dma((len(Y_PLACES),)),
+        dma((1,)),
+        dma((len(PLAIN_UNITS) + 2,)),
+        dma((1,)),
+        dma((len(PLAIN_UNITS) + 1,)),
+        pltpu.SemaphoreType.REGULAR((UNITS - LANDINGS,)),
+        dma((1,)),
+        dma((2,)),
+        dma((1,)),
+        dma((1,)),
+        dma((1,)),
+        dma((2, 4)),
+        pltpu.VMEM((2, 2, 2, 2, width // 8, width), BF),
+        pltpu.VMEM((4 + len(PLAIN_UNITS), rows, width), F32),
+        dma((STORES,)),
+        pltpu.VMEM((rows, 2 * width), F32),
+        pltpu.VMEM((rows, 2 * width), F32),
+        dma((1,)),
+        dma((1,)),
+        pltpu.VMEM((pairs, 2, count), F32),
+        pltpu.VMEM((pairs, 2, count), F32),
+        pltpu.VMEM((pairs, 2, WIDE, WIDE), BF),
+        pltpu.VMEM((WIDE, count), BF),
+        pltpu.VMEM((WIDE, count), BF),
+        pltpu.VMEM(small, F32),
+        pltpu.VMEM((WIDE, WIDE), F32),
+        pltpu.VMEM((2, 1, rows), F32),
+        pltpu.VMEM((WIDE // 16, 2 * heads), F32),
+        pltpu.VMEM((8, *small), F32),
+        dma((1,)),
+        dma((5,)),
+        pltpu.VMEM((pairs, 2, WIDE, WIDE), F32),
+    ]
+    outputs = pl.pallas_call(
+        functools.partial(layer_kernel, scale),
+        in_specs=[anywhere] * INPUTS + [scalars] + [inside] * (SMALL_INPUTS - 1),
+        out_specs=[anywhere] * OUTPUTS + [inside] * KEPT_OUTPUTS,
+        out_shape=outs,
+        scratch_shapes=scratch,
+        compiler_params=pltpu.CompilerParams(
+            collective_id=0, has_side_effects=True, vmem_limit_bytes=(64 << 20) - (256 << 10)
+        ),
+        cost_estimate=cost(150),
+    )(*operands)
+    down = outputs[3].reshape(4 * rows, width)
+    return [*outputs[:2], down, *outputs[4:]]
 
 
 def norm_rows(inputs, gain_row):
@@ -432,9 +1596,9 @@
     buckets = box_table.shape[1] // 2
     scale = (width // heads) ** (-0.5)
     pairs = heads // 2
-    parts = lax.axis_size("page")
-    side = lax.axis_index("stream")
-    me = lax.axis_index("page").astype(jnp.int32).reshape(1)
+    parts = lax.axis_size(PAGE)
+    side = lax.axis_index(STREAM)
+    me = lax.axis_index(PAGE).astype(jnp.int32).reshape(1)
     own_count = jnp.take(counts[:, 0], side)
     other_count = jnp.take(counts[:, 0], 1 - side)
     slots = jnp.arange(slot_count)
@@ -450,11 +1614,47 @@
     weights = [w[0] for w in (w_qkv, w_out, w_cq, w_ckv, w_cout, w_up, w_down)]
     w_qkv, w_out, w_cq, w_ckv, w_cout, w_up, w_down = weights
 
+    if parts == 16 and width == WIDTH and w_up.shape[1] == 4 * width:
+        operands = [
+            states[0, 0],
+            cotangent[0, 0],
+            w_qkv,
+            w_out,
+            w_cq,
+            w_ckv,
+            w_cout,
+            w_up,
+            w_down,
+            counts[:, 0],
+            box_x,
+            box_y,
+            ln1_gain,
+            ln2_gain,
+            box_table[0].T,
+        ]
+        result, states_grad, down, up, cout, cq, out, qkv, ckv, gain1, gain2, table = deliver(
+            whole_layer(operands, scale)
+        )
+        return (
+            result[None, None],
+            states_grad[None, None],
+            gain1,
+            gain2,
+            table[None],
+            qkv[None],
+            out[None],
+            cq[None],
+            ckv[None],
+            cout[None],
+            up[None],
+            down[None],
+        )
+
     inputs = states[0, 0].astype(F32)
     normed, norm_pull = jax.vjp(norm_rows, inputs, ln1_gain[0])
     normed = normed.astype(BF)
     cross_kv = matmul(normed, w_ckv).astype(BF)
-    partner = swapped(cross_kv, "stream", 1)
+    partner = swapped(cross_kv, STREAM, 1)
     joined = matmul(normed, w_qkv).astype(BF)
     attended, self_lse = attend_forward(joined, joined, pairs, mask_own, (bands, onehot), scale, 18)
     middle = inputs + matmul(attended, w_out)
@@ -476,7 +1676,7 @@
     d_cross_query, d_partner = attend_backward(
         cross_query, partner, 0, d_crossed, crossed, cross_lse, mask_other, None, scale, 26
     )
-    returned = swapped(d_partner, "stream", 1)
+    returned = swapped(d_partner, STREAM, 1)
     d_middle = d_after + matmul_back(d_cross_query, w_cq)
     low_d_middle = d_middle.astype(BF)
     d_attended = matmul_back(low_d_middle, w_out).astype(BF)
@@ -543,49 +1743,49 @@
     parts = small.shape[0]
     order = jnp.arange(parts) ^ me
     small = jnp.take(small, order, axis=0).reshape(parts // 4, 2, 2, -1)
-    small = small[:, :, 0] + swapped(small[:, :, 1], "page", 1)
-    small = small[:, 0] + swapped(small[:, 1], "page", 2)
+    small = small[:, :, 0] + swapped(small[:, :, 1], PAGE, 1)
+    small = small[:, 0] + swapped(small[:, 1], PAGE, 2)
     total = small[0]
     for step in range(1, parts // 4):
-        total = total + swapped(small[step], "page", 4 * step)
+        total = total + swapped(small[step], PAGE, 4 * step)
     return total
 
 
 def solution(mesh):
     placed = (
-        P("stream", "page", None, None),
-        P(None, "page"),
-        P("page", None),
-        P("page", None),
-        P("stream", None),
-        P("stream", None),
-        P("stream", None, None),
-        P("stream", None, None),
-        P("stream", None, None),
-        P("stream", None, None),
-        P("stream", None, None),
-        P("stream", None, None),
-        P("stream", None, None),
-        P("stream", None, None),
-        P("stream", "page", None, None),
+        P(STREAM, PAGE, None, None),
+        P(None, PAGE),
+        P(PAGE, None),
+        P(PAGE, None),
+        P(STREAM, None),
+        P(STREAM, None),
+        P(STREAM, None, None),
+        P(STREAM, None, None),
+        P(STREAM, None, None),
+        P(STREAM, None, None),
+        P(STREAM, None, None),
+        P(STREAM, None, None),
+        P(STREAM, None, None),
+        P(STREAM, None, None),
+        P(STREAM, PAGE, None, None),
     )
     return jax.shard_map(
         body,
         mesh=mesh,
         in_specs=placed,
         out_specs=(
-            P("stream", "page", None, None),
-            P("stream", "page", None, None),
-            P("stream", "page"),
-            P("stream", "page"),
-            P("stream", "page", None),
-            P("stream", "page", None),
-            P("stream", "page", None),
-            P("stream", "page", None),
-            P("stream", "page", None),
-            P("stream", "page", None),
-            P("stream", "page", None),
-            P("stream", "page", None),
+            P(STREAM, PAGE, None, None),
+            P(STREAM, PAGE, None, None),
+            P(STREAM, PAGE),
+            P(STREAM, PAGE),
+            P(STREAM, PAGE, None),
+            P(STREAM, PAGE, None),
+            P(STREAM, PAGE, None),
+            P(STREAM, PAGE, None),
+            P(STREAM, PAGE, None),
+            P(STREAM, PAGE, None),
+            P(STREAM, PAGE, None),
+            P(STREAM, PAGE, None),
         ),
         check_vma=False,
     )

time: 394 us -> 175 us (0.44)
  waiting for transfers between devices: 149 us -> 0 us
  Pallas kernels: 114 us -> 170 us
  starting transfers between devices: 33.9 us -> 0 us
  matrix products: 33.4 us -> 0 us
  other arithmetic: 33.3 us -> 0 us
  local copies, waits for them, and re-layouts: 22 us -> 0 us
    ppermute x27 -> x0, waiting for transfers between devices: 149 us -> none  [swapped(): lax.ppermute(shard, axis, [(i, i ^ mask) for i in range(lax.axis_size(axi...]
    pallas_call x10 -> x2, Pallas kernels: 114 us -> 170 us  [the longest x1 166 us: whole_layer(): pl.pallas_call(functools.partial(layer_kernel, scale), in_specs=[anywhere...]
    ppermute x27 -> x0, starting transfers between devices: 33.9 us -> none  [swapped(): lax.ppermute(shard, axis, [(i, i ^ mask) for i in range(lax.axis_size(axi...]
    dot_general x15 -> x0, matrix products: 33.4 us -> none  [contract(): lax.dot_general(left, right, (((left_dim,), (right_dim,)), ((), ())), pre...]
    convert_element_type x15 -> x0, other arithmetic: 17.8 us -> none  [the longest x4 8.73 us: reduce_parts(): arrived = swapped(send, 'page', 1).astype(F32)]
    unnamed x112 -> x0, local copies, waits for them, and re-layouts: 9.2 us -> none
    reduce_sum x5 -> x0, other arithmetic: 5.17 us -> none  [the longest x2 2.26 us: norm_rows(): centre = inputs - jnp.mean(inputs, axis=-1, keepdims=True)]
    another operation x4 -> x0, other arithmetic: 4.45 us -> none
  transfers between devices with their start and end apart: 27 -> 0, of which waited for: 10 -> 0; matrix products, arithmetic and copies ran while one was open for 13% -> 0% of each run, Pallas kernels for 9% -> 0%
where the time goes in v3:
time: 175 us; the launch traced here: 171 us
  Pallas kernels  170 us (97%)
    pallas_call x1, Pallas kernels, whole_layer(): pl.pallas_call(functools.partial(layer_kernel, scale), in_specs=[anywhere...  166 us
    pallas_call x1, Pallas kernels, deliver(): pl.pallas_call(deliver_kernel, in_specs=[anywhere] * len(arrays), out_spe...  4.1 us

profile of v3, /device:TPU:0, one launch (start us, length us, event | category | flops | bytes accessed | tf_op | source)
XLA Modules:
  0.0 171.4 jit_solution(608733712086264722)
XLA Ops:
  0.7 166.3 %shard_map.238 = (bf16[640,768]{1,0:T(8,128)(2,1)}, f32[640,768]{1,0:T(8,128)}, bf16[3,640,768]{2,1,0:T(8,128)(2,1)}, f32[4,48,768]{2,1,0:T(8,128)}, f32[48,3072...) custom-call(bf16[640,768]{1,0:T(8,128)(2,1)} %bitcast.31, ...), custom_call_target="tpu_custom_call" | custom-call | flops 165000003584 | bytes 1048576 | tf_op jit(solution)/shard_map/pallas_call | solution.py:1543
  167.0 4.1 %shard_map.239 = (bf16[640,768]{1,0:T(8,128)(2,1)}, f32[640,768]{1,0:T(8,128)}, f32[192,768]{1,0:T(8,128)}, f32[48,3072]{1,0:T(8,128)}, f32[48,768]{1,0:T(8,128)...) custom-call(bf16[640,768]{1,0:T(8,128)(2,1)} %get-tuple-element.36.r, ...), custom_call_target="tpu_custom_call" | custom-call | flops 3300000000 | bytes 1048576 | tf_op jit(solution)/shard_map/pallas_call | solution.py:1454

commit v4 on v3

--- a/solution.py
+++ b/solution.py
@@ -418,10 +418,10 @@
 STORES = 8
 FETCHES = 14
 LANDINGS = 3
-LINK_US = 6.7
-CORE_US = 2.6
+LINK_US = 6.6
+CORE_US = 1.7
 LATE_US = 30.0
-LATENCY_US = 2.0
+LATENCY_US = 4.5
 
 
 CORE, NEAR, FAR, JOIN, LAST, DONE, Y, Z = range(8)
@@ -437,6 +437,7 @@
         self.now = 0.0
         self.y_free = 0.0
         self.z_free = 0.0
+        self.middle_free = 0.0
         self.pending = []
         self.near_done = {}
         self.stores = []
@@ -478,7 +479,7 @@
         r = self.r
         if unit in DOWN_UNITS:
             step = DOWN_STEPS[DOWN_UNITS.index(unit)]
-            if (step & 1 == 1) == arriving:
+            if (step in NEAR_STEPS) == arriving:
                 return None
             target = unit if arriving else DOWN_UNITS[DOWN_STEPS.index(step ^ 1)]
             source, landing = r.keep.at[unit], r.near_down.at[step // 2]
@@ -505,7 +506,7 @@
         r = self.r
         if unit in DOWN_UNITS:
             step = DOWN_STEPS[DOWN_UNITS.index(unit)]
-            if step != (0 if arriving else 2):
+            if step != (0 if arriving else 3):
                 return None
             target = DOWN_UNITS[DOWN_STEPS.index(0)]
             source, landing = r.keep.at[unit, 0], r.far_down
@@ -515,14 +516,14 @@
         else:
             target = unit
             if unit in UP_UNITS and not arriving:
-                target = UP_UNITS[DOWN_STEPS.index(DOWN_STEPS[UP_UNITS.index(unit)] ^ 2)]
+                target = UP_UNITS[DOWN_STEPS.index(DOWN_STEPS[UP_UNITS.index(unit)] ^ 3)]
             source, landing = r.keep.at[unit, 0, 1], r.z_in.at[PLAIN_UNITS.index(target), 2]
         return pltpu.make_async_remote_copy(
             src_ref=source,
             dst_ref=landing,
             send_sem=r.far_sent.at[0],
             recv_sem=r.far_got.at[self.z_place(target)],
-            device_id=self.at(8),
+            device_id=self.at(12),
             device_id_type=pl.DeviceIdType.MESH,
         )
 
@@ -562,9 +563,14 @@
     def advance(self, entry):
         self.plan(entry)()
 
-    def z_busy(self, us):
-        self.z_free = max(self.now, self.z_free) + us
+    def near_busy(self, blocks):
+        self.z_free = max(self.now, self.z_free) + blocks * LINK_US / 4
         return self.z_free + LATENCY_US
+
+    def far_busy(self, blocks):
+        self.z_free = max(self.now, self.z_free) + blocks * LINK_US / 4
+        self.middle_free = max(self.now, self.middle_free) + blocks * LINK_US / 2
+        return max(self.z_free, self.middle_free) + LATENCY_US
 
     def y_busy(self, us):
         self.y_free = max(self.now, self.y_free) + us
@@ -586,19 +592,10 @@
         elif unit == SMALL:
             free = max(self.now, self.y_free if stage == CORE else self.z_free)
             following = {CORE: Y, Y: Z, Z: DONE}[stage]
-            entry[1:] = [following, free + (2.0 if stage == CORE else 6.0)]
-        elif unit in TURNED_UNITS and stage != DONE:
-            if stage == CORE:
-                entry[1:] = [NEAR, self.z_busy(LINK_US)]
-            elif stage == NEAR:
-                entry[1:] = [FAR, self.z_busy(LINK_US)]
-            elif stage == FAR:
-                entry[1:] = [LAST, self.y_busy(LINK_US / 4) + LATE_US]
-            else:
-                entry[1] = DONE
+            entry[1:] = [following, free + (1.0 if stage == CORE else 7.0)]
         elif stage == CORE:
-            if step is not None and step & 1:
-                self.near_done[step ^ 1] = self.z_busy(2 * LINK_US)
+            if step in NEAR_STEPS:
+                self.near_done[step ^ 1] = self.near_busy(8)
                 entry[1] = DONE
             elif step is not None:
                 entry[1:] = [JOIN, self.near_done[step]]
@@ -608,14 +605,14 @@
             entry[1:] = [Y, self.y_busy(LINK_US)]
         elif stage == Y:
             if step is not None:
-                done = self.z_busy(2 * LINK_US) if step == 2 else self.z_free + LATE_US
-                entry[1:] = [DONE, 0.0] if step == 2 else [FAR, done + LATE_US]
+                done = self.far_busy(4) if step == 3 else self.z_free + LATE_US
+                entry[1:] = [DONE, 0.0] if step == 3 else [FAR, done + LATE_US]
             else:
-                entry[1:] = [NEAR, self.z_busy(LINK_US / 2)]
+                entry[1:] = [NEAR, self.near_busy(2)]
                 if unit in UP_UNITS:
                     self.meet(entry, [unit, UP_UNITS[DOWN_STEPS.index(DOWN_STEPS[UP_UNITS.index(unit)] ^ 1)]])
         elif stage == NEAR:
-            entry[1:] = [FAR, self.z_busy(LINK_US / 2) + (8.0 if unit in KV_UNITS else LATE_US)]
+            entry[1:] = [FAR, self.far_busy(1) + (8.0 if unit in KV_UNITS else LATE_US)]
             if unit in UP_UNITS:
                 self.meet(entry, UP_UNITS)
         else:
@@ -662,7 +659,7 @@
             if step is None and not turned:
                 self.y_copy(unit).start()
             self.join(unit, 0, (0, 1, 2, 3), arrived.at[0])
-            if turned or (step is not None and step & 1):
+            if turned or step in NEAR_STEPS:
                 self.near_copy(unit).start()
             if unit < UNITS - LANDINGS:
                 pl.semaphore_signal(
@@ -679,7 +676,7 @@
             self.join(unit, 0, (2, 3, 0, 1), r.y_in.at[Y_PLACES[unit]])
             if step is None:
                 self.near_copy(unit).start()
-            elif step == 2:
+            elif step == 3:
                 self.far_copy(unit).start()
         elif stage == NEAR:
             self.near_copy(unit, arriving=True).wait_recv()
@@ -898,8 +895,9 @@
 DOWN_UNITS = (1, 3, 5, 7)
 TURNED_UNITS = ()
 UP_UNITS = (0, 2, 4, 6)
-DOWN_STEPS = (1, 3, 2, 0)
-SLOT_OF = (0, 2, 1, 3)
+DOWN_STEPS = (1, 2, 3, 0)
+NEAR_STEPS = (1, 2)
+SLOT_OF = (0, 2, 3, 1)
 PLAIN_UNITS = (0, 2, 4, 6, 8, 9, 10, 11, 12, 13, 14, 15)
 UNITS = 16
 Y_PLACES = {unit: at for at, unit in enumerate((0, 2, 4, 5, 6, 7, 8, 9, 10, 11, 12, 13, 14, 15))}
@@ -1205,9 +1203,12 @@
         flow.produce(UP_UNITS[step], r.s[second_at], r.s[d_up_at])
         flow.tick(0.1)
         flow.produce(DOWN_UNITS[step], r.s[hidden_at], r.s[grad_at])
-        flow.tick(0.1)
-        back = contract(r.s[d_up_at], r.w[up_at], 1, 1)
-        r.f[0] = back if step == 0 else r.f[0] + back
+        flow.tick(0.2)
+    for step in range(4):
+        for part in range(2):
+            rows = slice(part * half_rows, (part + 1) * half_rows)
+            back = contract(r.s[back_slots[step], rows, :], r.w[1 + step], 1, 1)
+            r.f[0, rows, :] = back if step == 0 else r.f[0, rows, :] + back
         flow.tick(1.2)
     got_cq, got_out = fetch(r.w_cq, r.w.at[1]), fetch(r.w_out, r.w.at[2])
     got_q, got_k = [fetch(columns(r.w_qkv, i), r.w.at[3 + i]) for i in range(2)]
@@ -1245,6 +1246,7 @@
     flow.produce(9, slot(Slot.other)[...], r.s[d_key_at])
     flow.tick(0.1)
     flow.produce(10, slot(Slot.other)[...], r.s[d_value_at])
+    flow.tick(0.1)
     back_at = Slot.crossed
     r.s[back_at] = (
         contract(r.s[d_key_at], r.other_w[0].reshape(width, width), 1, 1)

time: 175 us -> 168 us (0.960)
  Pallas kernels: 170 us -> 164 us
    pallas_call x1, Pallas kernels: 166 us -> 160 us  [whole_layer(): pl.pallas_call(functools.partial(layer_kernel, scale), in_specs=[anywhere...]
where the time goes in v4:
time: 168 us; the launch traced here: 165 us
  Pallas kernels  164 us (98%)
    pallas_call x1, Pallas kernels, whole_layer(): pl.pallas_call(functools.partial(layer_kernel, scale), in_specs=[anywhere...  160 us
    pallas_call x1, Pallas kernels, deliver(): pl.pallas_call(deliver_kernel, in_specs=[anywhere] * len(arrays), out_spe...  4.1 us

profile of v4, /device:TPU:0, one launch (start us, length us, event | category | flops | bytes accessed | tf_op | source)
XLA Modules:
  0.0 164.6 jit_solution(15327358940762811113)
XLA Ops:
  0.7 159.5 %shard_map.238 = (bf16[640,768]{1,0:T(8,128)(2,1)}, f32[640,768]{1,0:T(8,128)}, bf16[3,640,768]{2,1,0:T(8,128)(2,1)}, f32[4,48,768]{2,1,0:T(8,128)}, f32[48,3072...) custom-call(bf16[640,768]{1,0:T(8,128)(2,1)} %bitcast.31, ...), custom_call_target="tpu_custom_call" | custom-call | flops 165000003584 | bytes 1048576 | tf_op jit(solution)/shard_map/pallas_call | solution.py:1545
  160.2 4.1 %shard_map.239 = (bf16[640,768]{1,0:T(8,128)(2,1)}, f32[640,768]{1,0:T(8,128)}, f32[192,768]{1,0:T(8,128)}, f32[48,3072]{1,0:T(8,128)}, f32[48,768]{1,0:T(8,128)...) custom-call(bf16[640,768]{1,0:T(8,128)(2,1)} %get-tuple-element.36.r, ...), custom_call_target="tpu_custom_call" | custom-call | flops 3300000000 | bytes 1048576 | tf_op jit(solution)/shard_map/pallas_call | solution.py:1456

commit v5 on v4

--- a/solution.py
+++ b/solution.py
@@ -268,13 +268,12 @@
 
 
 def gelu_pair(value):
-    distance = jnp.abs(value) * 0.7071067811865476
-    bell = jnp.exp(-0.5 * value * value)
-    t = 1.0 / (1.0 + 0.3275911 * distance)
-    poly = t * (0.254829592 + t * (-0.284496736 + t * (1.421413741 + t * (-1.453152027 + t * 1.061405429))))
-    tail = 0.5 * poly * bell
+    density = jnp.exp(value * value * -0.5) * 0.3989422804014327
+    t = 1.0 / (1.0 + 0.2316419 * jnp.abs(value))
+    poly = t * (0.319381530 + t * (-0.356563782 + t * (1.781477937 + t * (-1.821255978 + t * 1.330274429))))
+    tail = poly * density
     phi = jnp.where(value >= 0, 1.0 - tail, tail)
-    return value * phi, phi + value * bell * 0.3989422804014327
+    return value * phi, phi + value * density
 
 
 def feed_kernel(me_ref, second_ref, grad_ref, up_ref, down_ref, hidden_ref, d_up_ref, send_ref, keep_ref, sums_ref):
@@ -458,14 +457,15 @@
 
     def y_copy(self, unit):
         r = self.r
-        source, landing = r.keep.at[unit, 1], r.y_in.at[Y_PLACES[unit]]
         if unit in TURNED_UNITS:
             source, landing = r.keep.at[unit, 1, 0], r.z_in.at[PLAIN_UNITS.index(unit), 2]
+        else:
+            source, landing = r.keep.at[unit, 1], r.y_in.at[Y_PLACES[unit]]
         return pltpu.make_async_remote_copy(
             src_ref=source,
             dst_ref=landing,
-            send_sem=r.y_sent.at[0],
-            recv_sem=r.y_got.at[Y_PLACES[unit]],
+            send_sem=r.y_sent.at[int(unit in TURNED_UNITS)],
+            recv_sem=r.y_got.at[Y_PLACES.get(unit, len(Y_PLACES))],
             device_id=self.at(2),
             device_id_type=pl.DeviceIdType.MESH,
         )
@@ -496,7 +496,7 @@
         return pltpu.make_async_remote_copy(
             src_ref=source,
             dst_ref=landing,
-            send_sem=r.near_sent.at[0],
+            send_sem=r.near_sent.at[int(unit in TURNED_UNITS)],
             recv_sem=r.near_got.at[self.z_place(target)],
             device_id=self.at(4),
             device_id_type=pl.DeviceIdType.MESH,
@@ -521,7 +521,7 @@
         return pltpu.make_async_remote_copy(
             src_ref=source,
             dst_ref=landing,
-            send_sem=r.far_sent.at[0],
+            send_sem=r.far_sent.at[int(unit in TURNED_UNITS)],
             recv_sem=r.far_got.at[self.z_place(target)],
             device_id=self.at(12),
             device_id_type=pl.DeviceIdType.MESH,
@@ -593,6 +593,15 @@
             free = max(self.now, self.y_free if stage == CORE else self.z_free)
             following = {CORE: Y, Y: Z, Z: DONE}[stage]
             entry[1:] = [following, free + (1.0 if stage == CORE else 7.0)]
+        elif unit in TURNED_UNITS:
+            if stage == CORE:
+                entry[1:] = [NEAR, self.near_busy(4)]
+            elif stage == NEAR:
+                entry[1:] = [FAR, self.far_busy(2)]
+            elif stage == FAR:
+                entry[1:] = [LAST, self.y_busy(LINK_US / 4) + LATE_US]
+            else:
+                entry[1] = DONE
         elif stage == CORE:
             if step in NEAR_STEPS:
                 self.near_done[step ^ 1] = self.near_busy(8)
@@ -828,13 +837,16 @@
         r = self.r
         for whole, sent in (
             (r.y_in, r.y_sent),
-            (r.keep.at[pl.ds(0, 5)], r.near_sent),
-            (r.keep.at[pl.ds(0, 2)], r.far_sent),
+            (r.s.at[pl.ds(0, 3), pl.ds(0, 608)], r.near_sent),
+            (r.z_in.at[pl.ds(0, 5)], r.far_sent),
             (r.small_in.at[pl.ds(0, 5)], r.small_sent),
             (r.other_w, r.weight_sent),
             (r.s.at[Slot.normed], r.normed_sent),
         ):
             pltpu.make_async_copy(whole, whole, sent.at[0]).wait()
+        for unit in TURNED_UNITS:
+            for copy in (self.near_copy(unit), self.far_copy(unit), self.y_copy(unit)):
+                copy.wait_send()
         self.kv_copy().wait_send()
         for place in range(max(0, len(self.stores) - STORES), len(self.stores)):
             self.store_copy(place).wait()
@@ -893,14 +905,14 @@
 WIDTH = 768
 ROWS = 48
 DOWN_UNITS = (1, 3, 5, 7)
-TURNED_UNITS = ()
+TURNED_UNITS = (13,)
 UP_UNITS = (0, 2, 4, 6)
 DOWN_STEPS = (1, 2, 3, 0)
 NEAR_STEPS = (1, 2)
 SLOT_OF = (0, 2, 3, 1)
 PLAIN_UNITS = (0, 2, 4, 6, 8, 9, 10, 11, 12, 13, 14, 15)
 UNITS = 16
-Y_PLACES = {unit: at for at, unit in enumerate((0, 2, 4, 5, 6, 7, 8, 9, 10, 11, 12, 13, 14, 15))}
+Y_PLACES = {unit: at for at, unit in enumerate((0, 2, 4, 5, 6, 7, 8, 9, 10, 11, 12, 14, 15))}
 KV_UNITS = (9, 10)
 THIRD_UNITS = (13, 14, 15)
 
@@ -1192,9 +1204,8 @@
         hidden_at, d_up_at, up_at = hidden_slots[step], back_slots[step], 1 + step
         got_up[step].wait()
 
-        @pl.loop(0, 2)
-        def _(part, hidden_at=hidden_at, d_up_at=d_up_at, up_at=up_at):
-            rows = pl.ds(pl.multiple_of(part * half_rows, 16), half_rows)
+        for part in range(4):
+            rows = slice(part * (count // 4), (part + 1) * (count // 4))
             hidden, slope = gelu_pair(contract(r.s[second_at, rows, :], r.w[up_at], 1, 0))
             r.s[hidden_at, rows, :] = hidden.astype(BF)
             r.s[d_up_at, rows, :] = (slope * r.s[d_up_at, rows, :].astype(F32)).astype(BF)
@@ -1508,11 +1519,11 @@
         pltpu.VMEM((max(1, len(TURNED_UNITS)), 2, 2, 16 if not TURNED_UNITS else rows, width), BF),
         dma((RING,)),
         dma((LANDINGS,)),
-        dma((1,)),
-        dma((len(Y_PLACES),)),
-        dma((1,)),
+        dma((2,)),
+        dma((len(Y_PLACES) + 1,)),
+        dma((2,)),
         dma((len(PLAIN_UNITS) + 2,)),
-        dma((1,)),
+        dma((2,)),
         dma((len(PLAIN_UNITS) + 1,)),
         pltpu.SemaphoreType.REGULAR((UNITS - LANDINGS,)),
         dma((1,)),

time: 168 us -> 166 us (0.988)
  Pallas kernels: 164 us -> 162 us
where the time goes in v5:
time: 166 us; the launch traced here: 163 us
  Pallas kernels  162 us (98%)
    pallas_call x1, Pallas kernels, whole_layer(): pl.pallas_call(functools.partial(layer_kernel, scale), in_specs=[anywhere...  158 us
    pallas_call x1, Pallas kernels, deliver(): pl.pallas_call(deliver_kernel, in_specs=[anywhere] * len(arrays), out_spe...  4.1 us

profile of v5, /device:TPU:0, one launch (start us, length us, event | category | flops | bytes accessed | tf_op | source)
XLA Modules:
  0.0 163.2 jit_solution(12275746381573433508)
XLA Ops:
  0.7 158.2 %shard_map.238 = (bf16[640,768]{1,0:T(8,128)(2,1)}, f32[640,768]{1,0:T(8,128)}, bf16[3,640,768]{2,1,0:T(8,128)(2,1)}, f32[4,48,768]{2,1,0:T(8,128)}, f32[48,3072...) custom-call(bf16[640,768]{1,0:T(8,128)(2,1)} %bitcast.31, ...), custom_call_target="tpu_custom_call" | custom-call | flops 165000003584 | bytes 1048576 | tf_op jit(solution)/shard_map/pallas_call | solution.py:1556
  158.8 4.1 %shard_map.239 = (bf16[640,768]{1,0:T(8,128)(2,1)}, f32[640,768]{1,0:T(8,128)}, f32[192,768]{1,0:T(8,128)}, f32[48,3072]{1,0:T(8,128)}, f32[48,768]{1,0:T(8,128)...) custom-call(bf16[640,768]{1,0:T(8,128)(2,1)} %get-tuple-element.36.r, ...), custom_call_target="tpu_custom_call" | custom-call | flops 3300000000 | bytes 1048576 | tf_op jit(solution)/shard_map/pallas_call | solution.py:1467

commit v6 on v5

--- a/solution.py
+++ b/solution.py
@@ -1098,8 +1098,7 @@
     pl.semaphore_wait(barrier, len(others))
 
     flow.start_weights()
-    for part in range(2):
-        normed_copy(part).start()
+    normed_copy(0).start()
     flow.tick(0.1)
     for name, copy, at in ((Slot.query, got_q, 0), (Slot.key, got_k, 1), (Slot.value, got_v, 2)):
         copy.wait()
@@ -1146,6 +1145,10 @@
         r.s[Slot.attended, :, lanes] = output
         r.self_lse[pair] = lse
 
+        @pl.when(pair == pairs // 2)
+        def _():
+            normed_copy(1).start()
+
     pair_loop(1.95, self_forward)
 
     got_out.wait()
@@ -1171,11 +1174,13 @@
     flow.finish_weights()
     for copy in held:
         copy.wait()
+    flow.now = max(flow.now, 30.0)
     for part in range(2):
         normed_copy(part).wait_recv()
-    flow.now = max(flow.now, 30.0)
-    for at, name in enumerate((Slot.cross_key, Slot.cross_value)):
-        slot(name)[...] = contract(slot(Slot.other)[...], r.other_w[at].reshape(width, width), 1, 0).astype(BF)
+        rows = slice(part * half_rows, (part + 1) * half_rows)
+        for at, name in enumerate((Slot.cross_key, Slot.cross_value)):
+            weight = r.other_w[at].reshape(width, width)
+            r.s[name, rows, :] = contract(r.s[Slot.other, rows, :], weight, 1, 0).astype(BF)
     flow.tick(2.0)
 
     def cross_forward(pair):

time: 166 us -> 166 us (level)
  no operation moved by 1% of the time
where the time goes in v6:
time: 166 us; the launch traced here: 162 us
  Pallas kernels  161 us (97%)
    pallas_call x1, Pallas kernels, whole_layer(): pl.pallas_call(functools.partial(layer_kernel, scale), in_specs=[anywhere...  157 us
    pallas_call x1, Pallas kernels, deliver(): pl.pallas_call(deliver_kernel, in_specs=[anywhere] * len(arrays), out_spe...  4.1 us

profile of v6, /device:TPU:0, one launch (start us, length us, event | category | flops | bytes accessed | tf_op | source)
XLA Modules:
  0.0 162.4 jit_solution(7753881911871802524)
XLA Ops:
  0.7 157.4 %shard_map.238 = (bf16[640,768]{1,0:T(8,128)(2,1)}, f32[640,768]{1,0:T(8,128)}, bf16[3,640,768]{2,1,0:T(8,128)(2,1)}, f32[4,48,768]{2,1,0:T(8,128)}, f32[48,3072...) custom-call(bf16[640,768]{1,0:T(8,128)(2,1)} %bitcast.31, ...), custom_call_target="tpu_custom_call" | custom-call | flops 165000003584 | bytes 1048576 | tf_op jit(solution)/shard_map/pallas_call | solution.py:1561
  158.0 4.1 %shard_map.239 = (bf16[640,768]{1,0:T(8,128)(2,1)}, f32[640,768]{1,0:T(8,128)}, f32[192,768]{1,0:T(8,128)}, f32[48,3072]{1,0:T(8,128)}, f32[48,768]{1,0:T(8,128)...) custom-call(bf16[640,768]{1,0:T(8,128)(2,1)} %get-tuple-element.36.r, ...), custom_call_target="tpu_custom_call" | custom-call | flops 3300000000 | bytes 1048576 | tf_op jit(solution)/shard_map/pallas_call | solution.py:1472
